TPU v7x, 32 devices: a whole 2x2x4 slice. The times are simulated.
32 devices in a mesh: rep: 2 (over y), gx: 4 (over z), gy: 4 (over x, core).
Axes of the slice: x: 2, y: 2, z: 4, core: 2. Of those that a mesh axis runs over, the one named last changes fastest.
Arguments:
- residual: bfloat16 [64, 16384], P('rep', 'gx'), parts along dimension 0, may hold values from -1.5 to 1.5
- ffn_partial: float32 [4, 64, 16384], P('gy', 'rep', 'gx'), parts along dimension 1, may hold values from -1.5 to 1.5
- norm_gain: float32 [16384], P('gx'), may hold values from 0.1 to 1.9
- smooth_scale: float32 [16384], P('gx'), may hold values from 0.25 to 4
- w_query: bfloat16 [16384, 8192], P('gx', 'gy'), may hold values from -127 to 127, as said below
- query_scale: float32 [8192], P('gy'), may hold values from 3.125e-05 to 0.000125
- w_keyval: bfloat16 [16384, 1024], P('gx', 'gy'), may hold values from -127 to 127, as said below
- keyval_scale: float32 [1024], P('gy'), may hold values from 3.125e-05 to 0.000125
- key_cache: bfloat16 [64, 4, 512, 128], P(('rep', 'gy'), None, 'gx'), parts along dimension 0, may hold values from -127 to 127, as said below
- value_cache: bfloat16 [64, 4, 512, 128], P(('rep', 'gy'), None, 'gx'), parts along dimension 0, may hold values from -127 to 127, as said below
- key_scale: float32 [64, 4, 512], P(('rep', 'gy'), None, 'gx'), parts along dimension 0, may hold values from 0.007 to 8
- value_scale: float32 [64, 4, 512], P(('rep', 'gy'), None, 'gx'), parts along dimension 0, may hold values from 0.007 to 0.027
- lengths: int32 [64], P(('rep', 'gy')), parts along dimension 0, may hold values from 1 to 512, as said below
- w_out: bfloat16 [8192, 16384], P('gy', 'gx'), may hold values from -127 to 127, as said below
- out_scale: float32 [16384], P('gx'), may hold values from 0.00030935922 to 0.0011932427
Outputs:
- new_residual: bfloat16 [64, 16384], P('rep', 'gx'), parts along dimension 0
There are 2 independent parts, one for each index of `rep`. A program takes and returns all parts, laid end to end along the dimension named above; an argument that names none is the same for every part. Nothing has to cross between parts.
Inputs may be any that keep to these rules, and one draw needn't show every extreme that they name: `w_query`: integer codes of the weights. `w_keyval`: integer codes of the weights. `w_out`: integer codes of the weights. `key_cache`: integer codes. `value_cache`: integer codes. `lengths`: some request uses all 512 positions and some request uses one.
All inputs are finite; a program needn't handle non-finite values.
Results may differ from a plain program's by a relative error of at most 0.011.
Values may be sent and summed in bfloat16 or wider, within the bound.
No kernel may reach another device: no remote copies, remote signals or barrier semaphores. Data moves between devices by JAX's collectives and lax.ppermute only.
A program may use at most 128 MiB of HBM per device.

v0:
```python
import jax
import jax.numpy as jnp
from jax import lax
from jax.sharding import PartitionSpec as P

D = 16384
HEADS = 64
KV_HEADS = 4
HEAD_DIM = 128


EPSILON = 1e-05
NEGATIVE = -1e30


def joined(value, axis, join):
    pieces = jax.tree.map(lambda part: lax.all_gather(part, axis), value)
    head = jax.tree.map(lambda part: part[0], pieces)
    tail = jax.tree.map(lambda part: part[1:], pieces)
    subtotal, _ = lax.scan(lambda subtotal, piece: (join(subtotal, piece), None), head, tail)
    return subtotal


def combine(former, latter):
    top = jnp.maximum(former[0], latter[0])
    first_factor = jnp.exp(former[0] - top)
    second_factor = jnp.exp(latter[0] - top)
    total = former[1] * first_factor + latter[1] * second_factor
    mixed = former[2] * first_factor[..., None] + latter[2] * second_factor[..., None]
    return (top, total, mixed)


def body(
    residual,
    ffn_partial,
    norm_gain,
    smooth_scale,
    w_query,
    query_scale,
    w_keyval,
    keyval_scale,
    key_cache,
    value_cache,
    key_scale,
    value_scale,
    lengths,
    w_out,
    out_scale,
):
    widened = residual.astype(jnp.float32)
    ffn_total = lax.psum(ffn_partial[0], "gy")
    squares = jnp.sum(widened * widened, axis=1)
    smoothed = (widened * (norm_gain / smooth_scale)).astype(jnp.bfloat16)
    query_part = jnp.dot(smoothed, w_query, preferred_element_type=jnp.float32) * query_scale
    keyval_part = jnp.dot(smoothed, w_keyval, preferred_element_type=jnp.float32) * keyval_scale
    query_sum, keyval_sum, square_sum = lax.psum((query_part, keyval_part, squares), "gx")
    row_scale = lax.rsqrt(square_sum / D + EPSILON)[:, None]
    query_rows = (row_scale * query_sum).astype(jnp.bfloat16)
    keyval_rows = (row_scale * keyval_sum).astype(jnp.bfloat16)
    query_vectors, keyvals = (
        lax.all_to_all(query_rows, "gy", split_axis=0, concat_axis=1, tiled=True),
        lax.all_to_all(keyval_rows, "gy", split_axis=0, concat_axis=1, tiled=True),
    )
    requests = query_vectors.shape[0]
    local = key_cache.shape[2]
    group = HEADS // KV_HEADS
    score_multiplier = HEAD_DIM ** (-0.5)
    grouped = query_vectors.reshape(requests, KV_HEADS, group, HEAD_DIM)
    fresh_key_rows = keyvals[:, : KV_HEADS * HEAD_DIM].reshape(requests, KV_HEADS, HEAD_DIM)
    fresh_value_rows = keyvals[:, KV_HEADS * HEAD_DIM :].reshape(requests, KV_HEADS, HEAD_DIM)
    logit_scores = jnp.einsum(
        "rgqd,rgsd->rgqs", grouped, key_cache, preferred_element_type=jnp.float32
    )
    logit_scores = logit_scores * key_scale[:, :, None, :] * score_multiplier
    position = lax.axis_index("gx") * local + jnp.arange(local, dtype=jnp.int32)
    visible = (position[None, :] < lengths[:, None])[:, None, None, :]
    logit_scores = jnp.where(visible, logit_scores, NEGATIVE)
    local_top = jnp.max(logit_scores, axis=-1)
    weights = jnp.where(visible, jnp.exp(logit_scores - local_top[..., None]), 0.0)
    local_total = jnp.sum(weights, axis=-1)
    scaled = (weights * value_scale[:, :, None, :]).astype(jnp.bfloat16)
    local_mixed = jnp.einsum(
        "rgqs,rgsd->rgqd", scaled, value_cache, preferred_element_type=jnp.float32
    )
    top, total, mixed = joined((local_top, local_total, local_mixed), "gx", combine)
    own = (
        jnp.einsum("rgqd,rgd->rgq", grouped, fresh_key_rows, preferred_element_type=jnp.float32)
        * score_multiplier
    )
    largest = jnp.maximum(top, own)
    old_factor = jnp.exp(top - largest)
    own_weight = jnp.exp(own - largest)
    total = total * old_factor + own_weight
    mixed = (
        mixed * old_factor[..., None]
        + own_weight[..., None] * fresh_value_rows.astype(jnp.float32)[:, :, None, :]
    )
    attended = (mixed / total[..., None]).astype(jnp.bfloat16).reshape(requests, HEADS * HEAD_DIM)
    head_block = lax.all_to_all(attended, "gy", split_axis=1, concat_axis=0, tiled=True)
    projected = jnp.dot(head_block, w_out, preferred_element_type=jnp.float32) * out_scale
    attention_total = lax.psum(projected, "gy")
    new_residual = (widened + ffn_total + attention_total).astype(jnp.bfloat16)
    return new_residual


def solution(mesh):
    placed = (
        P("rep", "gx"),
        P("gy", "rep", "gx"),
        P("gx"),
        P("gx"),
        P("gx", "gy"),
        P("gy"),
        P("gx", "gy"),
        P("gy"),
        P(("rep", "gy"), None, "gx", None),
        P(("rep", "gy"), None, "gx", None),
        P(("rep", "gy"), None, "gx"),
        P(("rep", "gy"), None, "gx"),
        P(("rep", "gy")),
        P("gy", "gx"),
        P("gx"),
    )
    return jax.shard_map(
        body, mesh=mesh, in_specs=placed, out_specs=P("rep", "gx"), check_vma=False
    )
```

profile of v0, /device:TPU:0, one launch (start us, length us, event | category | flops | bytes accessed | tf_op | source)
XLA Modules:
  0.0 169.9 jit_solution(12676379669167503359)
XLA Ops:
  6.6 0.9 div.19
  7.5 9.5 %convolution_multiply_fusion.1 = f32[32,2048]{1,0:T(8,128)} fusion(bf16[4096,2048]{1,0:T(8,128)(2,1)} %param.21, bf16[32,4096]{1,0:T(8,128)(2,1)} %param.17, f32[4096]{0:T(1024)S(1)} %div.19, f32[2048]{0:T(1024)} %param.22), kind=kOutput, calls=%fused_computation.9 | convolution fusion | flops 537329664 | bytes 17326080 | tf_op jit(solution)/shard_map/dot_general | solution.py:54
  17.0 0.2 fusion.7
  17.2 0.4 convolution_multiply_fusion.3
  17.6 21.7 %all-reduce.1 = (f32[32]{0:T(128)S(1)}, f32[32,256]{1,0:T(8,128)S(1)}) all-reduce(f32[32]{0:T(128)S(1)} %fusion.7, f32[32,256]{1,0:T(8,128)S(1)} %convolution_multiply_fusion.3), channel_id=1, replica_groups=mesh['rep'=2,'gx'=4,'gy'=4] {'gx'}, use_global_device_ids=true, to_apply=%region_2.0 | all-reduce | flops 8224 | bytes 65792 | tf_op jit(solution)/shard_map/psum | solution.py:56
  39.4 16.3 %all-reduce.5.cloned.1.call-done = f32[32,2048]{1,0:T(8,128)} async-done(((f32[32,2048]{1,0:T(8,128)}), f32[32,2048]{1,0:T(8,128)}) %all-reduce.5.cloned.1.call-update) | async-done | bytes 262160 | tf_op jit(solution)/shard_map/psum | solution.py:56
  55.6 1.7 fusion.12
  57.3 3.3 %all-to-all-start = ((bf16[4,8,2048]{2,1,0:T(8,128)(2,1)}), bf16[4,8,2048]{2,1,0:T(8,128)(2,1)S(1)}, u32[]{:S(2)}, u32[]{:S(2)}) async-start(bf16[4,8,2048]{2,1,0:T(8,128)(2,1)} %fusion.12), calls=%async_computation | async-start | bytes 262144 | tf_op jit(solution)/shard_map/all_to_all | solution.py:61
  60.7 0.1 broadcast_compare_fusion
  60.8 4.5 %all-to-all-done = bf16[4,8,2048]{2,1,0:T(8,128)(2,1)S(1)} async-done(((bf16[4,8,2048]{2,1,0:T(8,128)(2,1)}), bf16[4,8,2048]{2,1,0:T(8,128)(2,1)S(1)}, u32[]{:S(2)}, u32[]{:S(2)}) %all-to-all-start) | async-done | bytes 131104 | tf_op jit(solution)/shard_map/all_to_all | solution.py:61
  65.3 2.0 %fusion.30 = (f32[8,4,16]{2,1,0:T(4,128)S(1)}, f32[8,4,16,128]{3,2,1,0:T(8,128)S(1)}) fusion(f32[8,4,128]{2,1,0:T(4,128)S(1)} %copy-done.2, bf16[8,4,128,128]{3,2,1,0:T(8,128)(2,1)} %param.25, pred[8,128]{1,0:T(8,128)(4,1)S(1)} %broadcast_compare_fusion, bf16[4,8,16,128]{3,1,2,0:T(8,128)(2,1)S(1)} %bitcast.62), kind=kOutput, calls=%fused_computation.52 | convolution fusion | flops 17038848 | bytes 1461248 | tf_op jit(solution)/shard_map/rgqd,rgsd->rgqs/dot_general | solution.py:71
  67.2 2.4 %fusion.13 = f32[8,4,16,128]{3,2,1,0:T(8,128)} fusion(bf16[8,4,128,128]{3,2,1,0:T(8,128)(2,1)} %param.26, f32[8,4,16,128]{3,2,1,0:T(8,128)S(1)} %get-tuple-element.75, f32[8,4,128]{2,1,0:T(4,128)S(1)} %copy-done.3, f32[8,4,16]{2,1,0:T(4,128)S(1)} %get-tuple-element.74, pred[8,128]{1,0:T(8,128)(4,1)S(1)} %broadcast_compare_fusion), kind=kOutput, calls=%fused_computation.27 | convolution fusion | flops 17039360 | bytes 1592320 | tf_op jit(solution)/shard_map/rgqs,rgsd->rgqd/dot_general | solution.py:82
  69.6 0.7 fusion.24
  70.3 3.2 %all-to-all-start.1 = ((bf16[4,8,256]{2,1,0:T(8,128)(2,1)}), bf16[4,8,256]{2,1,0:T(8,128)(2,1)S(1)}, u32[]{:S(2)}, u32[]{:S(2)}) async-start(bf16[4,8,256]{2,1,0:T(8,128)(2,1)} %fusion.24), calls=%async_computation.1 | async-start | bytes 32768 | tf_op jit(solution)/shard_map/all_to_all | solution.py:62
  73.6 3.8 %all-to-all-done.1 = bf16[4,8,256]{2,1,0:T(8,128)(2,1)S(1)} async-done(((bf16[4,8,256]{2,1,0:T(8,128)(2,1)}), bf16[4,8,256]{2,1,0:T(8,128)(2,1)S(1)}, u32[]{:S(2)}, u32[]{:S(2)}) %all-to-all-start.1) | async-done | bytes 16416 | tf_op jit(solution)/shard_map/all_to_all | solution.py:62
  77.4 13.6 %all-gather = f32[32,4,16]{2,1,0:T(4,128)S(1)} all-gather(f32[8,4,16]{2,1,0:T(4,128)S(1)} %get-tuple-element.74), channel_id=2, replica_groups=mesh['rep'=2,'gx'=4,'gy'=4] {'gx'}, dimensions={0}, use_global_device_ids=true | all-gather | bytes 10240 | tf_op jit(solution)/shard_map/all_gather | solution.py:17
  91.0 0.3 fusion.11
  91.3 13.4 %all-gather.1 = f32[32,4,16]{2,1,0:T(4,128)S(1)} all-gather(f32[8,4,16]{2,1,0:T(4,128)S(1)} %fusion.11), channel_id=3, replica_groups=mesh['rep'=2,'gx'=4,'gy'=4] {'gx'}, dimensions={0}, use_global_device_ids=true | all-gather | bytes 10240 | tf_op jit(solution)/shard_map/all_gather | solution.py:17
  104.7 0.8 fusion.19
  105.5 1.0 slice.40
  106.5 1.2 slice.43
  107.7 1.0 while.14
  107.7 0.3 fusion.39
  108.0 0.3 fusion.39
  108.4 0.3 fusion.39
  108.7 0.7 multiply_add_fusion
  109.4 0.3 divide_convert_fusion
  109.7 0.1 copy.39
  109.8 7.0 %all_to_all.54 = bf16[8,4,2048]{2,0,1:T(8,128)(2,1)S(1)} all-to-all(bf16[8,4,2048]{2,0,1:T(8,128)(2,1)S(1)} %bitcast.65), channel_id=1, replica_groups=mesh['rep'=2,'gx'=4,'gy'=4] {'gy'}, dimensions={1} | all-to-all | bytes 262144 | tf_op jit(solution)/shard_map/all_to_all | solution.py:99
  116.8 9.6 %convolution_multiply_fusion = f32[32,4096]{1,0:T(8,128)} fusion(bf16[2048,4096]{1,0:T(8,128)(2,1)} %param.30, f32[4096]{0:T(1024)} %param.31, bf16[8,4,2048]{2,0,1:T(8,128)(2,1)S(1)} %all_to_all.54), kind=kOutput, calls=%fused_computation.8 | convolution fusion | flops 537001984 | bytes 17448960 | tf_op jit(solution)/shard_map/dot_general | solution.py:100
  126.4 35.0 %all-reduce.7.cloned.1.call-done = (f32[32,4096]{1,0:T(8,128)}, f32[32,4096]{1,0:T(8,128)}) async-done(((f32[32,4096]{1,0:T(8,128)}, f32[32,4096]{1,0:T(8,128)}), (f32[32,4096]{1,0:T(8,128)}, f32[32,4096]{1,0:T(8,128)})) %all-reduce.7.cloned.1.call-update) | async-done | bytes 1048592 | tf_op jit(solution)/shard_map/psum | solution.py:101
  161.4 2.0 %fusion.6 = bf16[32,4096]{1,0:T(8,128)(2,1)} fusion(f32[32,4096]{1,0:T(8,128)} %get-tuple-element.61, f32[32,4096]{1,0:T(8,128)} %get-tuple-element.62, bf16[32,4096]{1,0:T(8,128)(2,1)S(1)} %copy-done.1), kind=kLoop, calls=%fused_computation.18 | loop fusion | flops 524288 | bytes 1572864 | tf_op jit(solution)/shard_map/convert_element_type | solution.py:102
  (30 shorter events, 0.4 us)
Async XLA Ops:
  6.5 10.6 %copy-start = (bf16[4096,256]{1,0:T(8,128)(2,1)S(1)}, bf16[4096,256]{1,0:T(8,128)(2,1)}, u32[]{:S(2)}) copy-start(bf16[4096,256]{1,0:T(8,128)(2,1)} %param.23) | copy-start | bytes 6291460
  6.5 10.5 %copy-start.1 = (bf16[32,4096]{1,0:T(8,128)(2,1)S(1)}, bf16[32,4096]{1,0:T(8,128)(2,1)}, u32[]{:S(2)}) copy-start(bf16[32,4096]{1,0:T(8,128)(2,1)} %param.17) | copy-start | bytes 786436
  6.5 10.6 %copy-start.4 = (f32[256]{0:T(256)S(1)}, f32[256]{0:T(256)}, u32[]{:S(2)}) copy-start(f32[256]{0:T(256)} %param.24) | copy-start | bytes 3076
  6.5 54.2 %copy-start.5 = (s32[8]{0:T(128)S(1)}, s32[8]{0:T(128)}, u32[]{:S(2)}) copy-start(s32[8]{0:T(128)} %param.29) | copy-start | bytes 100
  6.5 58.7 %copy-start.2 = (f32[8,4,128]{2,1,0:T(4,128)S(1)}, f32[8,4,128]{2,1,0:T(4,128)}, u32[]{:S(2)}) copy-start(f32[8,4,128]{2,1,0:T(4,128)} %param.27) | copy-start | bytes 49156
  6.5 60.7 %copy-start.3 = (f32[8,4,128]{2,1,0:T(4,128)S(1)}, f32[8,4,128]{2,1,0:T(4,128)}, u32[]{:S(2)}) copy-start(f32[8,4,128]{2,1,0:T(4,128)} %param.28) | copy-start | bytes 49156
  6.6 49.1 %all-reduce.5.cloned.1.call-start = ((), (), s32[]{:S(2)}) async-start(), calls=%async_computation.3 | async-start | bytes 524288 | tf_op jit(solution)/shard_map/psum | solution.py:56
  57.3 7.9 %all-to-all-start = ((bf16[4,8,2048]{2,1,0:T(8,128)(2,1)}), bf16[4,8,2048]{2,1,0:T(8,128)(2,1)S(1)}, u32[]{:S(2)}, u32[]{:S(2)}) async-start(bf16[4,8,2048]{2,1,0:T(8,128)(2,1)} %fusion.12), calls=%async_computation | async-start | bytes 262144 | tf_op jit(solution)/shard_map/all_to_all | solution.py:61
  60.7 44.8 %all-gather.5.cloned.1.call-start = ((), (), s32[]{:S(2)}) async-start(), calls=%async_computation.4 | async-start | bytes 1310720 | tf_op jit(solution)/shard_map/all_gather | solution.py:17
  70.3 7.1 %all-to-all-start.1 = ((bf16[4,8,256]{2,1,0:T(8,128)(2,1)}), bf16[4,8,256]{2,1,0:T(8,128)(2,1)S(1)}, u32[]{:S(2)}, u32[]{:S(2)}) async-start(bf16[4,8,256]{2,1,0:T(8,128)(2,1)} %fusion.24), calls=%async_computation.1 | async-start | bytes 32768 | tf_op jit(solution)/shard_map/all_to_all | solution.py:62
  73.6 87.9 %all-reduce.7.cloned.1.call-start = ((), (), s32[]{:S(2)}) async-start(), calls=%async_computation.5 | async-start | bytes 2097152 | tf_op jit(solution)/shard_map/psum | solution.py:101
Sparse Core Ops, SparseCore 0:
  17.1 38.4 all-reduce.4
  69.8 28.3 all-gather.4
  126.5 34.8 all-reduce.6
where the time goes:
time: 171 us; the launch traced here: 170 us
  waiting for transfers between devices  59.6 us (35%)
  blocking collectives  55.7 us (33%)
  matrix products  24.6 us (14%)
  between operations  13.3 us (8%)
  other arithmetic  7.72 us (5%)
  starting transfers between devices  6.68 us (4%)
  local copies, waits for them, and re-layouts  2.3 us (1%)
    psum x1, waiting for transfers between devices, body(): attention_total = lax.psum(projected, 'gy')  35 us
    all_gather x2, blocking collectives, joined(): pieces = jax.tree.map(lambda part: lax.all_gather(part, axis), value)  27 us
    psum x1, blocking collectives, body(): lax.psum((query_part, keyval_part, squares), 'gx')  21.7 us
    psum x1, waiting for transfers between devices, body(): lax.psum((query_part, keyval_part, squares), 'gx')  16.3 us
    dot_general x1, matrix products, body(): jnp.dot(head_block, w_out, preferred_element_type=jnp.float32) * out_scale  9.59 us
    dot_general x1, matrix products, body(): jnp.dot(smoothed, w_query, preferred_element_type=jnp.float32) * query_scale  9.46 us
    all_to_all x1, blocking collectives, body(): lax.all_to_all(attended, 'gy', split_axis=1, concat_axis=0, tiled=True)  7.02 us
    all_to_all x1, waiting for transfers between devices, body(): lax.all_to_all(query_rows, 'gy', split_axis=0, concat_axis=1, tiled=True)  4.46 us
  transfers between devices with their start and end apart: 5, of which 4 were waited for; matrix products, arithmetic and copies ran while one was open for 1% of the time, Pallas kernels for 0%

commit v1 on v0

--- a/solution.py
+++ b/solution.py
@@ -7,10 +7,113 @@
 HEADS = 64
 KV_HEADS = 4
 HEAD_DIM = 128
-
-
+GROUP = HEADS // KV_HEADS
 EPSILON = 1e-05
 NEGATIVE = -1e30
+f32 = jnp.float32
+bf16 = jnp.bfloat16
+
+
+def partners(n, offset):
+    return [(i, i ^ offset) for i in range(n)]
+
+
+def ordered(pieces, me):
+    n = len(pieces)
+    return [lax.select_n(me, *[pieces[j ^ i] for i in range(n)]) for j in range(n)]
+
+
+def exchange(chunks, axis, n):
+    me = lax.axis_index(axis)
+    own = lax.dynamic_index_in_dim(chunks, me, 0, keepdims=False)
+    return [own] + [
+        lax.ppermute(lax.dynamic_index_in_dim(chunks, me ^ k, 0, keepdims=False), axis, partners(n, k))
+        for k in range(1, n)
+    ]
+
+
+def gather(value, axis, n):
+    return [value] + [lax.ppermute(value, axis, partners(n, k)) for k in range(1, n)]
+
+
+def swap(value, axis, n, offset):
+    return lax.ppermute(value, axis, partners(n, offset))
+
+
+def body(n_gx, n_gy, residual, ffn_partial, norm_gain, smooth_scale, w_query, query_scale, w_keyval, keyval_scale,
+         key_cache, value_cache, key_scale, value_scale, lengths, w_out, out_scale):
+    gx, gy = lax.axis_index("gx"), lax.axis_index("gy")
+    rows, width = residual.shape
+    requests = rows // n_gy
+    widened = residual.astype(f32)
+    squares = jnp.sum(widened * widened, axis=1)
+    smoothed = (widened * (norm_gain / smooth_scale)).astype(bf16)
+    query_part = jnp.dot(smoothed, w_query, preferred_element_type=f32) * query_scale
+    keyval_part = jnp.dot(smoothed, w_keyval, preferred_element_type=f32) * keyval_scale
+    qc, kc = query_part.shape[1] // n_gx, keyval_part.shape[1] // n_gx
+    pad = -(qc + kc + 1) % 128
+    packed = jnp.concatenate([
+        query_part.reshape(rows, n_gx, qc), keyval_part.reshape(rows, n_gx, kc),
+        jnp.broadcast_to(squares[:, None, None], (rows, n_gx, 1)), jnp.zeros((rows, n_gx, pad), f32)], axis=2)
+    pieces = exchange(packed.transpose(1, 0, 2), "gx", n_gx)
+    summed = sum(pieces[1:], pieces[0])
+    row_scale = lax.rsqrt(summed[:, qc + kc] / D + EPSILON)[:, None]
+    rounded = (row_scale * summed).astype(bf16)[:, : qc + kc]
+    rounded = jnp.pad(rounded, ((0, 0), (0, pad + 1)))
+    mine = jnp.stack(ordered(exchange(rounded.reshape(n_gy, requests, -1), "gy", n_gy), gy))
+    everything = jnp.stack(ordered(gather(mine, "gx", n_gx), gx))
+    query_vectors = everything[..., :qc].transpose(2, 1, 0, 3).reshape(requests, KV_HEADS, GROUP, HEAD_DIM)
+    keyvals = everything[..., qc : qc + kc].transpose(2, 1, 0, 3).reshape(requests, 2 * KV_HEADS, HEAD_DIM)
+    fresh_keys, fresh_values = keyvals[:, :KV_HEADS], keyvals[:, KV_HEADS:]
+
+    local = key_cache.shape[2]
+    multiplier = HEAD_DIM ** (-0.5)
+    logits = jnp.einsum("rgqd,rgsd->rgqs", query_vectors, key_cache, preferred_element_type=f32)
+    logits = logits * key_scale[:, :, None, :] * multiplier
+    position = gx * local + jnp.arange(local, dtype=jnp.int32)
+    visible = (position[None, :] < lengths[:, None])[:, None, None, :]
+    logits = jnp.where(visible, logits, NEGATIVE)
+    own = jnp.einsum("rgqd,rgd->rgq", query_vectors, fresh_keys, preferred_element_type=f32) * multiplier
+    own = jnp.where(gx == 0, own, NEGATIVE)
+    top = jnp.maximum(jnp.max(logits, axis=-1), own)
+    weights = jnp.where(visible, jnp.exp(logits - top[..., None]), 0.0)
+    own_weight = jnp.where(gx == 0, jnp.exp(own - top), 0.0)
+    total = jnp.sum(weights, axis=-1) + own_weight
+    scaled = (weights * value_scale[:, :, None, :]).astype(bf16)
+    mixed = jnp.einsum("rgqs,rgsd->rgqd", scaled, value_cache, preferred_element_type=f32)
+    mixed = mixed + own_weight[..., None] * fresh_values.astype(f32)[:, :, None, :]
+
+    share = requests // n_gx
+    mixed = mixed.reshape(n_gx, share * HEADS, HEAD_DIM)
+    stats = jnp.concatenate([top.reshape(n_gx, share * HEADS // HEAD_DIM, HEAD_DIM),
+                             total.reshape(n_gx, share * HEADS // HEAD_DIM, HEAD_DIM)], axis=1)
+    extra = stats.shape[1]
+    message = jnp.concatenate([mixed, stats, jnp.zeros((n_gx, -extra % 8, HEAD_DIM), f32)], axis=1)
+    parts = exchange(message, "gx", n_gx)
+    count = share * HEADS
+    tops = [part[count : count + extra // 2].reshape(count) for part in parts]
+    totals = [part[count + extra // 2 : count + extra].reshape(count) for part in parts]
+    largest = tops[0]
+    for other in tops[1:]:
+        largest = jnp.maximum(largest, other)
+    factors = [jnp.exp(t - largest) for t in tops]
+    total = sum(f * t for f, t in zip(factors, totals))
+    mixed = sum(f[:, None] * part[:count] for f, part in zip(factors, parts))
+    attended = (mixed / total[:, None]).astype(bf16)
+    attended = attended.reshape(share, n_gy, HEADS // n_gy * HEAD_DIM).transpose(1, 0, 2)
+    blocks = jnp.stack(ordered(exchange(attended, "gy", n_gy), gy))
+    blocks = jnp.stack(ordered(gather(blocks, "gx", n_gx), gx), axis=1)
+    projected = jnp.dot(blocks.reshape(rows, -1), w_out, preferred_element_type=f32) * out_scale
+
+    term = (projected + ffn_partial[0]).reshape(2, rows // 2, width)
+    core = gy & 1
+    kept = lax.dynamic_index_in_dim(term, core, 0, keepdims=False)
+    given = lax.dynamic_index_in_dim(term, 1 - core, 0, keepdims=False)
+    chip = kept + swap(given, "gy", n_gy, 1)
+    whole = chip + swap(chip, "gy", n_gy, 2)
+    half = lax.dynamic_slice_in_dim(widened, core * (rows // 2), rows // 2, 0)
+    half = (half + whole).astype(bf16)
+    return jnp.concatenate(ordered([half, swap(half, "gy", n_gy, 1)], core))
 
 
 def joined(value, axis, join):
@@ -30,7 +133,7 @@
     return (top, total, mixed)
 
 
-def body(
+def plain_body(
     residual,
     ffn_partial,
     norm_gain,
@@ -105,22 +208,15 @@
 
 def solution(mesh):
     placed = (
-        P("rep", "gx"),
-        P("gy", "rep", "gx"),
-        P("gx"),
-        P("gx"),
-        P("gx", "gy"),
-        P("gy"),
-        P("gx", "gy"),
-        P("gy"),
-        P(("rep", "gy"), None, "gx", None),
-        P(("rep", "gy"), None, "gx", None),
-        P(("rep", "gy"), None, "gx"),
-        P(("rep", "gy"), None, "gx"),
-        P(("rep", "gy")),
-        P("gy", "gx"),
-        P("gx"),
-    )
-    return jax.shard_map(
-        body, mesh=mesh, in_specs=placed, out_specs=P("rep", "gx"), check_vma=False
-    )
+        P("rep", "gx"), P("gy", "rep", "gx"), P("gx"), P("gx"), P("gx", "gy"), P("gy"), P("gx", "gy"), P("gy"),
+        P(("rep", "gy"), None, "gx", None), P(("rep", "gy"), None, "gx", None),
+        P(("rep", "gy"), None, "gx"), P(("rep", "gy"), None, "gx"), P(("rep", "gy")), P("gy", "gx"), P("gx"),
+    )
+    n_gx, n_gy = mesh.shape["gx"], mesh.shape["gy"]
+
+    def run(*arrays):
+        if n_gx == 4 and n_gy == 4:
+            return body(n_gx, n_gy, *arrays)
+        return plain_body(*arrays)
+
+    return jax.shard_map(run, mesh=mesh, in_specs=placed, out_specs=P("rep", "gx"), check_vma=False)

time: 171 us -> 97.6 us (0.57)
  blocking collectives: 55.7 us -> 0 us
  waiting for transfers between devices: 59.6 us -> 32.3 us
  starting transfers between devices: 6.68 us -> 21.9 us
  between operations: 13.3 us -> 0.36 us
  other arithmetic: 7.72 us -> 12.8 us
  local copies, waits for them, and re-layouts: 2.3 us -> 6.58 us
    psum x2 -> x0, waiting for transfers between devices: 51.3 us -> none  [the longest x1 35 us: body(): attention_total = lax.psum(projected, 'gy')]
    ppermute x0 -> x21, waiting for transfers between devices: none -> 32.3 us  [the longest x12 16.4 us: exchange(): lax.ppermute(lax.dynamic_index_in_dim(chunks, me ^ k, 0, keepdims=False),...]
    all_gather x2 -> x0, blocking collectives: 27 us -> none  [joined(): pieces = jax.tree.map(lambda part: lax.all_gather(part, axis), value)]
    ppermute x0 -> x21, starting transfers between devices: none -> 21.9 us  [the longest x12 13.4 us: exchange(): lax.ppermute(lax.dynamic_index_in_dim(chunks, me ^ k, 0, keepdims=False),...]
    psum x1 -> x0, blocking collectives: 21.7 us -> none  [body(): lax.psum((query_part, keyval_part, squares), 'gx')]
    all_to_all x2 -> x0, waiting for transfers between devices: 8.24 us -> none  [the longest x1 4.46 us: body(): lax.all_to_all(query_rows, 'gy', split_axis=0, concat_axis=1, tiled=True)]
    all_to_all x1 -> x0, blocking collectives: 7.02 us -> none  [body(): lax.all_to_all(attended, 'gy', split_axis=1, concat_axis=0, tiled=True)]
    all_to_all x2 -> x0, starting transfers between devices: 6.56 us -> none  [the longest x1 3.33 us: body(): lax.all_to_all(query_rows, 'gy', split_axis=0, concat_axis=1, tiled=True)]
  transfers between devices with their start and end apart: 5 -> 21, of which waited for: 4 -> 14; matrix products, arithmetic and copies ran while one was open for 1% -> 2% of each run, Pallas kernels for 0% -> 0%
where the time goes in v1:
time: 97.6 us; the launch traced here: 97 us
  waiting for transfers between devices  32.3 us (33%)
  matrix products  23.1 us (24%)
  starting transfers between devices  21.9 us (22%)
  other arithmetic  12.8 us (13%)
  local copies, waits for them, and re-layouts  6.58 us (7%)
    ppermute x12, waiting for transfers between devices, exchange(): lax.ppermute(lax.dynamic_index_in_dim(chunks, me ^ k, 0, keepdims=False),...  16.4 us
    ppermute x12, starting transfers between devices, exchange(): lax.ppermute(lax.dynamic_index_in_dim(chunks, me ^ k, 0, keepdims=False),...  13.4 us
    ppermute x3, waiting for transfers between devices, swap(): return lax.ppermute(value, axis, partners(n, offset))  10.3 us
    dot_general x1, matrix products, body(): jnp.dot(blocks.reshape(rows, -1), w_out, preferred_element_type=f32)  8.94 us
    dot_general x1, matrix products, body(): jnp.dot(smoothed, w_query, preferred_element_type=f32) * query_scale  8.75 us
    ppermute x6, starting transfers between devices, gather(): lax.ppermute(value, axis, partners(n, k))  7.42 us
    ppermute x6, waiting for transfers between devices, gather(): lax.ppermute(value, axis, partners(n, k))  5.53 us
    dot_general x1, matrix products, body(): jnp.einsum('rgqd,rgsd->rgqs', query_vectors, key_cache, preferred_element...  2.09 us
  transfers between devices with their start and end apart: 21, of which 14 were waited for; matrix products, arithmetic and copies ran while one was open for 2% of the time, Pallas kernels for 0%

profile of v1, /device:TPU:0, one launch (start us, length us, event | category | flops | bytes accessed | tf_op | source)
XLA Modules:
  0.0 97.0 jit_solution(15189931278754976747)
XLA Ops:
  0.0 1.3 %multiply_reduce_fusion = f32[32]{0:T(128)S(1)} fusion(bf16[32,4096]{1,0:T(8,128)(2,1)} %param.15), kind=kLoop, calls=%fused_computation.8 | loop fusion | flops 393184 | bytes 262272 | tf_op jit(solution)/shard_map/reduce_sum | solution.py:49
  2.0 1.4 %convolution_multiply_fusion.3 = f32[32,256]{1,0:T(8,128)S(1)} fusion(bf16[4096,256]{1,0:T(8,128)(2,1)S(1)} %copy-done, f32[4096]{0:T(1024)S(1)} %div.17, bf16[32,4096]{1,0:T(8,128)(2,1)} %param.15, f32[256]{0:T(256)} %param.22), kind=kOutput, calls=%fused_computation.7 | convolution fusion | flops 67510272 | bytes 2409472 | tf_op jit(solution)/shard_map/dot_general | solution.py:52
  3.5 8.7 %convolution_multiply_fusion.1 = f32[32,2048]{1,0:T(8,128)S(1)} fusion(bf16[4096,2048]{1,0:T(8,128)(2,1)} %param.19, f32[4096]{0:T(1024)S(1)} %div.17, bf16[32,4096]{1,0:T(8,128)(2,1)} %param.15, f32[2048]{0:T(1024)} %param.20), kind=kOutput, calls=%fused_computation.2 | convolution fusion | flops 537329664 | bytes 17326080 | tf_op jit(solution)/shard_map/dot_general | solution.py:51
  13.3 1.1 %maximum_maximum_fusion = f32[32,4,640]{2,1,0:T(4,128)S(1)} fusion(f32[32,4,1]{2,1,0:T(4,128)S(1)} %broadcast_in_dim.32, f32[32,4,64]{2,1,0:T(4,128)S(1)} %reshape.236, f32[32,4,512]{2,1,0:T(4,128)} %reshape.235, f32[640]{0:T(1024)S(1)} %pad.30.clone), kind=kLoop, calls=%fused_computation.10 | loop fusion | flops 245760 | bytes 625664 | tf_op jit(solution)/shard_map/concatenate | solution.py:55
  14.7 3.1 %collective-permute-start = (f32[32,640]{1,0:T(8,128)S(1)}, f32[32,640]{1,0:T(8,128)S(1)}, u32[]{:S(2)}, u32[]{:S(2)}) collective-permute-start(f32[32,640]{1,0:T(8,128)S(1)} %bitcast.191), channel_id=1, source_target_pairs={{0,4},{4,0},{8,12},{12,8},{1,5},{5,1},{9,13},{13,9},{2,6},{6,2},{1... | collective-permute-start | bytes 245768 | tf_op jit(solution)/shard_map/ppermute | solution.py:30
  17.8 2.6 %collective-permute-start.1 = (f32[32,640]{1,0:T(8,128)S(1)}, f32[32,640]{1,0:T(8,128)}, u32[]{:S(2)}, u32[]{:S(2)}) collective-permute-start(f32[32,640]{1,0:T(8,128)S(1)} %bitcast.192), channel_id=1, source_target_pairs={{0,8},{4,12},{8,0},{12,4},{1,9},{5,13},{9,1},{13,5},{2,10},{6,14},... | collective-permute-start | bytes 245768 | tf_op jit(solution)/shard_map/ppermute | solution.py:30
  20.4 6.7 %collective-permute-done.1 = f32[32,640]{1,0:T(8,128)} collective-permute-done((f32[32,640]{1,0:T(8,128)S(1)}, f32[32,640]{1,0:T(8,128)}, u32[]{:S(2)}, u32[]{:S(2)}) %collective-permute-start.1) | collective-permute-done | bytes 81952 | tf_op jit(solution)/shard_map/ppermute | solution.py:30
  29.0 1.6 %collective-permute-start.4 = (bf16[8,640]{1,0:T(8,128)(2,1)S(1)}, bf16[8,640]{1,0:T(8,128)(2,1)S(1)}, u32[]{:S(2)}, u32[]{:S(2)}) collective-permute-start(bf16[8,640]{1,0:T(8,128)(2,1)S(1)} %get-tuple-element.34), channel_id=1, source_target_pairs={{0,2},{1,3},{2,0},{3,1},{4,6},{5,7},{6,4},{7,5},{8,10},{9,11},{10,... | collective-permute-start | bytes 30728 | tf_op jit(solution)/shard_map/ppermute | solution.py:30
  31.2 1.5 %collective-permute-done.4 = bf16[8,640]{1,0:T(8,128)(2,1)S(1)} collective-permute-done((bf16[8,640]{1,0:T(8,128)(2,1)S(1)}, bf16[8,640]{1,0:T(8,128)(2,1)S(1)}, u32[]{:S(2)}, u32[]{:S(2)}) %collective-permute-start.4) | collective-permute-done | bytes 10272 | tf_op jit(solution)/shard_map/ppermute | solution.py:30
  33.7 2.5 %collective-permute-start.7 = (bf16[4,8,640]{2,1,0:T(8,128)(2,1)S(1)}, bf16[4,8,640]{2,1,0:T(8,128)(2,1)S(1)}, u32[]{:S(2)}, u32[]{:S(2)}) collective-permute-start(bf16[4,8,640]{2,1,0:T(8,128)(2,1)S(1)} %pad_maximum_fusion.3), channel_id=1, source_target_pairs={{0,8},{4,12},{8,0},{12,4},{1,9},{5,13},{9,1},{13,5},{2,10},{6,14},... | collective-permute-start | bytes 122888 | tf_op jit(solution)/shard_map/ppermute | solution.py:36
  36.2 1.4 %collective-permute-start.8 = (bf16[4,8,640]{2,1,0:T(8,128)(2,1)S(1)}, bf16[4,8,640]{2,1,0:T(8,128)(2,1)S(1)}, u32[]{:S(2)}, u32[]{:S(2)}) collective-permute-start(bf16[4,8,640]{2,1,0:T(8,128)(2,1)S(1)} %pad_maximum_fusion.3), channel_id=1, source_target_pairs={{0,12},{4,8},{8,4},{12,0},{1,13},{5,9},{9,5},{13,1},{2,14},{6,10},... | collective-permute-start | bytes 122888 | tf_op jit(solution)/shard_map/ppermute | solution.py:36
  37.6 1.3 %broadcast_compare_fusion = pred[8,128]{1,0:T(8,128)(4,1)} fusion(s32[128]{0:T(128)S(1)} %iota_add_fusion, s32[8]{0:T(128)} %param.27), kind=kLoop, calls=%fused_computation.128 | loop fusion | flops 1024 | bytes 1568 | tf_op jit(solution)/shard_map/lt | solution.py:74
  39.5 2.5 %collective-permute-done.8 = bf16[4,8,640]{2,1,0:T(8,128)(2,1)S(1)} collective-permute-done((bf16[4,8,640]{2,1,0:T(8,128)(2,1)S(1)}, bf16[4,8,640]{2,1,0:T(8,128)(2,1)S(1)}, u32[]{:S(2)}, u32[]{:S(2)}) %collective-permute-start.8) | collective-permute-done | bytes 40992 | tf_op jit(solution)/shard_map/ppermute | solution.py:36
  44.5 1.4 %copy.33 = bf16[8,4,4,64]{3,2,1,0:T(4,128)(2,1)} copy(bf16[8,4,4,64]{3,0,1,2:T(8,128)(2,1)} %maximum_bitcast_fusion) | data formatting | bytes 32768 | tf_op jit(solution)/shard_map/transpose | solution.py:66
  47.5 2.1 %fusion.51 = (f32[8,4,16]{2,1,0:T(4,128)S(1)}, f32[8,4,16,128]{3,2,1,0:T(8,128)}) fusion(f32[8,4,128]{2,1,0:T(4,128)} %param.25, bf16[8,4,16,128]{3,2,1,0:T(8,128)(2,1)S(1)} %reshape.238, bf16[8,4,128,128]{3,2,1,0:T(8,128)(2,1)S(1)} %copy-done.2, pred[8,128]{1,0:T(8,128)(4,1)} %broadcast_compare_fusion), kind=kOutput, calls=%fused_computation.152 | convolution fusion | flops 17038848 | bytes 1461248 | tf_op jit(solution)/shard_map/rgqd,rgsd->rgqs/dot_general | solution.py:71
  49.7 1.2 %fusion.3 = f32[8,4,16]{2,1,0:T(4,128)S(1)} fusion(f32[8,4,16,128]{3,2,1,0:T(8,128)} %get-tuple-element.47, f32[8,4,16]{2,1,0:T(4,128)S(1)} %fusion.27, pred[8,128]{1,0:T(8,128)(4,1)} %broadcast_compare_fusion), kind=kLoop, calls=%fused_computation.18 | loop fusion | flops 196096 | bytes 267264 | tf_op jit(solution)/shard_map/reduce_sum | solution.py:81
  51.8 1.7 %convolution_add_fusion = f32[8,4,16,128]{3,2,1,0:T(8,128)S(1)} fusion(bf16[8,4,128,128]{3,2,1,0:T(8,128)(2,1)} %param.24, f32[8,4,16,128]{3,2,1,0:T(8,128)} %get-tuple-element.47, f32[8,4,128]{2,1,0:T(4,128)} %get-tuple-element.44, f32[8,4,16]{2,1,0:T(4,128)S(1)} %get-tuple-element.13, f32[8,4,128]{2,1,0:T(4,128)} %param.26, f32[8,4,16]{2,1,0:T(4,128)S(1)} %fusion.27, ...), kind=kOutput, calls=%fused_computation.3 | convolution fusion | flops 17170432 | bytes 1610752 | tf_op jit(solution)/shard_map/rgqs,rgsd->rgqd/dot_general | solution.py:83
  54.4 2.4 %collective-permute-start.11 = (f32[136,128]{1,0:T(8,128)S(1)}, f32[136,128]{1,0:T(8,128)S(1)}, u32[]{:S(2)}, u32[]{:S(2)}) collective-permute-start(f32[136,128]{1,0:T(8,128)S(1)} %get-tuple-element.19), channel_id=1, source_target_pairs={{0,12},{4,8},{8,4},{12,0},{1,13},{5,9},{9,5},{13,1},{2,14},{6,10},... | collective-permute-start | bytes 208904 | tf_op jit(solution)/shard_map/ppermute | solution.py:30
  56.8 1.0 %collective-permute-start.10 = (f32[136,128]{1,0:T(8,128)S(1)}, f32[136,128]{1,0:T(8,128)S(1)}, u32[]{:S(2)}, u32[]{:S(2)}) collective-permute-start(f32[136,128]{1,0:T(8,128)S(1)} %get-tuple-element.20), channel_id=1, source_target_pairs={{0,8},{4,12},{8,0},{12,4},{1,9},{5,13},{9,1},{13,5},{2,10},{6,14},... | collective-permute-start | bytes 208904 | tf_op jit(solution)/shard_map/ppermute | solution.py:30
  57.8 1.6 %collective-permute-done.9 = f32[136,128]{1,0:T(8,128)S(1)} collective-permute-done((f32[136,128]{1,0:T(8,128)S(1)}, f32[136,128]{1,0:T(8,128)S(1)}, u32[]{:S(2)}, u32[]{:S(2)}) %collective-permute-start.9) | collective-permute-done | bytes 69664 | tf_op jit(solution)/shard_map/ppermute | solution.py:30
  59.4 1.2 %collective-permute-done.11 = f32[136,128]{1,0:T(8,128)S(1)} collective-permute-done((f32[136,128]{1,0:T(8,128)S(1)}, f32[136,128]{1,0:T(8,128)S(1)}, u32[]{:S(2)}, u32[]{:S(2)}) %collective-permute-start.11) | collective-permute-done | bytes 69664 | tf_op jit(solution)/shard_map/ppermute | solution.py:30
  60.6 2.1 %collective-permute-done.10 = f32[136,128]{1,0:T(8,128)S(1)} collective-permute-done((f32[136,128]{1,0:T(8,128)S(1)}, f32[136,128]{1,0:T(8,128)S(1)}, u32[]{:S(2)}, u32[]{:S(2)}) %collective-permute-start.10) | collective-permute-done | bytes 69664 | tf_op jit(solution)/shard_map/ppermute | solution.py:30
  63.2 1.1 %collective-permute-start.13 = (bf16[2,2048]{1,0:T(2,128)(2,1)S(1)}, bf16[2,2048]{1,0:T(2,128)(2,1)S(1)}, u32[]{:S(2)}, u32[]{:S(2)}) collective-permute-start(bf16[2,2048]{1,0:T(2,128)(2,1)S(1)} %bitcast.197), channel_id=1, source_target_pairs={{0,2},{1,3},{2,0},{3,1},{4,6},{5,7},{6,4},{7,5},{8,10},{9,11},{10,... | collective-permute-start | bytes 24584 | tf_op jit(solution)/shard_map/ppermute | solution.py:30
  65.1 1.9 %collective-permute-done.13 = bf16[2,2048]{1,0:T(2,128)(2,1)S(1)} collective-permute-done((bf16[2,2048]{1,0:T(2,128)(2,1)S(1)}, bf16[2,2048]{1,0:T(2,128)(2,1)S(1)}, u32[]{:S(2)}, u32[]{:S(2)}) %collective-permute-start.13) | collective-permute-done | bytes 8224 | tf_op jit(solution)/shard_map/ppermute | solution.py:30
  68.1 1.7 %collective-permute-start.17 = (bf16[4,2,2048]{2,1,0:T(2,128)(2,1)S(1)}, bf16[4,2,2048]{2,1,0:T(2,128)(2,1)S(1)}, u32[]{:S(2)}, u32[]{:S(2)}) collective-permute-start(bf16[4,2,2048]{2,1,0:T(2,128)(2,1)S(1)} %pad_maximum_fusion.4), channel_id=1, source_target_pairs={{0,12},{4,8},{8,4},{12,0},{1,13},{5,9},{9,5},{13,1},{2,14},{6,10},... | collective-permute-start | bytes 98312 | tf_op jit(solution)/shard_map/ppermute | solution.py:36
  69.8 1.3 %collective-permute-start.15 = (bf16[4,2,2048]{2,1,0:T(2,128)(2,1)S(1)}, bf16[4,2,2048]{2,1,0:T(2,128)(2,1)S(1)}, u32[]{:S(2)}, u32[]{:S(2)}) collective-permute-start(bf16[4,2,2048]{2,1,0:T(2,128)(2,1)S(1)} %pad_maximum_fusion.4), channel_id=1, source_target_pairs={{0,4},{4,0},{8,12},{12,8},{1,5},{5,1},{9,13},{13,9},{2,6},{6,2},{1... | collective-permute-start | bytes 98312 | tf_op jit(solution)/shard_map/ppermute | solution.py:36
  71.1 1.9 %collective-permute-done.16 = bf16[4,2,2048]{2,1,0:T(2,128)(2,1)S(1)} collective-permute-done((bf16[4,2,2048]{2,1,0:T(2,128)(2,1)S(1)}, bf16[4,2,2048]{2,1,0:T(2,128)(2,1)S(1)}, u32[]{:S(2)}, u32[]{:S(2)}) %collective-permute-start.16) | collective-permute-done | bytes 32800 | tf_op jit(solution)/shard_map/ppermute | solution.py:36
  73.0 1.1 %collective-permute-done.17 = bf16[4,2,2048]{2,1,0:T(2,128)(2,1)S(1)} collective-permute-done((bf16[4,2,2048]{2,1,0:T(2,128)(2,1)S(1)}, bf16[4,2,2048]{2,1,0:T(2,128)(2,1)S(1)}, u32[]{:S(2)}, u32[]{:S(2)}) %collective-permute-start.17) | collective-permute-done | bytes 32800 | tf_op jit(solution)/shard_map/ppermute | solution.py:36
  74.7 8.9 %fusion = f32[32,4096]{1,0:T(8,128)S(1)} fusion(bf16[32,2048]{1,0:T(8,128)(2,1)S(1)} %reshape.252, bf16[2048,4096]{1,0:T(8,128)(2,1)} %param.28, f32[1,32,4096]{2,1,0:T(8,128)} %param.16, f32[4096]{0:T(1024)} %param.29), kind=kOutput, calls=%fused_computation.1 | convolution fusion | flops 537133056 | bytes 17973248 | tf_op jit(solution)/shard_map/dot_general | solution.py:106
  83.8 1.5 %collective-permute-done.18 = f32[16,4096]{1,0:T(8,128)S(1)} collective-permute-done((f32[16,4096]{1,0:T(8,128)S(1)}, f32[16,4096]{1,0:T(8,128)S(1)}, u32[]{:S(2)}, u32[]{:S(2)}) %collective-permute-start.18) | collective-permute-done | bytes 262176 | tf_op jit(solution)/shard_map/ppermute | solution.py:40
  86.3 7.5 %collective-permute-done.19 = f32[16,4096]{1,0:T(8,128)} collective-permute-done((f32[16,4096]{1,0:T(8,128)S(1)}, f32[16,4096]{1,0:T(8,128)}, u32[]{:S(2)}, u32[]{:S(2)}) %collective-permute-start.19) | collective-permute-done | bytes 262176 | tf_op jit(solution)/shard_map/ppermute | solution.py:40
  94.9 1.3 %collective-permute-done.20 = bf16[16,4096]{1,0:T(8,128)(2,1)S(1)} collective-permute-done((bf16[16,4096]{1,0:T(8,128)(2,1)S(1)}, bf16[16,4096]{1,0:T(8,128)(2,1)S(1)}, u32[]{:S(2)}, u32[]{:S(2)}) %collective-permute-start.20) | collective-permute-done | bytes 131104 | tf_op jit(solution)/shard_map/ppermute | solution.py:40
  (83 shorter events, 18.0 us)
Async XLA Ops:
  0.0 2.0 %copy-start = (bf16[4096,256]{1,0:T(8,128)(2,1)S(1)}, bf16[4096,256]{1,0:T(8,128)(2,1)}, u32[]{:S(2)}) copy-start(bf16[4096,256]{1,0:T(8,128)(2,1)} %param.21) | copy-start | bytes 6291460
  0.0 47.5 %copy-start.2 = (bf16[8,4,128,128]{3,2,1,0:T(8,128)(2,1)S(1)}, bf16[8,4,128,128]{3,2,1,0:T(8,128)(2,1)}, u32[]{:S(2)}) copy-start(bf16[8,4,128,128]{3,2,1,0:T(8,128)(2,1)} %param.23) | copy-start | bytes 3145732
  14.7 5.7 %collective-permute-start = (f32[32,640]{1,0:T(8,128)S(1)}, f32[32,640]{1,0:T(8,128)S(1)}, u32[]{:S(2)}, u32[]{:S(2)}) collective-permute-start(f32[32,640]{1,0:T(8,128)S(1)} %bitcast.191), channel_id=1, source_target_pairs={{0,4},{4,0},{8,12},{12,8},{1,5},{5,1},{9,13},{13,9},{2,6},{6,2},{1... | collective-permute-start | bytes 245768 | tf_op jit(solution)/shard_map/ppermute | solution.py:30
  17.8 9.3 %collective-permute-start.1 = (f32[32,640]{1,0:T(8,128)S(1)}, f32[32,640]{1,0:T(8,128)}, u32[]{:S(2)}, u32[]{:S(2)}) collective-permute-start(f32[32,640]{1,0:T(8,128)S(1)} %bitcast.192), channel_id=1, source_target_pairs={{0,8},{4,12},{8,0},{12,4},{1,9},{5,13},{9,1},{13,5},{2,10},{6,14},... | collective-permute-start | bytes 245768 | tf_op jit(solution)/shard_map/ppermute | solution.py:30
  20.4 6.7 %collective-permute-start.2 = (f32[32,640]{1,0:T(8,128)S(1)}, f32[32,640]{1,0:T(8,128)}, u32[]{:S(2)}, u32[]{:S(2)}) collective-permute-start(f32[32,640]{1,0:T(8,128)S(1)} %bitcast.193), channel_id=1, source_target_pairs={{0,12},{4,8},{8,4},{12,0},{1,13},{5,9},{9,5},{13,1},{2,14},{6,10},... | collective-permute-start | bytes 245768 | tf_op jit(solution)/shard_map/ppermute | solution.py:30
  29.0 3.7 %collective-permute-start.4 = (bf16[8,640]{1,0:T(8,128)(2,1)S(1)}, bf16[8,640]{1,0:T(8,128)(2,1)S(1)}, u32[]{:S(2)}, u32[]{:S(2)}) collective-permute-start(bf16[8,640]{1,0:T(8,128)(2,1)S(1)} %get-tuple-element.34), channel_id=1, source_target_pairs={{0,2},{1,3},{2,0},{3,1},{4,6},{5,7},{6,4},{7,5},{8,10},{9,11},{10,... | collective-permute-start | bytes 30728 | tf_op jit(solution)/shard_map/ppermute | solution.py:30
  30.6 3.1 %collective-permute-start.5 = (bf16[8,640]{1,0:T(8,128)(2,1)S(1)}, bf16[8,640]{1,0:T(8,128)(2,1)S(1)}, u32[]{:S(2)}, u32[]{:S(2)}) collective-permute-start(bf16[8,640]{1,0:T(8,128)(2,1)S(1)} %get-tuple-element.35), channel_id=1, source_target_pairs={{0,3},{1,2},{2,1},{3,0},{4,7},{5,6},{6,5},{7,4},{8,11},{9,10},{10,... | collective-permute-start | bytes 30728 | tf_op jit(solution)/shard_map/ppermute | solution.py:30
  30.6 3.1 %collective-permute-start.3 = (bf16[8,640]{1,0:T(8,128)(2,1)S(1)}, bf16[8,640]{1,0:T(8,128)(2,1)S(1)}, u32[]{:S(2)}, u32[]{:S(2)}) collective-permute-start(bf16[8,640]{1,0:T(8,128)(2,1)S(1)} %get-tuple-element.36), channel_id=1, source_target_pairs={{0,1},{1,0},{2,3},{3,2},{4,5},{5,4},{6,7},{7,6},{8,9},{9,8},{10,11... | collective-permute-start | bytes 30728 | tf_op jit(solution)/shard_map/ppermute | solution.py:30
  33.7 5.8 %collective-permute-start.7 = (bf16[4,8,640]{2,1,0:T(8,128)(2,1)S(1)}, bf16[4,8,640]{2,1,0:T(8,128)(2,1)S(1)}, u32[]{:S(2)}, u32[]{:S(2)}) collective-permute-start(bf16[4,8,640]{2,1,0:T(8,128)(2,1)S(1)} %pad_maximum_fusion.3), channel_id=1, source_target_pairs={{0,8},{4,12},{8,0},{12,4},{1,9},{5,13},{9,1},{13,5},{2,10},{6,14},... | collective-permute-start | bytes 122888 | tf_op jit(solution)/shard_map/ppermute | solution.py:36
  36.2 5.8 %collective-permute-start.8 = (bf16[4,8,640]{2,1,0:T(8,128)(2,1)S(1)}, bf16[4,8,640]{2,1,0:T(8,128)(2,1)S(1)}, u32[]{:S(2)}, u32[]{:S(2)}) collective-permute-start(bf16[4,8,640]{2,1,0:T(8,128)(2,1)S(1)} %pad_maximum_fusion.3), channel_id=1, source_target_pairs={{0,12},{4,8},{8,4},{12,0},{1,13},{5,9},{9,5},{13,1},{2,14},{6,10},... | collective-permute-start | bytes 122888 | tf_op jit(solution)/shard_map/ppermute | solution.py:36
  37.6 4.5 %collective-permute-start.6 = (bf16[4,8,640]{2,1,0:T(8,128)(2,1)S(1)}, bf16[4,8,640]{2,1,0:T(8,128)(2,1)S(1)}, u32[]{:S(2)}, u32[]{:S(2)}) collective-permute-start(bf16[4,8,640]{2,1,0:T(8,128)(2,1)S(1)} %pad_maximum_fusion.3), channel_id=1, source_target_pairs={{0,4},{4,0},{8,12},{12,8},{1,5},{5,1},{9,13},{13,9},{2,6},{6,2},{1... | collective-permute-start | bytes 122888 | tf_op jit(solution)/shard_map/ppermute | solution.py:36
  42.7 43.6 %copy-start.1 = (bf16[32,4096]{1,0:T(8,128)(2,1)S(1)}, bf16[32,4096]{1,0:T(8,128)(2,1)}, u32[]{:S(2)}) copy-start(bf16[32,4096]{1,0:T(8,128)(2,1)} %param.15) | copy-start | bytes 786436
  47.5 2.1 %copy-start.3 = (f32[8,4,1,16]{3,2,1,0:T(1,128)}, f32[8,4,1,16]{3,2,1,0:T(1,128)S(1)}, u32[]{:S(2)}) copy-start(f32[8,4,1,16]{3,2,1,0:T(1,128)S(1)} %fusion.25) | copy-start | bytes 6148
  54.3 5.1 %collective-permute-start.9 = (f32[136,128]{1,0:T(8,128)S(1)}, f32[136,128]{1,0:T(8,128)S(1)}, u32[]{:S(2)}, u32[]{:S(2)}) collective-permute-start(f32[136,128]{1,0:T(8,128)S(1)} %get-tuple-element.18), channel_id=1, source_target_pairs={{0,4},{4,0},{8,12},{12,8},{1,5},{5,1},{9,13},{13,9},{2,6},{6,2},{1... | collective-permute-start | bytes 208904 | tf_op jit(solution)/shard_map/ppermute | solution.py:30
  54.4 6.3 %collective-permute-start.11 = (f32[136,128]{1,0:T(8,128)S(1)}, f32[136,128]{1,0:T(8,128)S(1)}, u32[]{:S(2)}, u32[]{:S(2)}) collective-permute-start(f32[136,128]{1,0:T(8,128)S(1)} %get-tuple-element.19), channel_id=1, source_target_pairs={{0,12},{4,8},{8,4},{12,0},{1,13},{5,9},{9,5},{13,1},{2,14},{6,10},... | collective-permute-start | bytes 208904 | tf_op jit(solution)/shard_map/ppermute | solution.py:30
  56.8 6.0 %collective-permute-start.10 = (f32[136,128]{1,0:T(8,128)S(1)}, f32[136,128]{1,0:T(8,128)S(1)}, u32[]{:S(2)}, u32[]{:S(2)}) collective-permute-start(f32[136,128]{1,0:T(8,128)S(1)} %get-tuple-element.20), channel_id=1, source_target_pairs={{0,8},{4,12},{8,0},{12,4},{1,9},{5,13},{9,1},{13,5},{2,10},{6,14},... | collective-permute-start | bytes 208904 | tf_op jit(solution)/shard_map/ppermute | solution.py:30
  63.1 1.9 %collective-permute-start.12 = (bf16[2,2048]{1,0:T(2,128)(2,1)S(1)}, bf16[2,2048]{1,0:T(2,128)(2,1)S(1)}, u32[]{:S(2)}, u32[]{:S(2)}) collective-permute-start(bf16[2,2048]{1,0:T(2,128)(2,1)S(1)} %bitcast.198), channel_id=1, source_target_pairs={{0,1},{1,0},{2,3},{3,2},{4,5},{5,4},{6,7},{7,6},{8,9},{9,8},{10,11... | collective-permute-start | bytes 24584 | tf_op jit(solution)/shard_map/ppermute | solution.py:30
  63.2 3.7 %collective-permute-start.13 = (bf16[2,2048]{1,0:T(2,128)(2,1)S(1)}, bf16[2,2048]{1,0:T(2,128)(2,1)S(1)}, u32[]{:S(2)}, u32[]{:S(2)}) collective-permute-start(bf16[2,2048]{1,0:T(2,128)(2,1)S(1)} %bitcast.197), channel_id=1, source_target_pairs={{0,2},{1,3},{2,0},{3,1},{4,6},{5,7},{6,4},{7,5},{8,10},{9,11},{10,... | collective-permute-start | bytes 24584 | tf_op jit(solution)/shard_map/ppermute | solution.py:30
  64.3 3.1 %collective-permute-start.14 = (bf16[2,2048]{1,0:T(2,128)(2,1)S(1)}, bf16[2,2048]{1,0:T(2,128)(2,1)S(1)}, u32[]{:S(2)}, u32[]{:S(2)}) collective-permute-start(bf16[2,2048]{1,0:T(2,128)(2,1)S(1)} %bitcast.196), channel_id=1, source_target_pairs={{0,3},{1,2},{2,1},{3,0},{4,7},{5,6},{6,5},{7,4},{8,11},{9,10},{10,... | collective-permute-start | bytes 24584 | tf_op jit(solution)/shard_map/ppermute | solution.py:30
  67.5 5.4 %collective-permute-start.16 = (bf16[4,2,2048]{2,1,0:T(2,128)(2,1)S(1)}, bf16[4,2,2048]{2,1,0:T(2,128)(2,1)S(1)}, u32[]{:S(2)}, u32[]{:S(2)}) collective-permute-start(bf16[4,2,2048]{2,1,0:T(2,128)(2,1)S(1)} %pad_maximum_fusion.4), channel_id=1, source_target_pairs={{0,8},{4,12},{8,0},{12,4},{1,9},{5,13},{9,1},{13,5},{2,10},{6,14},... | collective-permute-start | bytes 98312 | tf_op jit(solution)/shard_map/ppermute | solution.py:36
  68.1 6.0 %collective-permute-start.17 = (bf16[4,2,2048]{2,1,0:T(2,128)(2,1)S(1)}, bf16[4,2,2048]{2,1,0:T(2,128)(2,1)S(1)}, u32[]{:S(2)}, u32[]{:S(2)}) collective-permute-start(bf16[4,2,2048]{2,1,0:T(2,128)(2,1)S(1)} %pad_maximum_fusion.4), channel_id=1, source_target_pairs={{0,12},{4,8},{8,4},{12,0},{1,13},{5,9},{9,5},{13,1},{2,14},{6,10},... | collective-permute-start | bytes 98312 | tf_op jit(solution)/shard_map/ppermute | solution.py:36
  69.8 4.3 %collective-permute-start.15 = (bf16[4,2,2048]{2,1,0:T(2,128)(2,1)S(1)}, bf16[4,2,2048]{2,1,0:T(2,128)(2,1)S(1)}, u32[]{:S(2)}, u32[]{:S(2)}) collective-permute-start(bf16[4,2,2048]{2,1,0:T(2,128)(2,1)S(1)} %pad_maximum_fusion.4), channel_id=1, source_target_pairs={{0,4},{4,0},{8,12},{12,8},{1,5},{5,1},{9,13},{13,9},{2,6},{6,2},{1... | collective-permute-start | bytes 98312 | tf_op jit(solution)/shard_map/ppermute | solution.py:36
  83.7 1.6 %collective-permute-start.18 = (f32[16,4096]{1,0:T(8,128)S(1)}, f32[16,4096]{1,0:T(8,128)S(1)}, u32[]{:S(2)}, u32[]{:S(2)}) collective-permute-start(f32[16,4096]{1,0:T(8,128)S(1)} %dynamic-slice_bitcast_fusion), channel_id=1, source_target_pairs={{0,1},{1,0},{2,3},{3,2},{4,5},{5,4},{6,7},{7,6},{8,9},{9,8},{10,11... | collective-permute-start | bytes 786440 | tf_op jit(solution)/shard_map/ppermute | solution.py:40
  85.3 8.5 %collective-permute-start.19 = (f32[16,4096]{1,0:T(8,128)S(1)}, f32[16,4096]{1,0:T(8,128)}, u32[]{:S(2)}, u32[]{:S(2)}) collective-permute-start(f32[16,4096]{1,0:T(8,128)S(1)} %bitcast_add_fusion), channel_id=1, source_target_pairs={{0,2},{1,3},{2,0},{3,1},{4,6},{5,7},{6,4},{7,5},{8,10},{9,11},{10,... | collective-permute-start | bytes 786440 | tf_op jit(solution)/shard_map/ppermute | solution.py:40
  94.8 1.4 %collective-permute-start.20 = (bf16[16,4096]{1,0:T(8,128)(2,1)S(1)}, bf16[16,4096]{1,0:T(8,128)(2,1)S(1)}, u32[]{:S(2)}, u32[]{:S(2)}) collective-permute-start(bf16[16,4096]{1,0:T(8,128)(2,1)S(1)} %add_convert_fusion), channel_id=1, source_target_pairs={{0,1},{1,0},{2,3},{3,2},{4,5},{5,4},{6,7},{7,6},{8,9},{9,8},{10,11... | collective-permute-start | bytes 393224 | tf_op jit(solution)/shard_map/ppermute | solution.py:40

commit v2 on v1

--- a/solution.py
+++ b/solution.py
@@ -1,6 +1,10 @@
+import functools
+
 import jax
 import jax.numpy as jnp
 from jax import lax
+from jax.experimental import pallas as pl
+from jax.experimental.pallas import tpu as pltpu
 from jax.sharding import PartitionSpec as P
 
 D = 16384
@@ -10,8 +14,12 @@
 GROUP = HEADS // KV_HEADS
 EPSILON = 1e-05
 NEGATIVE = -1e30
+LANES = 128
 f32 = jnp.float32
 bf16 = jnp.bfloat16
+VMEM = pl.BlockSpec(memory_space=pltpu.VMEM)
+SMEM = pl.BlockSpec(memory_space=pltpu.SMEM)
+ANY = pl.BlockSpec(memory_space=pl.ANY)
 
 
 def partners(n, offset):
@@ -23,74 +31,320 @@
     return [lax.select_n(me, *[pieces[j ^ i] for i in range(n)]) for j in range(n)]
 
 
-def exchange(chunks, axis, n):
-    me = lax.axis_index(axis)
-    own = lax.dynamic_index_in_dim(chunks, me, 0, keepdims=False)
-    return [own] + [
-        lax.ppermute(lax.dynamic_index_in_dim(chunks, me ^ k, 0, keepdims=False), axis, partners(n, k))
-        for k in range(1, n)
-    ]
+def trade(chunks, axis, n):
+    return [chunks[0]] + [lax.ppermute(chunks[k], axis, partners(n, k)) for k in range(1, n)]
 
 
 def gather(value, axis, n):
-    return [value] + [lax.ppermute(value, axis, partners(n, k)) for k in range(1, n)]
+    return trade([value] * n, axis, n)
 
 
 def swap(value, axis, n, offset):
     return lax.ppermute(value, axis, partners(n, offset))
+
+
+def params(mib):
+    return pltpu.CompilerParams(vmem_limit_bytes=mib << 20)
+
+
+def project_kernel(n, residual, gain, smooth, w_query, query_scale, w_keyval, keyval_scale, *rest):
+    outs = rest[:n]
+    x_buf, g_buf, s_buf, q_buf, k_buf, qs_buf, ks_buf, smoothed, q_sum, k_sum, packed, sems, big_sems = rest[n:]
+    rows, width = x_buf.shape
+    steps = big_sems.shape[0] // 2
+    depth = width // steps
+    small = [
+        pltpu.make_async_copy(source, target, sems.at[i])
+        for i, (source, target) in enumerate(
+            [(residual, x_buf), (gain, g_buf), (smooth, s_buf), (query_scale, qs_buf), (keyval_scale, ks_buf)]
+        )
+    ]
+    for copy in small[:3]:
+        copy.start()
+    large = []
+    for i in range(steps):
+        part = pl.ds(i * depth, depth)
+        large.append(
+            (
+                pltpu.make_async_copy(w_keyval.at[part], k_buf.at[part], big_sems.at[2 * i]),
+                pltpu.make_async_copy(w_query.at[part], q_buf.at[part], big_sems.at[2 * i + 1]),
+            )
+        )
+        for copy in large[-1]:
+            copy.start()
+    for copy in small[3:]:
+        copy.start()
+    for copy in small[:3]:
+        copy.wait()
+    squares = jnp.zeros((rows, LANES), f32)
+    for i in range(width // LANES):
+        lanes = slice(i * LANES, (i + 1) * LANES)
+        x = x_buf[:, lanes].astype(f32)
+        squares += x * x
+        smoothed[:, lanes] = (x * (g_buf[i : i + 1, :] / s_buf[i : i + 1, :])).astype(bf16)
+    squares = jnp.sum(squares, axis=1, keepdims=True)
+    for i in range(steps):
+        part = slice(i * depth, (i + 1) * depth)
+        large[i][0].wait()
+        k_part = jnp.dot(smoothed[:, part], k_buf[part, :], preferred_element_type=f32)
+        large[i][1].wait()
+        q_part = jnp.dot(smoothed[:, part], q_buf[part, :], preferred_element_type=f32)
+        if i == 0:
+            q_sum[...], k_sum[...] = q_part, k_part
+        else:
+            q_sum[...] += q_part
+            k_sum[...] += k_part
+    for copy in small[3:]:
+        copy.wait()
+    q_tiles = q_sum.shape[1] // LANES
+    per = q_tiles // n
+    for t in range(q_tiles):
+        lanes = slice(t * LANES, (t + 1) * LANES)
+        packed[t // per, :, (t % per) * LANES : (t % per + 1) * LANES] = q_sum[:, lanes] * qs_buf[t : t + 1, :]
+    lane = lax.broadcasted_iota(jnp.int32, (rows, LANES), 1)
+    half = k_sum.shape[1] // n
+    for p in range(n):
+        start = p * half
+        t, shift = start // LANES, start % LANES
+        tile = k_sum[:, t * LANES : (t + 1) * LANES] * ks_buf[t : t + 1, :]
+        if shift:
+            tile = pltpu.roll(tile, LANES - shift, 1)
+        packed[p, :, per * LANES :] = jnp.where(lane < half, tile, squares)
+    me = lax.axis_index("gx")
+    for k in range(n):
+        outs[k][...] = packed[me ^ k]
+
+
+def project(n, residual, gain, smooth, w_query, query_scale, w_keyval, keyval_scale):
+    rows, width = residual.shape
+    queries, keyvals = w_query.shape[1], w_keyval.shape[1]
+    columns = queries // n + LANES
+    steps = 8
+    return pl.pallas_call(
+        functools.partial(project_kernel, n),
+        in_specs=[ANY] * 7,
+        out_specs=[VMEM] * n,
+        out_shape=[jax.ShapeDtypeStruct((rows, columns), f32)] * n,
+        scratch_shapes=[
+            pltpu.VMEM((rows, width), bf16),
+            pltpu.VMEM((width // LANES, LANES), f32),
+            pltpu.VMEM((width // LANES, LANES), f32),
+            pltpu.VMEM((width, queries), bf16),
+            pltpu.VMEM((width, keyvals), bf16),
+            pltpu.VMEM((queries // LANES, LANES), f32),
+            pltpu.VMEM((keyvals // LANES, LANES), f32),
+            pltpu.VMEM((rows, width), bf16),
+            pltpu.VMEM((rows, queries), f32),
+            pltpu.VMEM((rows, keyvals), f32),
+            pltpu.VMEM((n, rows, columns), f32),
+            pltpu.SemaphoreType.DMA((5,)),
+            pltpu.SemaphoreType.DMA((2 * steps,)),
+        ],
+        compiler_params=params(50),
+        name="project",
+    )(
+        residual,
+        gain.reshape(-1, LANES),
+        smooth.reshape(-1, LANES),
+        w_query,
+        query_scale.reshape(-1, LANES),
+        w_keyval,
+        keyval_scale.reshape(-1, LANES),
+    )
+
+
+def norm_kernel(n_gx, n_gy, half, *refs):
+    parts, outs, full = refs[:n_gx], refs[n_gx : n_gx + n_gy], refs[-1]
+    total = parts[0][...]
+    for part in parts[1:]:
+        total = total + part[...]
+    columns = total.shape[1]
+    squares = total[:, columns - LANES + half : columns - LANES + half + 1]
+    full[...] = total * lax.rsqrt(squares / D + EPSILON)
+    requests = total.shape[0] // n_gy
+    me = lax.axis_index("gy")
+    for k in range(n_gy):
+        start = pl.multiple_of((me ^ k) * requests, requests)
+        outs[k][...] = full[pl.ds(start, requests), :].astype(bf16)
+
+
+def norm(n_gx, n_gy, half, parts):
+    rows, columns = parts[0].shape
+    return pl.pallas_call(
+        functools.partial(norm_kernel, n_gx, n_gy, half),
+        in_specs=[VMEM] * n_gx,
+        out_specs=[VMEM] * n_gy,
+        out_shape=[jax.ShapeDtypeStruct((rows // n_gy, columns), bf16)] * n_gy,
+        scratch_shapes=[pltpu.VMEM((rows, columns), f32)],
+        compiler_params=params(8),
+        name="norm",
+    )(*parts)
+
+
+def attend_kernel(n, half, *refs):
+    pieces = refs[:n]
+    lengths, keys, values, key_scale, value_scale = refs[n : n + 5]
+    outs = refs[n + 5 : 2 * n + 5]
+    placed, k_buf, v_buf, q_rows, logits, messages, fresh, sems = refs[2 * n + 5 :]
+    requests, _, local, _ = k_buf.shape
+    load_keys = pltpu.make_async_copy(keys, k_buf, sems.at[0])
+    load_values = pltpu.make_async_copy(values, v_buf, sems.at[1])
+    load_keys.start()
+    load_values.start()
+    me = lax.axis_index("gx")
+    for k in range(n):
+        placed[me ^ k] = pieces[k][...].astype(f32)
+    per = GROUP // n
+    for g in range(KV_HEADS):
+        for p in range(n):
+            for j in range(per):
+                tile = placed[p, g, :, j * LANES : (j + 1) * LANES]
+                q_rows[pl.ds(g * GROUP + p * per + j, requests, stride=HEADS), :] = tile
+    lane = lax.broadcasted_iota(jnp.int32, (requests, LANES), 1)
+    tail = placed.shape[3] - LANES
+    share = half * n
+    for c in range(2 * KV_HEADS):
+        block, start = c * LANES // share, c * LANES % share
+        low = placed[start // half, block, :, tail:]
+        high = placed[start // half + 1, block, :, tail:]
+        fresh[pl.ds(c, requests, stride=2 * KV_HEADS), :] = jnp.where(lane < half, low, pltpu.roll(high, half, 1))
+    multiplier = HEAD_DIM ** (-0.5)
+    load_keys.wait()
+    for r in range(requests):
+        for g in range(KV_HEADS):
+            at = slice(r * HEADS + g * GROUP, r * HEADS + (g + 1) * GROUP)
+            logits[at, :] = lax.dot_general(
+                q_rows[at, :].astype(bf16), k_buf[r, g], (((1,), (1,)), ((), ())), preferred_element_type=f32
+            )
+    load_values.wait()
+    position = lax.broadcasted_iota(jnp.int32, (GROUP, local), 1) + me * local
+    first = me == 0
+    count = requests * HEADS // n
+    tops, totals = [], []
+    for r in range(requests):
+        for g in range(KV_HEADS):
+            row = r * HEADS + g * GROUP
+            at = slice(row, row + GROUP)
+            scale_at = r * KV_HEADS + g
+            visible = position < lengths[r]
+            scores = logits[at, :] * key_scale[scale_at : scale_at + 1, :] * multiplier
+            scores = jnp.where(visible, scores, NEGATIVE)
+            new_key = fresh[r * 2 * KV_HEADS + g : r * 2 * KV_HEADS + g + 1, :]
+            new_value = fresh[r * 2 * KV_HEADS + KV_HEADS + g : r * 2 * KV_HEADS + KV_HEADS + g + 1, :]
+            own = jnp.sum(q_rows[at, :] * new_key, axis=1, keepdims=True) * multiplier
+            own = jnp.where(first, own, NEGATIVE)
+            top = jnp.maximum(jnp.max(scores, axis=1, keepdims=True), own)
+            weights = jnp.where(visible, jnp.exp(scores - top), 0.0)
+            own_weight = jnp.where(first, jnp.exp(own - top), 0.0)
+            totals.append(jnp.sum(weights, axis=1, keepdims=True) + own_weight)
+            tops.append(top)
+            scaled = (weights * value_scale[scale_at : scale_at + 1, :]).astype(bf16)
+            mixed = jnp.dot(scaled, v_buf[r, g], preferred_element_type=f32) + own_weight * new_value
+            messages[row // count, row % count : row % count + GROUP, :] = mixed
+    diagonal = lax.broadcasted_iota(jnp.int32, (LANES, LANES), 0) == lax.broadcasted_iota(jnp.int32, (LANES, LANES), 1)
+    step = count // GROUP
+    wide = LANES // GROUP
+    for p in range(n):
+        rows = []
+        for kind in (tops, totals):
+            for b in range(count // LANES):
+                column = jnp.concatenate(kind[p * step + b * wide : p * step + (b + 1) * wide], axis=0)
+                rows.append(jnp.sum(jnp.where(diagonal, column, 0.0), axis=0, keepdims=True))
+        spare = messages.shape[1] - count - len(rows)
+        messages[p, count:, :] = jnp.concatenate(rows + [jnp.zeros((spare, LANES), f32)], axis=0)
+    for k in range(n):
+        outs[k][...] = messages[me ^ k]
+
+
+def attend(n, half, pieces, lengths, keys, values, key_scale, value_scale):
+    requests, _, local, _ = keys.shape
+    count = requests * HEADS // n
+    height = count + -(-2 * count // LANES // 8) * 8
+    return pl.pallas_call(
+        functools.partial(attend_kernel, n, half),
+        in_specs=[VMEM] * n + [SMEM, ANY, ANY, VMEM, VMEM],
+        out_specs=[VMEM] * n,
+        out_shape=[jax.ShapeDtypeStruct((height, LANES), f32)] * n,
+        scratch_shapes=[
+            pltpu.VMEM((n,) + pieces[0].shape, f32),
+            pltpu.VMEM(keys.shape, bf16),
+            pltpu.VMEM(values.shape, bf16),
+            pltpu.VMEM((requests * HEADS, HEAD_DIM), f32),
+            pltpu.VMEM((requests * HEADS, local), f32),
+            pltpu.VMEM((n, height, LANES), f32),
+            pltpu.VMEM((requests * 2 * KV_HEADS, HEAD_DIM), f32),
+            pltpu.SemaphoreType.DMA((2,)),
+        ],
+        compiler_params=params(32),
+        name="attend",
+    )(*pieces, lengths, keys, values, key_scale.reshape(-1, local), value_scale.reshape(-1, local))
+
+
+def output_kernel(attended, w_out, out_scale, ffn, kept, given, w_buf, ffn_buf, total, sems):
+    depth_all, width = w_buf.shape
+    steps = sems.shape[0] - 1
+    depth = depth_all // steps
+    copies = []
+    for i in range(steps):
+        part = pl.ds(i * depth, depth)
+        copies.append(pltpu.make_async_copy(w_out.at[part], w_buf.at[part], sems.at[i]))
+        copies[-1].start()
+    load = pltpu.make_async_copy(ffn, ffn_buf, sems.at[steps])
+    load.start()
+    for i in range(steps):
+        part = slice(i * depth, (i + 1) * depth)
+        copies[i].wait()
+        term = jnp.dot(attended[:, part], w_buf[part, :], preferred_element_type=f32)
+        if i == 0:
+            total[...] = term
+        else:
+            total[...] += term
+    load.wait()
+    for t in range(width // LANES):
+        lanes = slice(t * LANES, (t + 1) * LANES)
+        total[:, lanes] = total[:, lanes] * out_scale[t : t + 1, :] + ffn_buf[:, lanes]
+    rows = total.shape[0] // 2
+    core = lax.axis_index("gy") & 1
+    kept[...] = total[pl.ds(pl.multiple_of(core * rows, rows), rows), :]
+    given[...] = total[pl.ds(pl.multiple_of((1 - core) * rows, rows), rows), :]
+
+
+def output(attended, w_out, out_scale, ffn):
+    rows, depth = attended.shape
+    width = w_out.shape[1]
+    steps = 8
+    return pl.pallas_call(
+        output_kernel,
+        in_specs=[VMEM, ANY, VMEM, ANY],
+        out_specs=[VMEM] * 2,
+        out_shape=[jax.ShapeDtypeStruct((rows // 2, width), f32)] * 2,
+        scratch_shapes=[
+            pltpu.VMEM(w_out.shape, bf16),
+            pltpu.VMEM((rows, width), f32),
+            pltpu.VMEM((rows, width), f32),
+            pltpu.SemaphoreType.DMA((steps + 1,)),
+        ],
+        compiler_params=params(50),
+        name="output",
+    )(attended, w_out, out_scale.reshape(-1, LANES), ffn)
 
 
 def body(n_gx, n_gy, residual, ffn_partial, norm_gain, smooth_scale, w_query, query_scale, w_keyval, keyval_scale,
          key_cache, value_cache, key_scale, value_scale, lengths, w_out, out_scale):
     gx, gy = lax.axis_index("gx"), lax.axis_index("gy")
     rows, width = residual.shape
-    requests = rows // n_gy
-    widened = residual.astype(f32)
-    squares = jnp.sum(widened * widened, axis=1)
-    smoothed = (widened * (norm_gain / smooth_scale)).astype(bf16)
-    query_part = jnp.dot(smoothed, w_query, preferred_element_type=f32) * query_scale
-    keyval_part = jnp.dot(smoothed, w_keyval, preferred_element_type=f32) * keyval_scale
-    qc, kc = query_part.shape[1] // n_gx, keyval_part.shape[1] // n_gx
-    pad = -(qc + kc + 1) % 128
-    packed = jnp.concatenate([
-        query_part.reshape(rows, n_gx, qc), keyval_part.reshape(rows, n_gx, kc),
-        jnp.broadcast_to(squares[:, None, None], (rows, n_gx, 1)), jnp.zeros((rows, n_gx, pad), f32)], axis=2)
-    pieces = exchange(packed.transpose(1, 0, 2), "gx", n_gx)
-    summed = sum(pieces[1:], pieces[0])
-    row_scale = lax.rsqrt(summed[:, qc + kc] / D + EPSILON)[:, None]
-    rounded = (row_scale * summed).astype(bf16)[:, : qc + kc]
-    rounded = jnp.pad(rounded, ((0, 0), (0, pad + 1)))
-    mine = jnp.stack(ordered(exchange(rounded.reshape(n_gy, requests, -1), "gy", n_gy), gy))
-    everything = jnp.stack(ordered(gather(mine, "gx", n_gx), gx))
-    query_vectors = everything[..., :qc].transpose(2, 1, 0, 3).reshape(requests, KV_HEADS, GROUP, HEAD_DIM)
-    keyvals = everything[..., qc : qc + kc].transpose(2, 1, 0, 3).reshape(requests, 2 * KV_HEADS, HEAD_DIM)
-    fresh_keys, fresh_values = keyvals[:, :KV_HEADS], keyvals[:, KV_HEADS:]
-
-    local = key_cache.shape[2]
-    multiplier = HEAD_DIM ** (-0.5)
-    logits = jnp.einsum("rgqd,rgsd->rgqs", query_vectors, key_cache, preferred_element_type=f32)
-    logits = logits * key_scale[:, :, None, :] * multiplier
-    position = gx * local + jnp.arange(local, dtype=jnp.int32)
-    visible = (position[None, :] < lengths[:, None])[:, None, None, :]
-    logits = jnp.where(visible, logits, NEGATIVE)
-    own = jnp.einsum("rgqd,rgd->rgq", query_vectors, fresh_keys, preferred_element_type=f32) * multiplier
-    own = jnp.where(gx == 0, own, NEGATIVE)
-    top = jnp.maximum(jnp.max(logits, axis=-1), own)
-    weights = jnp.where(visible, jnp.exp(logits - top[..., None]), 0.0)
-    own_weight = jnp.where(gx == 0, jnp.exp(own - top), 0.0)
-    total = jnp.sum(weights, axis=-1) + own_weight
-    scaled = (weights * value_scale[:, :, None, :]).astype(bf16)
-    mixed = jnp.einsum("rgqs,rgsd->rgqd", scaled, value_cache, preferred_element_type=f32)
-    mixed = mixed + own_weight[..., None] * fresh_values.astype(f32)[:, :, None, :]
-
-    share = requests // n_gx
-    mixed = mixed.reshape(n_gx, share * HEADS, HEAD_DIM)
-    stats = jnp.concatenate([top.reshape(n_gx, share * HEADS // HEAD_DIM, HEAD_DIM),
-                             total.reshape(n_gx, share * HEADS // HEAD_DIM, HEAD_DIM)], axis=1)
-    extra = stats.shape[1]
-    message = jnp.concatenate([mixed, stats, jnp.zeros((n_gx, -extra % 8, HEAD_DIM), f32)], axis=1)
-    parts = exchange(message, "gx", n_gx)
+    half = w_keyval.shape[1] // n_gx
+    parts = project(n_gx, residual, norm_gain, smooth_scale, w_query, query_scale, w_keyval, keyval_scale)
+    parts = trade(parts, "gx", n_gx)
+    blocks = trade(norm(n_gx, n_gy, half, parts), "gy", n_gy)
+    mine = jnp.stack(ordered(blocks, gy))
+    pieces = gather(mine, "gx", n_gx)
+    parts = attend(n_gx, half, pieces, lengths, key_cache, value_cache, key_scale, value_scale)
+    parts = trade(parts, "gx", n_gx)
+
+    share = rows // n_gy // n_gx
     count = share * HEADS
+    extra = 2 * count // LANES
     tops = [part[count : count + extra // 2].reshape(count) for part in parts]
     totals = [part[count + extra // 2 : count + extra].reshape(count) for part in parts]
     largest = tops[0]
@@ -101,19 +355,16 @@
     mixed = sum(f[:, None] * part[:count] for f, part in zip(factors, parts))
     attended = (mixed / total[:, None]).astype(bf16)
     attended = attended.reshape(share, n_gy, HEADS // n_gy * HEAD_DIM).transpose(1, 0, 2)
-    blocks = jnp.stack(ordered(exchange(attended, "gy", n_gy), gy))
+    sends = [lax.dynamic_index_in_dim(attended, gy ^ k, 0, keepdims=False) for k in range(n_gy)]
+    blocks = jnp.stack(ordered(trade(sends, "gy", n_gy), gy))
     blocks = jnp.stack(ordered(gather(blocks, "gx", n_gx), gx), axis=1)
-    projected = jnp.dot(blocks.reshape(rows, -1), w_out, preferred_element_type=f32) * out_scale
-
-    term = (projected + ffn_partial[0]).reshape(2, rows // 2, width)
+    kept, given = output(blocks.reshape(rows, -1), w_out, out_scale, ffn_partial[0])
     core = gy & 1
-    kept = lax.dynamic_index_in_dim(term, core, 0, keepdims=False)
-    given = lax.dynamic_index_in_dim(term, 1 - core, 0, keepdims=False)
     chip = kept + swap(given, "gy", n_gy, 1)
     whole = chip + swap(chip, "gy", n_gy, 2)
-    half = lax.dynamic_slice_in_dim(widened, core * (rows // 2), rows // 2, 0)
-    half = (half + whole).astype(bf16)
-    return jnp.concatenate(ordered([half, swap(half, "gy", n_gy, 1)], core))
+    mine = lax.dynamic_slice_in_dim(residual, core * (rows // 2), rows // 2, 0)
+    mine = (mine.astype(f32) + whole).astype(bf16)
+    return jnp.concatenate(ordered([mine, swap(mine, "gy", n_gy, 1)], core))
 
 
 def joined(value, axis, join):

time: 97.6 us -> 82.3 us (0.84)
  matrix products: 23.1 us -> 0 us
  Pallas kernels: 0 us -> 17 us
  other arithmetic: 12.8 us -> 1.54 us
  starting transfers between devices: 21.9 us -> 24.1 us
  waiting for transfers between devices: 32.3 us -> 33.3 us
    dot_general x6 -> x0, matrix products: 23.1 us -> none  [the longest x1 8.94 us: body(): jnp.dot(blocks.reshape(rows, -1), w_out, preferred_element_type=f32)]
    pallas_call x0 -> x4, Pallas kernels: none -> 17 us  [the longest x1 6.83 us: project(): pl.pallas_call(functools.partial(project_kernel, n), in_specs=[ANY] * 7,...]
    unnamed x14 -> x31, local copies, waits for them, and re-layouts: 0.07 us -> 5.42 us
    reshape x6 -> x0, local copies, waits for them, and re-layouts: 2.95 us -> none  [the longest x1 0.96 us: body(): everything[..., :qc].transpose(2, 1, 0, 3)]
    ppermute x18, starting transfers between devices: 20.8 us -> 23.3 us  [trade(): lax.ppermute(chunks[k], axis, partners(n, k))]
    reduce_sum x2 -> x0, other arithmetic: 2.48 us -> none  [the longest x1 1.26 us: body(): squares = jnp.sum(widened * widened, axis=1)]
    transpose x3 -> x0, local copies, waits for them, and re-layouts: 2.16 us -> none  [the longest x1 1.39 us: body(): everything[..., qc:qc + kc].transpose(2, 1, 0, 3)]
    concatenate x3 -> x1, other arithmetic: 2.53 us -> 0.72 us  [body(): return jnp.concatenate(ordered([mine, swap(mine, 'gy', n_gy, 1)], core))]
  transfers between devices with their start and end apart: 21 -> 21, of which waited for: 14 -> 14; matrix products, arithmetic and copies ran while one was open for 2% -> 0% of each run, Pallas kernels for 0% -> 0%
where the time goes in v2:
time: 82.3 us; the launch traced here: 81.9 us
  waiting for transfers between devices  33.3 us (40%)
  starting transfers between devices  24.1 us (29%)
  Pallas kernels  17 us (21%)
  local copies, waits for them, and re-layouts  5.66 us (7%)
  other arithmetic  1.54 us (2%)
    ppermute x18, starting transfers between devices, trade(): lax.ppermute(chunks[k], axis, partners(n, k))  23.3 us
    ppermute x18, waiting for transfers between devices, trade(): lax.ppermute(chunks[k], axis, partners(n, k))  22.7 us
    ppermute x3, waiting for transfers between devices, swap(): return lax.ppermute(value, axis, partners(n, offset))  10.6 us
    pallas_call x1, Pallas kernels, project(): pl.pallas_call(functools.partial(project_kernel, n), in_specs=[ANY] * 7,...  6.83 us
    pallas_call x1, Pallas kernels, output(): pl.pallas_call(output_kernel, in_specs=[VMEM, ANY, VMEM, ANY], out_specs=...  6.52 us
    unnamed x31, local copies, waits for them, and re-layouts  5.42 us
    pallas_call x1, Pallas kernels, attend(): pl.pallas_call(functools.partial(attend_kernel, n, half), in_specs=[VMEM]...  3.54 us
  transfers between devices with their start and end apart: 21, of which 14 were waited for; matrix products, arithmetic and copies ran while one was open for 0% of the time, Pallas kernels for 0%

profile of v2, /device:TPU:0, one launch (start us, length us, event | category | flops | bytes accessed | tf_op | source)
XLA Modules:
  0.0 81.9 jit_solution(7515288064361248339)
XLA Ops:
  0.0 1.6 %copy-done = bf16[4096,256]{1,0:T(8,128)(2,1)S(1)} copy-done((bf16[4096,256]{1,0:T(8,128)(2,1)S(1)}, bf16[4096,256]{1,0:T(8,128)(2,1)}, u32[]{:S(2)}) %copy-start) | copy-done | bytes 2097176
  1.6 0.9 %copy-done.3 = bf16[32,4096]{1,0:T(8,128)(2,1)S(1)} copy-done((bf16[32,4096]{1,0:T(8,128)(2,1)S(1)}, bf16[32,4096]{1,0:T(8,128)(2,1)}, u32[]{:S(2)}) %copy-start.3) | copy-done | bytes 262168
  5.4 6.8 %project.1 = (f32[32,640]{1,0:T(8,128)S(1)}, f32[32,640]{1,0:T(8,128)S(1)}, f32[32,640]{1,0:T(8,128)S(1)}, f32[32,640]{1,0:T(8,128)S(1)}) custom-call(bf16[32,4096]{1,0:T(8,128)(2,1)S(1)} %copy-done.3, f32[32,128]{1,0:T(8,128)S(1)} %bitcast.102, f32[32,128]{1,0:T(8,128)S(1)} %bitcast.103, bf16[4096,2048]{1,0:T(8,128)(2,1)} %w_query.1, ...), custom_call_target="tpu_custom_call" | custom-call | tf_op jit(solution)/shard_map/project/pallas_call | solution.py:123
  12.3 3.1 %collective-permute-start = (f32[32,640]{1,0:T(8,128)S(1)}, f32[32,640]{1,0:T(8,128)S(1)}, u32[]{:S(2)}, u32[]{:S(2)}) collective-permute-start(f32[32,640]{1,0:T(8,128)S(1)} %get-tuple-element.20), channel_id=1, source_target_pairs={{0,4},{4,0},{8,12},{12,8},{1,5},{5,1},{9,13},{13,9},{2,6},{6,2},{1... | collective-permute-start | bytes 245768 | tf_op jit(solution)/shard_map/ppermute | solution.py:35
  15.3 2.6 %collective-permute-start.1 = (f32[32,640]{1,0:T(8,128)S(1)}, f32[32,640]{1,0:T(8,128)S(1)}, u32[]{:S(2)}, u32[]{:S(2)}) collective-permute-start(f32[32,640]{1,0:T(8,128)S(1)} %get-tuple-element.21), channel_id=1, source_target_pairs={{0,8},{4,12},{8,0},{12,4},{1,9},{5,13},{9,1},{13,5},{2,10},{6,14},... | collective-permute-start | bytes 245768 | tf_op jit(solution)/shard_map/ppermute | solution.py:35
  17.9 6.6 %collective-permute-done.1.refs_2_ = f32[32,640]{1,0:T(8,128)S(1)} collective-permute-done((f32[32,640]{1,0:T(8,128)S(1)}, f32[32,640]{1,0:T(8,128)S(1)}, u32[]{:S(2)}, u32[]{:S(2)}) %collective-permute-start.1) | collective-permute-done | bytes 81952 | tf_op jit(solution)/shard_map/ppermute | solution.py:35
  24.6 1.6 %collective-permute-start.4 = (bf16[8,640]{1,0:T(8,128)(2,1)S(1)}, bf16[8,640]{1,0:T(8,128)(2,1)S(1)}, u32[]{:S(2)}, u32[]{:S(2)}) collective-permute-start(bf16[8,640]{1,0:T(8,128)(2,1)S(1)} %get-tuple-element.25), channel_id=1, source_target_pairs={{0,2},{1,3},{2,0},{3,1},{4,6},{5,7},{6,4},{7,5},{8,10},{9,11},{10,... | collective-permute-start | bytes 30728 | tf_op jit(solution)/shard_map/ppermute | solution.py:35
  26.8 1.5 %collective-permute-done.4 = bf16[8,640]{1,0:T(8,128)(2,1)S(1)} collective-permute-done((bf16[8,640]{1,0:T(8,128)(2,1)S(1)}, bf16[8,640]{1,0:T(8,128)(2,1)S(1)}, u32[]{:S(2)}, u32[]{:S(2)}) %collective-permute-start.4) | collective-permute-done | bytes 10272 | tf_op jit(solution)/shard_map/ppermute | solution.py:35
  28.4 0.9 %collective-permute-done.5 = bf16[8,640]{1,0:T(8,128)(2,1)S(1)} collective-permute-done((bf16[8,640]{1,0:T(8,128)(2,1)S(1)}, bf16[8,640]{1,0:T(8,128)(2,1)S(1)}, u32[]{:S(2)}, u32[]{:S(2)}) %collective-permute-start.5) | collective-permute-done | bytes 10272 | tf_op jit(solution)/shard_map/ppermute | solution.py:35
  29.3 1.5 %collective-permute-start.6 = (bf16[4,8,640]{2,1,0:T(8,128)(2,1)S(1)}, bf16[4,8,640]{2,1,0:T(8,128)(2,1)S(1)}, u32[]{:S(2)}, u32[]{:S(2)}) collective-permute-start(bf16[4,8,640]{2,1,0:T(8,128)(2,1)S(1)} %pad_maximum_fusion.2.refs_0_), channel_id=1, source_target_pairs={{0,4},{4,0},{8,12},{12,8},{1,5},{5,1},{9,13},{13,9},{2,6},{6,2},{1... | collective-permute-start | bytes 122888 | tf_op jit(solution)/shard_map/ppermute | solution.py:35
  30.8 1.6 %collective-permute-start.7 = (bf16[4,8,640]{2,1,0:T(8,128)(2,1)S(1)}, bf16[4,8,640]{2,1,0:T(8,128)(2,1)S(1)}, u32[]{:S(2)}, u32[]{:S(2)}) collective-permute-start(bf16[4,8,640]{2,1,0:T(8,128)(2,1)S(1)} %pad_maximum_fusion.2.refs_0_), channel_id=1, source_target_pairs={{0,8},{4,12},{8,0},{12,4},{1,9},{5,13},{9,1},{13,5},{2,10},{6,14},... | collective-permute-start | bytes 122888 | tf_op jit(solution)/shard_map/ppermute | solution.py:35
  32.4 1.3 %collective-permute-start.8 = (bf16[4,8,640]{2,1,0:T(8,128)(2,1)S(1)}, bf16[4,8,640]{2,1,0:T(8,128)(2,1)S(1)}, u32[]{:S(2)}, u32[]{:S(2)}) collective-permute-start(bf16[4,8,640]{2,1,0:T(8,128)(2,1)S(1)} %pad_maximum_fusion.2.refs_0_), channel_id=1, source_target_pairs={{0,12},{4,8},{8,4},{12,0},{1,13},{5,9},{9,5},{13,1},{2,14},{6,10},... | collective-permute-start | bytes 122888 | tf_op jit(solution)/shard_map/ppermute | solution.py:35
  33.8 2.8 %collective-permute-done.7.refs_2_ = bf16[4,8,640]{2,1,0:T(8,128)(2,1)S(1)} collective-permute-done((bf16[4,8,640]{2,1,0:T(8,128)(2,1)S(1)}, bf16[4,8,640]{2,1,0:T(8,128)(2,1)S(1)}, u32[]{:S(2)}, u32[]{:S(2)}) %collective-permute-start.7) | collective-permute-done | bytes 40992 | tf_op jit(solution)/shard_map/ppermute | solution.py:35
  36.6 1.6 %collective-permute-done.8.refs_3_ = bf16[4,8,640]{2,1,0:T(8,128)(2,1)S(1)} collective-permute-done((bf16[4,8,640]{2,1,0:T(8,128)(2,1)S(1)}, bf16[4,8,640]{2,1,0:T(8,128)(2,1)S(1)}, u32[]{:S(2)}, u32[]{:S(2)}) %collective-permute-start.8) | collective-permute-done | bytes 40992 | tf_op jit(solution)/shard_map/ppermute | solution.py:35
  38.3 3.5 %attend.1 = (f32[136,128]{1,0:T(8,128)S(1)}, f32[136,128]{1,0:T(8,128)S(1)}, f32[136,128]{1,0:T(8,128)S(1)}, f32[136,128]{1,0:T(8,128)S(1)}) custom-call(bf16[4,8,640]{2,1,0:T(8,128)(2,1)S(1)} %pad_maximum_fusion.2.refs_0_, bf16[4,8,640]{2,1,0:T(8,128)(2,1)S(1)} %collective-permute-done.6.refs_1_, bf16[4,8,640]{2,1,0:T(8,128)(2,1)S(1)} %collective-permute-done.7.refs_2_, ...), custom_call_target="tpu_custom_call" | custom-call | tf_op jit(solution)/shard_map/attend/pallas_call | solution.py:263
  41.8 1.4 %collective-permute-start.11 = (f32[136,128]{1,0:T(8,128)S(1)}, f32[136,128]{1,0:T(8,128)S(1)}, u32[]{:S(2)}, u32[]{:S(2)}) collective-permute-start(f32[136,128]{1,0:T(8,128)S(1)} %get-tuple-element.30), channel_id=1, source_target_pairs={{0,12},{4,8},{8,4},{12,0},{1,13},{5,9},{9,5},{13,1},{2,14},{6,10},... | collective-permute-start | bytes 208904 | tf_op jit(solution)/shard_map/ppermute | solution.py:35
  43.2 3.0 %collective-permute-start.9 = (f32[136,128]{1,0:T(8,128)S(1)}, f32[136,128]{1,0:T(8,128)S(1)}, u32[]{:S(2)}, u32[]{:S(2)}) collective-permute-start(f32[136,128]{1,0:T(8,128)S(1)} %get-tuple-element.28), channel_id=1, source_target_pairs={{0,4},{4,0},{8,12},{12,8},{1,5},{5,1},{9,13},{13,9},{2,6},{6,2},{1... | collective-permute-start | bytes 208904 | tf_op jit(solution)/shard_map/ppermute | solution.py:35
  46.3 1.8 %collective-permute-done.11 = f32[136,128]{1,0:T(8,128)S(1)} collective-permute-done((f32[136,128]{1,0:T(8,128)S(1)}, f32[136,128]{1,0:T(8,128)S(1)}, u32[]{:S(2)}, u32[]{:S(2)}) %collective-permute-start.11) | collective-permute-done | bytes 69664 | tf_op jit(solution)/shard_map/ppermute | solution.py:35
  48.0 1.4 %collective-permute-done.10 = f32[136,128]{1,0:T(8,128)S(1)} collective-permute-done((f32[136,128]{1,0:T(8,128)S(1)}, f32[136,128]{1,0:T(8,128)S(1)}, u32[]{:S(2)}, u32[]{:S(2)}) %collective-permute-start.10) | collective-permute-done | bytes 69664 | tf_op jit(solution)/shard_map/ppermute | solution.py:35
  49.9 1.2 %collective-permute-start.13 = (bf16[2,2048]{1,0:T(2,128)(2,1)S(1)}, bf16[2,2048]{1,0:T(2,128)(2,1)S(1)}, u32[]{:S(2)}, u32[]{:S(2)}) collective-permute-start(bf16[2,2048]{1,0:T(2,128)(2,1)S(1)} %bitcast.110), channel_id=1, source_target_pairs={{0,2},{1,3},{2,0},{3,1},{4,6},{5,7},{6,4},{7,5},{8,10},{9,11},{10,... | collective-permute-start | bytes 24584 | tf_op jit(solution)/shard_map/ppermute | solution.py:35
  51.1 0.8 collective-permute-start.14
  51.9 1.7 %collective-permute-done.13 = bf16[2,2048]{1,0:T(2,128)(2,1)S(1)} collective-permute-done((bf16[2,2048]{1,0:T(2,128)(2,1)S(1)}, bf16[2,2048]{1,0:T(2,128)(2,1)S(1)}, u32[]{:S(2)}, u32[]{:S(2)}) %collective-permute-start.13) | collective-permute-done | bytes 8224 | tf_op jit(solution)/shard_map/ppermute | solution.py:35
  54.3 0.7 collective-permute-start.15
  55.1 1.7 %collective-permute-start.16 = (bf16[4,2,2048]{2,1,0:T(2,128)(2,1)S(1)}, bf16[4,2,2048]{2,1,0:T(2,128)(2,1)S(1)}, u32[]{:S(2)}, u32[]{:S(2)}) collective-permute-start(bf16[4,2,2048]{2,1,0:T(2,128)(2,1)S(1)} %pad_maximum_fusion.3), channel_id=1, source_target_pairs={{0,8},{4,12},{8,0},{12,4},{1,9},{5,13},{9,1},{13,5},{2,10},{6,14},... | collective-permute-start | bytes 98312 | tf_op jit(solution)/shard_map/ppermute | solution.py:35
  56.8 2.0 %collective-permute-start.17 = (bf16[4,2,2048]{2,1,0:T(2,128)(2,1)S(1)}, bf16[4,2,2048]{2,1,0:T(2,128)(2,1)S(1)}, u32[]{:S(2)}, u32[]{:S(2)}) collective-permute-start(bf16[4,2,2048]{2,1,0:T(2,128)(2,1)S(1)} %pad_maximum_fusion.3), channel_id=1, source_target_pairs={{0,12},{4,8},{8,4},{12,0},{1,13},{5,9},{9,5},{13,1},{2,14},{6,10},... | collective-permute-start | bytes 98312 | tf_op jit(solution)/shard_map/ppermute | solution.py:35
  58.8 1.2 %collective-permute-done.16 = bf16[4,2,2048]{2,1,0:T(2,128)(2,1)S(1)} collective-permute-done((bf16[4,2,2048]{2,1,0:T(2,128)(2,1)S(1)}, bf16[4,2,2048]{2,1,0:T(2,128)(2,1)S(1)}, u32[]{:S(2)}, u32[]{:S(2)}) %collective-permute-start.16) | collective-permute-done | bytes 32800 | tf_op jit(solution)/shard_map/ppermute | solution.py:35
  60.0 2.5 %collective-permute-done.17 = bf16[4,2,2048]{2,1,0:T(2,128)(2,1)S(1)} collective-permute-done((bf16[4,2,2048]{2,1,0:T(2,128)(2,1)S(1)}, bf16[4,2,2048]{2,1,0:T(2,128)(2,1)S(1)}, u32[]{:S(2)}, u32[]{:S(2)}) %collective-permute-start.17) | collective-permute-done | bytes 32800 | tf_op jit(solution)/shard_map/ppermute | solution.py:35
  63.1 6.5 %output.1 = (f32[16,4096]{1,0:T(8,128)S(1)}, f32[16,4096]{1,0:T(8,128)S(1)}) custom-call(bf16[32,2048]{1,0:T(8,128)(2,1)S(1)} %reshape.192.attended, bf16[2048,4096]{1,0:T(8,128)(2,1)} %w_out.1, f32[32,128]{1,0:T(8,128)S(1)} %bitcast.106, f32[32,4096]{1,0:T(8,128)S(1)} %bitcast.101), custom_call_target="tpu_custom_call" | custom-call | tf_op jit(solution)/shard_map/output/pallas_call | solution.py:316
  69.7 1.5 %collective-permute-done.18 = f32[16,4096]{1,0:T(8,128)S(1)} collective-permute-done((f32[16,4096]{1,0:T(8,128)S(1)}, f32[16,4096]{1,0:T(8,128)S(1)}, u32[]{:S(2)}, u32[]{:S(2)}) %collective-permute-start.18) | collective-permute-done | bytes 262176 | tf_op jit(solution)/shard_map/ppermute | solution.py:43
  71.9 7.7 %collective-permute-done.19 = f32[16,4096]{1,0:T(8,128)S(1)} collective-permute-done((f32[16,4096]{1,0:T(8,128)S(1)}, f32[16,4096]{1,0:T(8,128)S(1)}, u32[]{:S(2)}, u32[]{:S(2)}) %collective-permute-start.19) | collective-permute-done | bytes 262176 | tf_op jit(solution)/shard_map/ppermute | solution.py:43
  79.8 1.3 %collective-permute-done.20 = bf16[16,4096]{1,0:T(8,128)(2,1)S(1)} collective-permute-done((bf16[16,4096]{1,0:T(8,128)(2,1)S(1)}, bf16[16,4096]{1,0:T(8,128)(2,1)S(1)}, u32[]{:S(2)}, u32[]{:S(2)}) %collective-permute-start.20) | collective-permute-done | bytes 131104 | tf_op jit(solution)/shard_map/ppermute | solution.py:43
  81.1 0.7 pad_maximum_fusion
  (62 shorter events, 6.2 us)
Async XLA Ops:
  0.0 38.2 %copy-start.13 = (s32[8]{0:T(128)S(1)}, s32[8]{0:T(128)}, u32[]{:S(2)}) copy-start(s32[8]{0:T(128)} %refs_4_.1) | copy-start | bytes 100
  0.0 1.6 %copy-start = (bf16[4096,256]{1,0:T(8,128)(2,1)S(1)}, bf16[4096,256]{1,0:T(8,128)(2,1)}, u32[]{:S(2)}) copy-start(bf16[4096,256]{1,0:T(8,128)(2,1)} %w_keyval.1) | copy-start | bytes 6291460
  1.6 0.9 %copy-start.3 = (bf16[32,4096]{1,0:T(8,128)(2,1)S(1)}, bf16[32,4096]{1,0:T(8,128)(2,1)}, u32[]{:S(2)}) copy-start(bf16[32,4096]{1,0:T(8,128)(2,1)} %residual.1) | copy-start | bytes 786436
  2.6 0.7 copy-start.6
  5.4 32.9 %copy-start.1 = (bf16[8,4,128,128]{3,2,1,0:T(8,128)(2,1)S(1)}, bf16[8,4,128,128]{3,2,1,0:T(8,128)(2,1)}, u32[]{:S(2)}) copy-start(bf16[8,4,128,128]{3,2,1,0:T(8,128)(2,1)} %refs_5_.1) | copy-start | bytes 3145732
  5.4 32.9 %copy-start.2 = (bf16[8,4,128,128]{3,2,1,0:T(8,128)(2,1)S(1)}, bf16[8,4,128,128]{3,2,1,0:T(8,128)(2,1)}, u32[]{:S(2)}) copy-start(bf16[8,4,128,128]{3,2,1,0:T(8,128)(2,1)} %refs_6_.1) | copy-start | bytes 3145732
  5.4 32.9 %copy-start.8 = (f32[8,4,128]{2,1,0:T(4,128)S(1)}, f32[8,4,128]{2,1,0:T(4,128)}, u32[]{:S(2)}) copy-start(f32[8,4,128]{2,1,0:T(4,128)} %param.25) | copy-start | bytes 49156
  5.4 32.9 %copy-start.9 = (f32[8,4,128]{2,1,0:T(4,128)S(1)}, f32[8,4,128]{2,1,0:T(4,128)}, u32[]{:S(2)}) copy-start(f32[8,4,128]{2,1,0:T(4,128)} %param.26) | copy-start | bytes 49156
  5.4 57.7 %copy-start.5 = (f32[1,32,4096]{2,1,0:T(8,128)S(1)}, f32[1,32,4096]{2,1,0:T(8,128)}, u32[]{:S(2)}) copy-start(f32[1,32,4096]{2,1,0:T(8,128)} %param.16) | copy-start | bytes 1572868
  5.4 57.7 %copy-start.10 = (f32[4096]{0:T(1024)S(1)}, f32[4096]{0:T(1024)}, u32[]{:S(2)}) copy-start(f32[4096]{0:T(1024)} %param.29) | copy-start | bytes 49156
  5.4 74.3 %copy-start.4 = (bf16[32,4096]{1,0:T(8,128)(2,1)S(1)}, bf16[32,4096]{1,0:T(8,128)(2,1)}, u32[]{:S(2)}) copy-start(bf16[32,4096]{1,0:T(8,128)(2,1)} %residual.1) | copy-start | bytes 786436
  12.3 5.7 %collective-permute-start = (f32[32,640]{1,0:T(8,128)S(1)}, f32[32,640]{1,0:T(8,128)S(1)}, u32[]{:S(2)}, u32[]{:S(2)}) collective-permute-start(f32[32,640]{1,0:T(8,128)S(1)} %get-tuple-element.20), channel_id=1, source_target_pairs={{0,4},{4,0},{8,12},{12,8},{1,5},{5,1},{9,13},{13,9},{2,6},{6,2},{1... | collective-permute-start | bytes 245768 | tf_op jit(solution)/shard_map/ppermute | solution.py:35
  15.3 9.2 %collective-permute-start.1 = (f32[32,640]{1,0:T(8,128)S(1)}, f32[32,640]{1,0:T(8,128)S(1)}, u32[]{:S(2)}, u32[]{:S(2)}) collective-permute-start(f32[32,640]{1,0:T(8,128)S(1)} %get-tuple-element.21), channel_id=1, source_target_pairs={{0,8},{4,12},{8,0},{12,4},{1,9},{5,13},{9,1},{13,5},{2,10},{6,14},... | collective-permute-start | bytes 245768 | tf_op jit(solution)/shard_map/ppermute | solution.py:35
  17.9 6.6 %collective-permute-start.2 = (f32[32,640]{1,0:T(8,128)S(1)}, f32[32,640]{1,0:T(8,128)S(1)}, u32[]{:S(2)}, u32[]{:S(2)}) collective-permute-start(f32[32,640]{1,0:T(8,128)S(1)} %get-tuple-element.22), channel_id=1, source_target_pairs={{0,12},{4,8},{8,4},{12,0},{1,13},{5,9},{9,5},{13,1},{2,14},{6,10},... | collective-permute-start | bytes 245768 | tf_op jit(solution)/shard_map/ppermute | solution.py:35
  24.6 3.7 %collective-permute-start.4 = (bf16[8,640]{1,0:T(8,128)(2,1)S(1)}, bf16[8,640]{1,0:T(8,128)(2,1)S(1)}, u32[]{:S(2)}, u32[]{:S(2)}) collective-permute-start(bf16[8,640]{1,0:T(8,128)(2,1)S(1)} %get-tuple-element.25), channel_id=1, source_target_pairs={{0,2},{1,3},{2,0},{3,1},{4,6},{5,7},{6,4},{7,5},{8,10},{9,11},{10,... | collective-permute-start | bytes 30728 | tf_op jit(solution)/shard_map/ppermute | solution.py:35
  26.2 3.1 %collective-permute-start.5 = (bf16[8,640]{1,0:T(8,128)(2,1)S(1)}, bf16[8,640]{1,0:T(8,128)(2,1)S(1)}, u32[]{:S(2)}, u32[]{:S(2)}) collective-permute-start(bf16[8,640]{1,0:T(8,128)(2,1)S(1)} %get-tuple-element.26), channel_id=1, source_target_pairs={{0,3},{1,2},{2,1},{3,0},{4,7},{5,6},{6,5},{7,4},{8,11},{9,10},{10,... | collective-permute-start | bytes 30728 | tf_op jit(solution)/shard_map/ppermute | solution.py:35
  26.2 3.1 %collective-permute-start.3 = (bf16[8,640]{1,0:T(8,128)(2,1)S(1)}, bf16[8,640]{1,0:T(8,128)(2,1)S(1)}, u32[]{:S(2)}, u32[]{:S(2)}) collective-permute-start(bf16[8,640]{1,0:T(8,128)(2,1)S(1)} %get-tuple-element.24), channel_id=1, source_target_pairs={{0,1},{1,0},{2,3},{3,2},{4,5},{5,4},{6,7},{7,6},{8,9},{9,8},{10,11... | collective-permute-start | bytes 30728 | tf_op jit(solution)/shard_map/ppermute | solution.py:35
  29.3 4.5 %collective-permute-start.6 = (bf16[4,8,640]{2,1,0:T(8,128)(2,1)S(1)}, bf16[4,8,640]{2,1,0:T(8,128)(2,1)S(1)}, u32[]{:S(2)}, u32[]{:S(2)}) collective-permute-start(bf16[4,8,640]{2,1,0:T(8,128)(2,1)S(1)} %pad_maximum_fusion.2.refs_0_), channel_id=1, source_target_pairs={{0,4},{4,0},{8,12},{12,8},{1,5},{5,1},{9,13},{13,9},{2,6},{6,2},{1... | collective-permute-start | bytes 122888 | tf_op jit(solution)/shard_map/ppermute | solution.py:35
  30.8 5.8 %collective-permute-start.7 = (bf16[4,8,640]{2,1,0:T(8,128)(2,1)S(1)}, bf16[4,8,640]{2,1,0:T(8,128)(2,1)S(1)}, u32[]{:S(2)}, u32[]{:S(2)}) collective-permute-start(bf16[4,8,640]{2,1,0:T(8,128)(2,1)S(1)} %pad_maximum_fusion.2.refs_0_), channel_id=1, source_target_pairs={{0,8},{4,12},{8,0},{12,4},{1,9},{5,13},{9,1},{13,5},{2,10},{6,14},... | collective-permute-start | bytes 122888 | tf_op jit(solution)/shard_map/ppermute | solution.py:35
  32.4 5.8 %collective-permute-start.8 = (bf16[4,8,640]{2,1,0:T(8,128)(2,1)S(1)}, bf16[4,8,640]{2,1,0:T(8,128)(2,1)S(1)}, u32[]{:S(2)}, u32[]{:S(2)}) collective-permute-start(bf16[4,8,640]{2,1,0:T(8,128)(2,1)S(1)} %pad_maximum_fusion.2.refs_0_), channel_id=1, source_target_pairs={{0,12},{4,8},{8,4},{12,0},{1,13},{5,9},{9,5},{13,1},{2,14},{6,10},... | collective-permute-start | bytes 122888 | tf_op jit(solution)/shard_map/ppermute | solution.py:35
  41.8 6.2 %collective-permute-start.11 = (f32[136,128]{1,0:T(8,128)S(1)}, f32[136,128]{1,0:T(8,128)S(1)}, u32[]{:S(2)}, u32[]{:S(2)}) collective-permute-start(f32[136,128]{1,0:T(8,128)S(1)} %get-tuple-element.30), channel_id=1, source_target_pairs={{0,12},{4,8},{8,4},{12,0},{1,13},{5,9},{9,5},{13,1},{2,14},{6,10},... | collective-permute-start | bytes 208904 | tf_op jit(solution)/shard_map/ppermute | solution.py:35
  43.2 6.2 %collective-permute-start.10 = (f32[136,128]{1,0:T(8,128)S(1)}, f32[136,128]{1,0:T(8,128)S(1)}, u32[]{:S(2)}, u32[]{:S(2)}) collective-permute-start(f32[136,128]{1,0:T(8,128)S(1)} %get-tuple-element.29), channel_id=1, source_target_pairs={{0,8},{4,12},{8,0},{12,4},{1,9},{5,13},{9,1},{13,5},{2,10},{6,14},... | collective-permute-start | bytes 208904 | tf_op jit(solution)/shard_map/ppermute | solution.py:35
  43.2 6.2 %collective-permute-start.9 = (f32[136,128]{1,0:T(8,128)S(1)}, f32[136,128]{1,0:T(8,128)S(1)}, u32[]{:S(2)}, u32[]{:S(2)}) collective-permute-start(f32[136,128]{1,0:T(8,128)S(1)} %get-tuple-element.28), channel_id=1, source_target_pairs={{0,4},{4,0},{8,12},{12,8},{1,5},{5,1},{9,13},{13,9},{2,6},{6,2},{1... | collective-permute-start | bytes 208904 | tf_op jit(solution)/shard_map/ppermute | solution.py:35
  49.8 2.1 %collective-permute-start.12 = (bf16[2,2048]{1,0:T(2,128)(2,1)S(1)}, bf16[2,2048]{1,0:T(2,128)(2,1)S(1)}, u32[]{:S(2)}, u32[]{:S(2)}) collective-permute-start(bf16[2,2048]{1,0:T(2,128)(2,1)S(1)} %bitcast.109), channel_id=1, source_target_pairs={{0,1},{1,0},{2,3},{3,2},{4,5},{5,4},{6,7},{7,6},{8,9},{9,8},{10,11... | collective-permute-start | bytes 24584 | tf_op jit(solution)/shard_map/ppermute | solution.py:35
  49.9 3.7 %collective-permute-start.13 = (bf16[2,2048]{1,0:T(2,128)(2,1)S(1)}, bf16[2,2048]{1,0:T(2,128)(2,1)S(1)}, u32[]{:S(2)}, u32[]{:S(2)}) collective-permute-start(bf16[2,2048]{1,0:T(2,128)(2,1)S(1)} %bitcast.110), channel_id=1, source_target_pairs={{0,2},{1,3},{2,0},{3,1},{4,6},{5,7},{6,4},{7,5},{8,10},{9,11},{10,... | collective-permute-start | bytes 24584 | tf_op jit(solution)/shard_map/ppermute | solution.py:35
  51.1 3.1 %collective-permute-start.14 = (bf16[2,2048]{1,0:T(2,128)(2,1)S(1)}, bf16[2,2048]{1,0:T(2,128)(2,1)S(1)}, u32[]{:S(2)}, u32[]{:S(2)}) collective-permute-start(bf16[2,2048]{1,0:T(2,128)(2,1)S(1)} %bitcast.111), channel_id=1, source_target_pairs={{0,3},{1,2},{2,1},{3,0},{4,7},{5,6},{6,5},{7,4},{8,11},{9,10},{10,... | collective-permute-start | bytes 24584 | tf_op jit(solution)/shard_map/ppermute | solution.py:35
  54.3 4.5 %collective-permute-start.15 = (bf16[4,2,2048]{2,1,0:T(2,128)(2,1)S(1)}, bf16[4,2,2048]{2,1,0:T(2,128)(2,1)S(1)}, u32[]{:S(2)}, u32[]{:S(2)}) collective-permute-start(bf16[4,2,2048]{2,1,0:T(2,128)(2,1)S(1)} %pad_maximum_fusion.3), channel_id=1, source_target_pairs={{0,4},{4,0},{8,12},{12,8},{1,5},{5,1},{9,13},{13,9},{2,6},{6,2},{1... | collective-permute-start | bytes 98312 | tf_op jit(solution)/shard_map/ppermute | solution.py:35
  55.1 4.9 %collective-permute-start.16 = (bf16[4,2,2048]{2,1,0:T(2,128)(2,1)S(1)}, bf16[4,2,2048]{2,1,0:T(2,128)(2,1)S(1)}, u32[]{:S(2)}, u32[]{:S(2)}) collective-permute-start(bf16[4,2,2048]{2,1,0:T(2,128)(2,1)S(1)} %pad_maximum_fusion.3), channel_id=1, source_target_pairs={{0,8},{4,12},{8,0},{12,4},{1,9},{5,13},{9,1},{13,5},{2,10},{6,14},... | collective-permute-start | bytes 98312 | tf_op jit(solution)/shard_map/ppermute | solution.py:35
  56.8 5.7 %collective-permute-start.17 = (bf16[4,2,2048]{2,1,0:T(2,128)(2,1)S(1)}, bf16[4,2,2048]{2,1,0:T(2,128)(2,1)S(1)}, u32[]{:S(2)}, u32[]{:S(2)}) collective-permute-start(bf16[4,2,2048]{2,1,0:T(2,128)(2,1)S(1)} %pad_maximum_fusion.3), channel_id=1, source_target_pairs={{0,12},{4,8},{8,4},{12,0},{1,13},{5,9},{9,5},{13,1},{2,14},{6,10},... | collective-permute-start | bytes 98312 | tf_op jit(solution)/shard_map/ppermute | solution.py:35
  69.6 1.6 %collective-permute-start.18 = (f32[16,4096]{1,0:T(8,128)S(1)}, f32[16,4096]{1,0:T(8,128)S(1)}, u32[]{:S(2)}, u32[]{:S(2)}) collective-permute-start(f32[16,4096]{1,0:T(8,128)S(1)} %get-tuple-element.32), channel_id=1, source_target_pairs={{0,1},{1,0},{2,3},{3,2},{4,5},{5,4},{6,7},{7,6},{8,9},{9,8},{10,11... | collective-permute-start | bytes 786440 | tf_op jit(solution)/shard_map/ppermute | solution.py:43
  71.2 8.4 %collective-permute-start.19 = (f32[16,4096]{1,0:T(8,128)S(1)}, f32[16,4096]{1,0:T(8,128)S(1)}, u32[]{:S(2)}, u32[]{:S(2)}) collective-permute-start(f32[16,4096]{1,0:T(8,128)S(1)} %add.66), channel_id=1, source_target_pairs={{0,2},{1,3},{2,0},{3,1},{4,6},{5,7},{6,4},{7,5},{8,10},{9,11},{10,... | collective-permute-start | bytes 786440 | tf_op jit(solution)/shard_map/ppermute | solution.py:43
  79.7 1.4 %collective-permute-start.20 = (bf16[16,4096]{1,0:T(8,128)(2,1)S(1)}, bf16[16,4096]{1,0:T(8,128)(2,1)S(1)}, u32[]{:S(2)}, u32[]{:S(2)}) collective-permute-start(bf16[16,4096]{1,0:T(8,128)(2,1)S(1)} %add_convert_fusion), channel_id=1, source_target_pairs={{0,1},{1,0},{2,3},{3,2},{4,5},{5,4},{6,7},{7,6},{8,9},{9,8},{10,11... | collective-permute-start | bytes 393224 | tf_op jit(solution)/shard_map/ppermute | solution.py:43
  (3 other events, 2.1 us)

commit v3 on v2

--- a/solution.py
+++ b/solution.py
@@ -20,6 +20,7 @@
 VMEM = pl.BlockSpec(memory_space=pltpu.VMEM)
 SMEM = pl.BlockSpec(memory_space=pltpu.SMEM)
 ANY = pl.BlockSpec(memory_space=pl.ANY)
+HBM = pl.BlockSpec(memory_space=pltpu.HBM)
 
 
 def partners(n, offset):
@@ -35,8 +36,11 @@
     return [chunks[0]] + [lax.ppermute(chunks[k], axis, partners(n, k)) for k in range(1, n)]
 
 
-def gather(value, axis, n):
-    return trade([value] * n, axis, n)
+def spread(value, n):
+    return [
+        lax.ppermute(value, ("gx", "gy"), [(a * n + b, (b ^ k) * n + a) for a in range(n) for b in range(n)])
+        for k in range(n)
+    ]
 
 
 def swap(value, axis, n, offset):
@@ -49,7 +53,7 @@
 
 def project_kernel(n, residual, gain, smooth, w_query, query_scale, w_keyval, keyval_scale, *rest):
     outs = rest[:n]
-    x_buf, g_buf, s_buf, q_buf, k_buf, qs_buf, ks_buf, smoothed, q_sum, k_sum, packed, sems, big_sems = rest[n:]
+    x_buf, g_buf, s_buf, q_buf, k_buf, qs_buf, ks_buf, smoothed, q_sum, k_sum, squares_sum, sems, big_sems = rest[n:]
     rows, width = x_buf.shape
     steps = big_sems.shape[0] // 2
     depth = width // steps
@@ -96,35 +100,31 @@
             k_sum[...] += k_part
     for copy in small[3:]:
         copy.wait()
-    q_tiles = q_sum.shape[1] // LANES
-    per = q_tiles // n
-    for t in range(q_tiles):
-        lanes = slice(t * LANES, (t + 1) * LANES)
-        packed[t // per, :, (t % per) * LANES : (t % per + 1) * LANES] = q_sum[:, lanes] * qs_buf[t : t + 1, :]
-    lane = lax.broadcasted_iota(jnp.int32, (rows, LANES), 1)
-    half = k_sum.shape[1] // n
-    for p in range(n):
-        start = p * half
-        t, shift = start // LANES, start % LANES
-        tile = k_sum[:, t * LANES : (t + 1) * LANES] * ks_buf[t : t + 1, :]
-        if shift:
-            tile = pltpu.roll(tile, LANES - shift, 1)
-        packed[p, :, per * LANES :] = jnp.where(lane < half, tile, squares)
     me = lax.axis_index("gx")
+    requests = rows // n
+    q_tiles, k_tiles = q_sum.shape[1] // LANES, k_sum.shape[1] // LANES
+    squares_sum[...] = jnp.broadcast_to(squares, (rows, LANES))
     for k in range(n):
-        outs[k][...] = packed[me ^ k]
+        at = pl.ds(pl.multiple_of((me ^ k) * requests, requests), requests)
+        for t in range(q_tiles):
+            lanes = slice(t * LANES, (t + 1) * LANES)
+            outs[k][:, lanes] = q_sum[at, lanes] * qs_buf[t : t + 1, :]
+        for t in range(k_tiles):
+            lanes = slice(t * LANES, (t + 1) * LANES)
+            outs[k][:, (q_tiles + t) * LANES : (q_tiles + t + 1) * LANES] = k_sum[at, lanes] * ks_buf[t : t + 1, :]
+        outs[k][:, (q_tiles + k_tiles) * LANES :] = squares_sum[at, :]
 
 
 def project(n, residual, gain, smooth, w_query, query_scale, w_keyval, keyval_scale):
     rows, width = residual.shape
     queries, keyvals = w_query.shape[1], w_keyval.shape[1]
-    columns = queries // n + LANES
+    columns = queries + keyvals + LANES
     steps = 8
     return pl.pallas_call(
         functools.partial(project_kernel, n),
-        in_specs=[ANY] * 7,
+        in_specs=[HBM] * 7,
         out_specs=[VMEM] * n,
-        out_shape=[jax.ShapeDtypeStruct((rows, columns), f32)] * n,
+        out_shape=[jax.ShapeDtypeStruct((rows // n, columns), f32)] * n,
         scratch_shapes=[
             pltpu.VMEM((rows, width), bf16),
             pltpu.VMEM((width // LANES, LANES), f32),
@@ -136,7 +136,7 @@
             pltpu.VMEM((rows, width), bf16),
             pltpu.VMEM((rows, queries), f32),
             pltpu.VMEM((rows, keyvals), f32),
-            pltpu.VMEM((n, rows, columns), f32),
+            pltpu.VMEM((rows, LANES), f32),
             pltpu.SemaphoreType.DMA((5,)),
             pltpu.SemaphoreType.DMA((2 * steps,)),
         ],
@@ -153,35 +153,28 @@
     )
 
 
-def norm_kernel(n_gx, n_gy, half, *refs):
-    parts, outs, full = refs[:n_gx], refs[n_gx : n_gx + n_gy], refs[-1]
+def norm_kernel(*refs):
+    parts, out = refs[:-1], refs[-1]
     total = parts[0][...]
     for part in parts[1:]:
         total = total + part[...]
-    columns = total.shape[1]
-    squares = total[:, columns - LANES + half : columns - LANES + half + 1]
-    full[...] = total * lax.rsqrt(squares / D + EPSILON)
-    requests = total.shape[0] // n_gy
-    me = lax.axis_index("gy")
-    for k in range(n_gy):
-        start = pl.multiple_of((me ^ k) * requests, requests)
-        outs[k][...] = full[pl.ds(start, requests), :].astype(bf16)
-
-
-def norm(n_gx, n_gy, half, parts):
+    columns = out.shape[1]
+    out[...] = (total[:, :columns] * lax.rsqrt(total[:, columns : columns + 1] / D + EPSILON)).astype(bf16)
+
+
+def norm(parts):
     rows, columns = parts[0].shape
     return pl.pallas_call(
-        functools.partial(norm_kernel, n_gx, n_gy, half),
-        in_specs=[VMEM] * n_gx,
-        out_specs=[VMEM] * n_gy,
-        out_shape=[jax.ShapeDtypeStruct((rows // n_gy, columns), bf16)] * n_gy,
-        scratch_shapes=[pltpu.VMEM((rows, columns), f32)],
+        norm_kernel,
+        in_specs=[VMEM] * len(parts),
+        out_specs=VMEM,
+        out_shape=jax.ShapeDtypeStruct((rows, columns - LANES), bf16),
         compiler_params=params(8),
         name="norm",
     )(*parts)
 
 
-def attend_kernel(n, half, *refs):
+def attend_kernel(n, *refs):
     pieces = refs[:n]
     lengths, keys, values, key_scale, value_scale = refs[n : n + 5]
     outs = refs[n + 5 : 2 * n + 5]
@@ -194,20 +187,15 @@
     me = lax.axis_index("gx")
     for k in range(n):
         placed[me ^ k] = pieces[k][...].astype(f32)
-    per = GROUP // n
-    for g in range(KV_HEADS):
-        for p in range(n):
-            for j in range(per):
-                tile = placed[p, g, :, j * LANES : (j + 1) * LANES]
-                q_rows[pl.ds(g * GROUP + p * per + j, requests, stride=HEADS), :] = tile
-    lane = lax.broadcasted_iota(jnp.int32, (requests, LANES), 1)
-    tail = placed.shape[3] - LANES
-    share = half * n
+    queries = HEADS * HEAD_DIM // n
+    per = queries // LANES
+    for h in range(HEADS):
+        tile = placed[h // per, :, (h % per) * LANES : (h % per + 1) * LANES]
+        q_rows[pl.ds(h, requests, stride=HEADS), :] = tile
+    share = (placed.shape[2] - queries) // LANES
     for c in range(2 * KV_HEADS):
-        block, start = c * LANES // share, c * LANES % share
-        low = placed[start // half, block, :, tail:]
-        high = placed[start // half + 1, block, :, tail:]
-        fresh[pl.ds(c, requests, stride=2 * KV_HEADS), :] = jnp.where(lane < half, low, pltpu.roll(high, half, 1))
+        start = queries + c % share * LANES
+        fresh[pl.ds(c, requests, stride=2 * KV_HEADS), :] = placed[c // share, :, start : start + LANES]
     multiplier = HEAD_DIM ** (-0.5)
     load_keys.wait()
     for r in range(requests):
@@ -219,8 +207,8 @@
     load_values.wait()
     position = lax.broadcasted_iota(jnp.int32, (GROUP, local), 1) + me * local
     first = me == 0
-    count = requests * HEADS // n
-    tops, totals = [], []
+    count = requests * GROUP
+    tops, totals = [[] for _ in range(n)], [[] for _ in range(n)]
     for r in range(requests):
         for g in range(KV_HEADS):
             row = r * HEADS + g * GROUP
@@ -236,19 +224,18 @@
             top = jnp.maximum(jnp.max(scores, axis=1, keepdims=True), own)
             weights = jnp.where(visible, jnp.exp(scores - top), 0.0)
             own_weight = jnp.where(first, jnp.exp(own - top), 0.0)
-            totals.append(jnp.sum(weights, axis=1, keepdims=True) + own_weight)
-            tops.append(top)
+            totals[g].append(jnp.sum(weights, axis=1, keepdims=True) + own_weight)
+            tops[g].append(top)
             scaled = (weights * value_scale[scale_at : scale_at + 1, :]).astype(bf16)
             mixed = jnp.dot(scaled, v_buf[r, g], preferred_element_type=f32) + own_weight * new_value
-            messages[row // count, row % count : row % count + GROUP, :] = mixed
+            messages[g, r * GROUP : (r + 1) * GROUP, :] = mixed
     diagonal = lax.broadcasted_iota(jnp.int32, (LANES, LANES), 0) == lax.broadcasted_iota(jnp.int32, (LANES, LANES), 1)
-    step = count // GROUP
     wide = LANES // GROUP
     for p in range(n):
         rows = []
         for kind in (tops, totals):
             for b in range(count // LANES):
-                column = jnp.concatenate(kind[p * step + b * wide : p * step + (b + 1) * wide], axis=0)
+                column = jnp.concatenate(kind[p][b * wide : (b + 1) * wide], axis=0)
                 rows.append(jnp.sum(jnp.where(diagonal, column, 0.0), axis=0, keepdims=True))
         spare = messages.shape[1] - count - len(rows)
         messages[p, count:, :] = jnp.concatenate(rows + [jnp.zeros((spare, LANES), f32)], axis=0)
@@ -256,12 +243,12 @@
         outs[k][...] = messages[me ^ k]
 
 
-def attend(n, half, pieces, lengths, keys, values, key_scale, value_scale):
+def attend(n, pieces, lengths, keys, values, key_scale, value_scale):
     requests, _, local, _ = keys.shape
-    count = requests * HEADS // n
+    count = requests * GROUP
     height = count + -(-2 * count // LANES // 8) * 8
     return pl.pallas_call(
-        functools.partial(attend_kernel, n, half),
+        functools.partial(attend_kernel, n),
         in_specs=[VMEM] * n + [SMEM, ANY, ANY, VMEM, VMEM],
         out_specs=[VMEM] * n,
         out_shape=[jax.ShapeDtypeStruct((height, LANES), f32)] * n,
@@ -280,7 +267,50 @@
     )(*pieces, lengths, keys, values, key_scale.reshape(-1, local), value_scale.reshape(-1, local))
 
 
-def output_kernel(attended, w_out, out_scale, ffn, kept, given, w_buf, ffn_buf, total, sems):
+def merge_kernel(*refs):
+    parts, out, mixed = refs[:-2], refs[-2], refs[-1]
+    count = mixed.shape[0]
+    requests = out.shape[0]
+    diagonal = lax.broadcasted_iota(jnp.int32, (LANES, LANES), 0) == lax.broadcasted_iota(jnp.int32, (LANES, LANES), 1)
+    blocks = count // LANES
+    for b in range(blocks):
+        at = slice(b * LANES, (b + 1) * LANES)
+        tops = [part[count + b : count + b + 1, :] for part in parts]
+        totals = [part[count + blocks + b : count + blocks + b + 1, :] for part in parts]
+        largest = tops[0]
+        for top in tops[1:]:
+            largest = jnp.maximum(largest, top)
+        factors = [jnp.exp(top - largest) for top in tops]
+        total = factors[0] * totals[0]
+        for factor, other in zip(factors[1:], totals[1:]):
+            total = total + factor * other
+        sums = None
+        for factor, part in zip(factors, parts):
+            column = jnp.sum(jnp.where(diagonal, factor, 0.0), axis=1, keepdims=True)
+            term = column * part[at, :]
+            sums = term if sums is None else sums + term
+        column = jnp.sum(jnp.where(diagonal, total, 0.0), axis=1, keepdims=True)
+        mixed[at, :] = sums / column
+    for h in range(count // requests):
+        out[:, h * HEAD_DIM : (h + 1) * HEAD_DIM] = mixed[pl.ds(h, requests, stride=count // requests), :].astype(bf16)
+
+
+def merge(parts, requests):
+    count = requests * GROUP
+    return pl.pallas_call(
+        merge_kernel,
+        in_specs=[VMEM] * len(parts),
+        out_specs=VMEM,
+        out_shape=jax.ShapeDtypeStruct((requests, GROUP * HEAD_DIM), bf16),
+        scratch_shapes=[pltpu.VMEM((count, HEAD_DIM), f32)],
+        compiler_params=params(8),
+        name="merge",
+    )(*parts)
+
+
+def output_kernel(n, *refs):
+    pieces = refs[:n]
+    w_out, out_scale, ffn, kept, given, w_buf, ffn_buf, total, placed, sems = refs[n:]
     depth_all, width = w_buf.shape
     steps = sems.shape[0] - 1
     depth = depth_all // steps
@@ -291,10 +321,14 @@
         copies[-1].start()
     load = pltpu.make_async_copy(ffn, ffn_buf, sems.at[steps])
     load.start()
+    me = lax.axis_index("gx")
+    for k in range(n):
+        placed[me ^ k] = pieces[k][...].astype(f32)
     for i in range(steps):
         part = slice(i * depth, (i + 1) * depth)
         copies[i].wait()
-        term = jnp.dot(attended[:, part], w_buf[part, :], preferred_element_type=f32)
+        attended = placed[:, :, part].reshape(total.shape[0], depth).astype(bf16)
+        term = jnp.dot(attended, w_buf[part, :], preferred_element_type=f32)
         if i == 0:
             total[...] = term
         else:
@@ -309,56 +343,38 @@
     given[...] = total[pl.ds(pl.multiple_of((1 - core) * rows, rows), rows), :]
 
 
-def output(attended, w_out, out_scale, ffn):
-    rows, depth = attended.shape
+def output(pieces, w_out, out_scale, ffn):
+    n = len(pieces)
+    rows = ffn.shape[0]
     width = w_out.shape[1]
     steps = 8
     return pl.pallas_call(
-        output_kernel,
-        in_specs=[VMEM, ANY, VMEM, ANY],
+        functools.partial(output_kernel, n),
+        in_specs=[VMEM] * n + [HBM, VMEM, HBM],
         out_specs=[VMEM] * 2,
         out_shape=[jax.ShapeDtypeStruct((rows // 2, width), f32)] * 2,
         scratch_shapes=[
             pltpu.VMEM(w_out.shape, bf16),
             pltpu.VMEM((rows, width), f32),
             pltpu.VMEM((rows, width), f32),
+            pltpu.VMEM((n,) + pieces[0].shape, f32),
             pltpu.SemaphoreType.DMA((steps + 1,)),
         ],
         compiler_params=params(50),
         name="output",
-    )(attended, w_out, out_scale.reshape(-1, LANES), ffn)
+    )(*pieces, w_out, out_scale.reshape(-1, LANES), ffn)
 
 
 def body(n_gx, n_gy, residual, ffn_partial, norm_gain, smooth_scale, w_query, query_scale, w_keyval, keyval_scale,
          key_cache, value_cache, key_scale, value_scale, lengths, w_out, out_scale):
-    gx, gy = lax.axis_index("gx"), lax.axis_index("gy")
-    rows, width = residual.shape
-    half = w_keyval.shape[1] // n_gx
+    gy = lax.axis_index("gy")
+    rows = residual.shape[0]
+    requests = rows // n_gy
     parts = project(n_gx, residual, norm_gain, smooth_scale, w_query, query_scale, w_keyval, keyval_scale)
-    parts = trade(parts, "gx", n_gx)
-    blocks = trade(norm(n_gx, n_gy, half, parts), "gy", n_gy)
-    mine = jnp.stack(ordered(blocks, gy))
-    pieces = gather(mine, "gx", n_gx)
-    parts = attend(n_gx, half, pieces, lengths, key_cache, value_cache, key_scale, value_scale)
-    parts = trade(parts, "gx", n_gx)
-
-    share = rows // n_gy // n_gx
-    count = share * HEADS
-    extra = 2 * count // LANES
-    tops = [part[count : count + extra // 2].reshape(count) for part in parts]
-    totals = [part[count + extra // 2 : count + extra].reshape(count) for part in parts]
-    largest = tops[0]
-    for other in tops[1:]:
-        largest = jnp.maximum(largest, other)
-    factors = [jnp.exp(t - largest) for t in tops]
-    total = sum(f * t for f, t in zip(factors, totals))
-    mixed = sum(f[:, None] * part[:count] for f, part in zip(factors, parts))
-    attended = (mixed / total[:, None]).astype(bf16)
-    attended = attended.reshape(share, n_gy, HEADS // n_gy * HEAD_DIM).transpose(1, 0, 2)
-    sends = [lax.dynamic_index_in_dim(attended, gy ^ k, 0, keepdims=False) for k in range(n_gy)]
-    blocks = jnp.stack(ordered(trade(sends, "gy", n_gy), gy))
-    blocks = jnp.stack(ordered(gather(blocks, "gx", n_gx), gx), axis=1)
-    kept, given = output(blocks.reshape(rows, -1), w_out, out_scale, ffn_partial[0])
+    pieces = spread(norm(trade(parts, "gx", n_gx)), n_gx)
+    parts = attend(n_gx, pieces, lengths, key_cache, value_cache, key_scale, value_scale)
+    pieces = spread(merge(trade(parts, "gx", n_gx), requests), n_gx)
+    kept, given = output(pieces, w_out, out_scale, ffn_partial[0])
     core = gy & 1
     chip = kept + swap(given, "gy", n_gy, 1)
     whole = chip + swap(chip, "gy", n_gy, 2)

time: 82.3 us -> 79.1 us (0.961)
  waiting for transfers between devices: 33.3 us -> 26.4 us
  starting transfers between devices: 24.1 us -> 28.9 us
    ppermute x0 -> x8, starting transfers between devices: none -> 13.2 us  [spread(): lax.ppermute(value, ('gx', 'gy'), [(a * n + b, (b ^ k) * n + a) for a in...]
    ppermute x18 -> x6, waiting for transfers between devices: 22.7 us -> 11.7 us  [trade(): lax.ppermute(chunks[k], axis, partners(n, k))]
    ppermute x18 -> x6, starting transfers between devices: 23.3 us -> 12.3 us  [trade(): lax.ppermute(chunks[k], axis, partners(n, k))]
    ppermute x0 -> x8, waiting for transfers between devices: none -> 5.42 us  [spread(): lax.ppermute(value, ('gx', 'gy'), [(a * n + b, (b ^ k) * n + a) for a in...]
    ppermute x3, starting transfers between devices: 0.83 us -> 3.42 us  [swap(): return lax.ppermute(value, axis, partners(n, offset))]
    ppermute x3, waiting for transfers between devices: 10.6 us -> 9.32 us  [swap(): return lax.ppermute(value, axis, partners(n, offset))]
    pallas_call x4 -> x5, Pallas kernels: 17 us -> 17.1 us  [the longest x1 6.77 us: project(): pl.pallas_call(functools.partial(project_kernel, n), in_specs=[HBM] * 7,...]
    unnamed x31 -> x28, local copies, waits for them, and re-layouts: 5.42 us -> 5.39 us
  transfers between devices with their start and end apart: 21 -> 17, of which waited for: 14 -> 11; matrix products, arithmetic and copies ran while one was open for 0% -> 0% of each run, Pallas kernels for 0% -> 0%
where the time goes in v3:
time: 79.1 us; the launch traced here: 78.7 us
  starting transfers between devices  28.9 us (37%)
  waiting for transfers between devices  26.4 us (33%)
  Pallas kernels  17.1 us (22%)
  local copies, waits for them, and re-layouts  5.39 us (7%)
  other arithmetic  0.81 us (1%)
    ppermute x8, starting transfers between devices, spread(): lax.ppermute(value, ('gx', 'gy'), [(a * n + b, (b ^ k) * n + a) for a in...  13.2 us
    ppermute x6, starting transfers between devices, trade(): lax.ppermute(chunks[k], axis, partners(n, k))  12.3 us
    ppermute x6, waiting for transfers between devices, trade(): lax.ppermute(chunks[k], axis, partners(n, k))  11.7 us
    ppermute x3, waiting for transfers between devices, swap(): return lax.ppermute(value, axis, partners(n, offset))  9.32 us
    pallas_call x1, Pallas kernels, project(): pl.pallas_call(functools.partial(project_kernel, n), in_specs=[HBM] * 7,...  6.77 us
    pallas_call x1, Pallas kernels, output(): pl.pallas_call(functools.partial(output_kernel, n), in_specs=[VMEM] * n +...  6.51 us
    ppermute x8, waiting for transfers between devices, spread(): lax.ppermute(value, ('gx', 'gy'), [(a * n + b, (b ^ k) * n + a) for a in...  5.42 us
    unnamed x28, local copies, waits for them, and re-layouts  5.39 us
  transfers between devices with their start and end apart: 17, of which 11 were waited for; matrix products, arithmetic and copies ran while one was open for 0% of the time, Pallas kernels for 0%

profile of v3, /device:TPU:0, one launch (start us, length us, event | category | flops | bytes accessed | tf_op | source)
XLA Modules:
  0.0 78.7 jit_solution(16589751165404055876)
XLA Ops:
  0.0 1.6 %copy-done = bf16[4096,256]{1,0:T(8,128)(2,1)S(1)} copy-done((bf16[4096,256]{1,0:T(8,128)(2,1)S(1)}, bf16[4096,256]{1,0:T(8,128)(2,1)}, u32[]{:S(2)}) %copy-start) | copy-done | bytes 2097176
  1.6 0.9 %copy-done.3 = bf16[32,4096]{1,0:T(8,128)(2,1)S(1)} copy-done((bf16[32,4096]{1,0:T(8,128)(2,1)S(1)}, bf16[32,4096]{1,0:T(8,128)(2,1)}, u32[]{:S(2)}) %copy-start.3) | copy-done | bytes 262168
  2.6 0.7 copy-done.6
  3.3 0.7 copy-done.7
  4.0 0.7 copy-done.11
  4.7 0.7 copy-done.12
  5.4 6.8 %project.1 = (f32[8,2432]{1,0:T(8,128)S(1)}, f32[8,2432]{1,0:T(8,128)S(1)}, f32[8,2432]{1,0:T(8,128)S(1)}, f32[8,2432]{1,0:T(8,128)S(1)}) custom-call(bf16[32,4096]{1,0:T(8,128)(2,1)S(1)} %copy-done.3, f32[32,128]{1,0:T(8,128)S(1)} %bitcast.9, f32[32,128]{1,0:T(8,128)S(1)} %bitcast.10, bf16[4096,2048]{1,0:T(8,128)(2,1)} %w_query.1, f32[16,128]{1,0:T(8,128)S(1)} %bitcast.14, ...), custom_call_target="tpu_custom_call" | custom-call | tf_op jit(solution)/shard_map/project/pallas_call | solution.py:123
  12.2 3.1 %collective-permute-start = (f32[8,2432]{1,0:T(8,128)S(1)}, f32[8,2432]{1,0:T(8,128)S(1)}, u32[]{:S(2)}, u32[]{:S(2)}) collective-permute-start(f32[8,2432]{1,0:T(8,128)S(1)} %get-tuple-element.16), channel_id=1, source_target_pairs={{0,4},{4,0},{8,12},{12,8},{1,5},{5,1},{9,13},{13,9},{2,6},{6,2},{1... | collective-permute-start | bytes 233480 | tf_op jit(solution)/shard_map/ppermute | solution.py:36
  15.3 2.6 %collective-permute-start.1 = (f32[8,2432]{1,0:T(8,128)S(1)}, f32[8,2432]{1,0:T(8,128)S(1)}, u32[]{:S(2)}, u32[]{:S(2)}) collective-permute-start(f32[8,2432]{1,0:T(8,128)S(1)} %get-tuple-element.17), channel_id=1, source_target_pairs={{0,8},{4,12},{8,0},{12,4},{1,9},{5,13},{9,1},{13,5},{2,10},{6,14},... | collective-permute-start | bytes 233480 | tf_op jit(solution)/shard_map/ppermute | solution.py:36
  17.9 5.5 %collective-permute-done.1.refs_2_ = f32[8,2432]{1,0:T(8,128)S(1)} collective-permute-done((f32[8,2432]{1,0:T(8,128)S(1)}, f32[8,2432]{1,0:T(8,128)S(1)}, u32[]{:S(2)}, u32[]{:S(2)}) %collective-permute-start.1) | collective-permute-done | bytes 77856 | tf_op jit(solution)/shard_map/ppermute | solution.py:36
  23.3 0.8 %collective-permute-done.2.refs_3_ = f32[8,2432]{1,0:T(8,128)S(1)} collective-permute-done((f32[8,2432]{1,0:T(8,128)S(1)}, f32[8,2432]{1,0:T(8,128)S(1)}, u32[]{:S(2)}, u32[]{:S(2)}) %collective-permute-start.2) | collective-permute-done | bytes 77856 | tf_op jit(solution)/shard_map/ppermute | solution.py:36
  24.3 0.7 collective-permute-start.3
  24.9 2.7 %collective-permute-start.4 = (bf16[8,2304]{1,0:T(8,128)(2,1)S(1)}, bf16[8,2304]{1,0:T(8,128)(2,1)S(1)}, u32[]{:S(2)}, u32[]{:S(2)}) collective-permute-start(bf16[8,2304]{1,0:T(8,128)(2,1)S(1)} %norm.1), channel_id=1, source_target_pairs={{0,4},{1,0},{2,12},{3,8},{4,5},{5,1},{6,13},{7,9},{8,6},{9,2},{10,... | collective-permute-start | bytes 110600 | tf_op jit(solution)/shard_map/ppermute | solution.py:41
  27.6 2.5 %collective-permute-start.5 = (bf16[8,2304]{1,0:T(8,128)(2,1)S(1)}, bf16[8,2304]{1,0:T(8,128)(2,1)S(1)}, u32[]{:S(2)}, u32[]{:S(2)}) collective-permute-start(bf16[8,2304]{1,0:T(8,128)(2,1)S(1)} %norm.1), channel_id=1, source_target_pairs={{0,8},{1,12},{2,0},{3,4},{4,9},{5,13},{6,1},{7,5},{8,10},{9,14},{1... | collective-permute-start | bytes 110600 | tf_op jit(solution)/shard_map/ppermute | solution.py:41
  30.2 1.3 %collective-permute-start.6 = (bf16[8,2304]{1,0:T(8,128)(2,1)S(1)}, bf16[8,2304]{1,0:T(8,128)(2,1)S(1)}, u32[]{:S(2)}, u32[]{:S(2)}) collective-permute-start(bf16[8,2304]{1,0:T(8,128)(2,1)S(1)} %norm.1), channel_id=1, source_target_pairs={{0,12},{1,8},{2,4},{3,0},{4,13},{5,9},{6,5},{7,1},{8,14},{9,10},{1... | collective-permute-start | bytes 110600 | tf_op jit(solution)/shard_map/ppermute | solution.py:41
  31.4 1.5 %collective-permute-done.5.refs_2_ = bf16[8,2304]{1,0:T(8,128)(2,1)S(1)} collective-permute-done((bf16[8,2304]{1,0:T(8,128)(2,1)S(1)}, bf16[8,2304]{1,0:T(8,128)(2,1)S(1)}, u32[]{:S(2)}, u32[]{:S(2)}) %collective-permute-start.5) | collective-permute-done | bytes 36896 | tf_op jit(solution)/shard_map/ppermute | solution.py:41
  33.6 3.5 %attend.1 = (f32[136,128]{1,0:T(8,128)S(1)}, f32[136,128]{1,0:T(8,128)S(1)}, f32[136,128]{1,0:T(8,128)S(1)}, f32[136,128]{1,0:T(8,128)S(1)}) custom-call(bf16[8,2304]{1,0:T(8,128)(2,1)S(1)} %collective-permute-done.3.refs_0_, bf16[8,2304]{1,0:T(8,128)(2,1)S(1)} %collective-permute-done.4.refs_1_, bf16[8,2304]{1,0:T(8,128)(2,1)S(1)} %collective-permute-done.5.refs_2_, ...), custom_call_target="tpu_custom_call" | custom-call | tf_op jit(solution)/shard_map/attend/pallas_call | solution.py:250
  37.1 4.1 %collective-permute-start.7 = (f32[136,128]{1,0:T(8,128)S(1)}, f32[136,128]{1,0:T(8,128)S(1)}, u32[]{:S(2)}, u32[]{:S(2)}) collective-permute-start(f32[136,128]{1,0:T(8,128)S(1)} %get-tuple-element.20), channel_id=1, source_target_pairs={{0,4},{4,0},{8,12},{12,8},{1,5},{5,1},{9,13},{13,9},{2,6},{6,2},{1... | collective-permute-start | bytes 208904 | tf_op jit(solution)/shard_map/ppermute | solution.py:36
  41.5 2.2 %collective-permute-start.9 = (f32[136,128]{1,0:T(8,128)S(1)}, f32[136,128]{1,0:T(8,128)S(1)}, u32[]{:S(2)}, u32[]{:S(2)}) collective-permute-start(f32[136,128]{1,0:T(8,128)S(1)} %get-tuple-element.22), channel_id=1, source_target_pairs={{0,12},{4,8},{8,4},{12,0},{1,13},{5,9},{9,5},{13,1},{2,14},{6,10},... | collective-permute-start | bytes 208904 | tf_op jit(solution)/shard_map/ppermute | solution.py:36
  43.7 5.3 %collective-permute-done.8.refs_2_ = f32[136,128]{1,0:T(8,128)S(1)} collective-permute-done((f32[136,128]{1,0:T(8,128)S(1)}, f32[136,128]{1,0:T(8,128)S(1)}, u32[]{:S(2)}, u32[]{:S(2)}) %collective-permute-start.8) | collective-permute-done | bytes 69664 | tf_op jit(solution)/shard_map/ppermute | solution.py:36
  49.2 0.7 collective-permute-start.10
  49.9 2.6 %collective-permute-start.11 = (bf16[8,2048]{1,0:T(8,128)(2,1)S(1)}, bf16[8,2048]{1,0:T(8,128)(2,1)S(1)}, u32[]{:S(2)}, u32[]{:S(2)}) collective-permute-start(bf16[8,2048]{1,0:T(8,128)(2,1)S(1)} %merge.1), channel_id=1, source_target_pairs={{0,4},{1,0},{2,12},{3,8},{4,5},{5,1},{6,13},{7,9},{8,6},{9,2},{10,... | collective-permute-start | bytes 98312 | tf_op jit(solution)/shard_map/ppermute | solution.py:41
  52.5 2.8 %collective-permute-start.12 = (bf16[8,2048]{1,0:T(8,128)(2,1)S(1)}, bf16[8,2048]{1,0:T(8,128)(2,1)S(1)}, u32[]{:S(2)}, u32[]{:S(2)}) collective-permute-start(bf16[8,2048]{1,0:T(8,128)(2,1)S(1)} %merge.1), channel_id=1, source_target_pairs={{0,8},{1,12},{2,0},{3,4},{4,9},{5,13},{6,1},{7,5},{8,10},{9,14},{1... | collective-permute-start | bytes 98312 | tf_op jit(solution)/shard_map/ppermute | solution.py:41
  55.3 1.6 %collective-permute-done.12.refs_2_ = bf16[8,2048]{1,0:T(8,128)(2,1)S(1)} collective-permute-done((bf16[8,2048]{1,0:T(8,128)(2,1)S(1)}, bf16[8,2048]{1,0:T(8,128)(2,1)S(1)}, u32[]{:S(2)}, u32[]{:S(2)}) %collective-permute-start.12) | collective-permute-done | bytes 32800 | tf_op jit(solution)/shard_map/ppermute | solution.py:41
  56.9 1.7 %collective-permute-done.13.refs_3_ = bf16[8,2048]{1,0:T(8,128)(2,1)S(1)} collective-permute-done((bf16[8,2048]{1,0:T(8,128)(2,1)S(1)}, bf16[8,2048]{1,0:T(8,128)(2,1)S(1)}, u32[]{:S(2)}, u32[]{:S(2)}) %collective-permute-start.13) | collective-permute-done | bytes 32800 | tf_op jit(solution)/shard_map/ppermute | solution.py:41
  58.6 6.5 %output.1 = (f32[16,4096]{1,0:T(8,128)S(1)}, f32[16,4096]{1,0:T(8,128)S(1)}) custom-call(bf16[8,2048]{1,0:T(8,128)(2,1)S(1)} %collective-permute-done.10.refs_0_, bf16[8,2048]{1,0:T(8,128)(2,1)S(1)} %collective-permute-done.11.refs_1_, bf16[8,2048]{1,0:T(8,128)(2,1)S(1)} %collective-permute-done.12.refs_2_, ...), custom_call_target="tpu_custom_call" | custom-call | tf_op jit(solution)/shard_map/output/pallas_call | solution.py:351
  65.1 0.6 collective-permute-start.14
  65.8 1.2 %collective-permute-done.14 = f32[16,4096]{1,0:T(8,128)S(1)} collective-permute-done((f32[16,4096]{1,0:T(8,128)S(1)}, f32[16,4096]{1,0:T(8,128)S(1)}, u32[]{:S(2)}, u32[]{:S(2)}) %collective-permute-start.14) | collective-permute-done | bytes 262176 | tf_op jit(solution)/shard_map/ppermute | solution.py:47
  67.0 2.7 %collective-permute-start.15 = (f32[16,4096]{1,0:T(8,128)S(1)}, f32[16,4096]{1,0:T(8,128)S(1)}, u32[]{:S(2)}, u32[]{:S(2)}) collective-permute-start(f32[16,4096]{1,0:T(8,128)S(1)} %add.13), channel_id=1, source_target_pairs={{0,2},{1,3},{2,0},{3,1},{4,6},{5,7},{6,4},{7,5},{8,10},{9,11},{10,... | collective-permute-start | bytes 786440 | tf_op jit(solution)/shard_map/ppermute | solution.py:47
  69.7 6.8 %collective-permute-done.15 = f32[16,4096]{1,0:T(8,128)S(1)} collective-permute-done((f32[16,4096]{1,0:T(8,128)S(1)}, f32[16,4096]{1,0:T(8,128)S(1)}, u32[]{:S(2)}, u32[]{:S(2)}) %collective-permute-start.15) | collective-permute-done | bytes 262176 | tf_op jit(solution)/shard_map/ppermute | solution.py:47
  76.6 1.3 %collective-permute-done.16 = bf16[16,4096]{1,0:T(8,128)(2,1)S(1)} collective-permute-done((bf16[16,4096]{1,0:T(8,128)(2,1)S(1)}, bf16[16,4096]{1,0:T(8,128)(2,1)S(1)}, u32[]{:S(2)}, u32[]{:S(2)}) %collective-permute-start.16) | collective-permute-done | bytes 131104 | tf_op jit(solution)/shard_map/ppermute | solution.py:47
  78.0 0.7 pad_maximum_fusion
  (39 shorter events, 1.5 us)
Async XLA Ops:
  0.0 33.5 %copy-start.13 = (s32[8]{0:T(128)S(1)}, s32[8]{0:T(128)}, u32[]{:S(2)}) copy-start(s32[8]{0:T(128)} %refs_4_.2) | copy-start | bytes 100
  0.0 1.6 %copy-start = (bf16[4096,256]{1,0:T(8,128)(2,1)S(1)}, bf16[4096,256]{1,0:T(8,128)(2,1)}, u32[]{:S(2)}) copy-start(bf16[4096,256]{1,0:T(8,128)(2,1)} %w_keyval.1) | copy-start | bytes 6291460
  1.6 0.9 %copy-start.3 = (bf16[32,4096]{1,0:T(8,128)(2,1)S(1)}, bf16[32,4096]{1,0:T(8,128)(2,1)}, u32[]{:S(2)}) copy-start(bf16[32,4096]{1,0:T(8,128)(2,1)} %residual.1) | copy-start | bytes 786436
  2.6 0.7 copy-start.6
  3.3 0.7 copy-start.7
  4.0 0.7 copy-start.11
  4.7 0.7 copy-start.12
  5.4 28.2 %copy-start.1 = (bf16[8,4,128,128]{3,2,1,0:T(8,128)(2,1)S(1)}, bf16[8,4,128,128]{3,2,1,0:T(8,128)(2,1)}, u32[]{:S(2)}) copy-start(bf16[8,4,128,128]{3,2,1,0:T(8,128)(2,1)} %refs_5_.1) | copy-start | bytes 3145732
  5.4 28.2 %copy-start.2 = (bf16[8,4,128,128]{3,2,1,0:T(8,128)(2,1)S(1)}, bf16[8,4,128,128]{3,2,1,0:T(8,128)(2,1)}, u32[]{:S(2)}) copy-start(bf16[8,4,128,128]{3,2,1,0:T(8,128)(2,1)} %refs_6_.1) | copy-start | bytes 3145732
  5.4 28.2 %copy-start.8 = (f32[8,4,128]{2,1,0:T(4,128)S(1)}, f32[8,4,128]{2,1,0:T(4,128)}, u32[]{:S(2)}) copy-start(f32[8,4,128]{2,1,0:T(4,128)} %param.25) | copy-start | bytes 49156
  5.4 28.2 %copy-start.9 = (f32[8,4,128]{2,1,0:T(4,128)S(1)}, f32[8,4,128]{2,1,0:T(4,128)}, u32[]{:S(2)}) copy-start(f32[8,4,128]{2,1,0:T(4,128)} %param.26) | copy-start | bytes 49156
  5.4 53.2 %copy-start.5 = (f32[1,32,4096]{2,1,0:T(8,128)S(1)}, f32[1,32,4096]{2,1,0:T(8,128)}, u32[]{:S(2)}) copy-start(f32[1,32,4096]{2,1,0:T(8,128)} %param.16) | copy-start | bytes 1572868
  5.4 53.2 %copy-start.10 = (f32[4096]{0:T(1024)S(1)}, f32[4096]{0:T(1024)}, u32[]{:S(2)}) copy-start(f32[4096]{0:T(1024)} %param.29) | copy-start | bytes 49156
  5.4 71.1 %copy-start.4 = (bf16[32,4096]{1,0:T(8,128)(2,1)S(1)}, bf16[32,4096]{1,0:T(8,128)(2,1)}, u32[]{:S(2)}) copy-start(bf16[32,4096]{1,0:T(8,128)(2,1)} %residual.1) | copy-start | bytes 786436
  12.2 5.7 %collective-permute-start = (f32[8,2432]{1,0:T(8,128)S(1)}, f32[8,2432]{1,0:T(8,128)S(1)}, u32[]{:S(2)}, u32[]{:S(2)}) collective-permute-start(f32[8,2432]{1,0:T(8,128)S(1)} %get-tuple-element.16), channel_id=1, source_target_pairs={{0,4},{4,0},{8,12},{12,8},{1,5},{5,1},{9,13},{13,9},{2,6},{6,2},{1... | collective-permute-start | bytes 233480 | tf_op jit(solution)/shard_map/ppermute | solution.py:36
  15.3 8.1 %collective-permute-start.1 = (f32[8,2432]{1,0:T(8,128)S(1)}, f32[8,2432]{1,0:T(8,128)S(1)}, u32[]{:S(2)}, u32[]{:S(2)}) collective-permute-start(f32[8,2432]{1,0:T(8,128)S(1)} %get-tuple-element.17), channel_id=1, source_target_pairs={{0,8},{4,12},{8,0},{12,4},{1,9},{5,13},{9,1},{13,5},{2,10},{6,14},... | collective-permute-start | bytes 233480 | tf_op jit(solution)/shard_map/ppermute | solution.py:36
  17.9 6.3 %collective-permute-start.2 = (f32[8,2432]{1,0:T(8,128)S(1)}, f32[8,2432]{1,0:T(8,128)S(1)}, u32[]{:S(2)}, u32[]{:S(2)}) collective-permute-start(f32[8,2432]{1,0:T(8,128)S(1)} %get-tuple-element.18), channel_id=1, source_target_pairs={{0,12},{4,8},{8,4},{12,0},{1,13},{5,9},{9,5},{13,1},{2,14},{6,10},... | collective-permute-start | bytes 233480 | tf_op jit(solution)/shard_map/ppermute | solution.py:36
  24.3 7.2 %collective-permute-start.3 = (bf16[8,2304]{1,0:T(8,128)(2,1)S(1)}, bf16[8,2304]{1,0:T(8,128)(2,1)S(1)}, u32[]{:S(2)}, u32[]{:S(2)}) collective-permute-start(bf16[8,2304]{1,0:T(8,128)(2,1)S(1)} %norm.1), channel_id=1, source_target_pairs={{0,0},{1,4},{2,8},{3,12},{4,1},{5,5},{6,9},{7,13},{8,2},{9,6},{10,... | collective-permute-start | bytes 110600 | tf_op jit(solution)/shard_map/ppermute | solution.py:41
  24.9 6.5 %collective-permute-start.4 = (bf16[8,2304]{1,0:T(8,128)(2,1)S(1)}, bf16[8,2304]{1,0:T(8,128)(2,1)S(1)}, u32[]{:S(2)}, u32[]{:S(2)}) collective-permute-start(bf16[8,2304]{1,0:T(8,128)(2,1)S(1)} %norm.1), channel_id=1, source_target_pairs={{0,4},{1,0},{2,12},{3,8},{4,5},{5,1},{6,13},{7,9},{8,6},{9,2},{10,... | collective-permute-start | bytes 110600 | tf_op jit(solution)/shard_map/ppermute | solution.py:41
  27.6 5.3 %collective-permute-start.5 = (bf16[8,2304]{1,0:T(8,128)(2,1)S(1)}, bf16[8,2304]{1,0:T(8,128)(2,1)S(1)}, u32[]{:S(2)}, u32[]{:S(2)}) collective-permute-start(bf16[8,2304]{1,0:T(8,128)(2,1)S(1)} %norm.1), channel_id=1, source_target_pairs={{0,8},{1,12},{2,0},{3,4},{4,9},{5,13},{6,1},{7,5},{8,10},{9,14},{1... | collective-permute-start | bytes 110600 | tf_op jit(solution)/shard_map/ppermute | solution.py:41
  30.2 3.4 %collective-permute-start.6 = (bf16[8,2304]{1,0:T(8,128)(2,1)S(1)}, bf16[8,2304]{1,0:T(8,128)(2,1)S(1)}, u32[]{:S(2)}, u32[]{:S(2)}) collective-permute-start(bf16[8,2304]{1,0:T(8,128)(2,1)S(1)} %norm.1), channel_id=1, source_target_pairs={{0,12},{1,8},{2,4},{3,0},{4,13},{5,9},{6,5},{7,1},{8,14},{9,10},{1... | collective-permute-start | bytes 110600 | tf_op jit(solution)/shard_map/ppermute | solution.py:41
  37.1 6.7 %collective-permute-start.7 = (f32[136,128]{1,0:T(8,128)S(1)}, f32[136,128]{1,0:T(8,128)S(1)}, u32[]{:S(2)}, u32[]{:S(2)}) collective-permute-start(f32[136,128]{1,0:T(8,128)S(1)} %get-tuple-element.20), channel_id=1, source_target_pairs={{0,4},{4,0},{8,12},{12,8},{1,5},{5,1},{9,13},{13,9},{2,6},{6,2},{1... | collective-permute-start | bytes 208904 | tf_op jit(solution)/shard_map/ppermute | solution.py:36
  41.2 7.8 %collective-permute-start.8 = (f32[136,128]{1,0:T(8,128)S(1)}, f32[136,128]{1,0:T(8,128)S(1)}, u32[]{:S(2)}, u32[]{:S(2)}) collective-permute-start(f32[136,128]{1,0:T(8,128)S(1)} %get-tuple-element.21), channel_id=1, source_target_pairs={{0,8},{4,12},{8,0},{12,4},{1,9},{5,13},{9,1},{13,5},{2,10},{6,14},... | collective-permute-start | bytes 208904 | tf_op jit(solution)/shard_map/ppermute | solution.py:36
  41.5 7.5 %collective-permute-start.9 = (f32[136,128]{1,0:T(8,128)S(1)}, f32[136,128]{1,0:T(8,128)S(1)}, u32[]{:S(2)}, u32[]{:S(2)}) collective-permute-start(f32[136,128]{1,0:T(8,128)S(1)} %get-tuple-element.22), channel_id=1, source_target_pairs={{0,12},{4,8},{8,4},{12,0},{1,13},{5,9},{9,5},{13,1},{2,14},{6,10},... | collective-permute-start | bytes 208904 | tf_op jit(solution)/shard_map/ppermute | solution.py:36
  49.2 6.1 %collective-permute-start.10 = (bf16[8,2048]{1,0:T(8,128)(2,1)S(1)}, bf16[8,2048]{1,0:T(8,128)(2,1)S(1)}, u32[]{:S(2)}, u32[]{:S(2)}) collective-permute-start(bf16[8,2048]{1,0:T(8,128)(2,1)S(1)} %merge.1), channel_id=1, source_target_pairs={{0,0},{1,4},{2,8},{3,12},{4,1},{5,5},{6,9},{7,13},{8,2},{9,6},{10,... | collective-permute-start | bytes 98312 | tf_op jit(solution)/shard_map/ppermute | solution.py:41
  49.9 5.4 %collective-permute-start.11 = (bf16[8,2048]{1,0:T(8,128)(2,1)S(1)}, bf16[8,2048]{1,0:T(8,128)(2,1)S(1)}, u32[]{:S(2)}, u32[]{:S(2)}) collective-permute-start(bf16[8,2048]{1,0:T(8,128)(2,1)S(1)} %merge.1), channel_id=1, source_target_pairs={{0,4},{1,0},{2,12},{3,8},{4,5},{5,1},{6,13},{7,9},{8,6},{9,2},{10,... | collective-permute-start | bytes 98312 | tf_op jit(solution)/shard_map/ppermute | solution.py:41
  52.5 4.4 %collective-permute-start.12 = (bf16[8,2048]{1,0:T(8,128)(2,1)S(1)}, bf16[8,2048]{1,0:T(8,128)(2,1)S(1)}, u32[]{:S(2)}, u32[]{:S(2)}) collective-permute-start(bf16[8,2048]{1,0:T(8,128)(2,1)S(1)} %merge.1), channel_id=1, source_target_pairs={{0,8},{1,12},{2,0},{3,4},{4,9},{5,13},{6,1},{7,5},{8,10},{9,14},{1... | collective-permute-start | bytes 98312 | tf_op jit(solution)/shard_map/ppermute | solution.py:41
  55.3 3.3 %collective-permute-start.13 = (bf16[8,2048]{1,0:T(8,128)(2,1)S(1)}, bf16[8,2048]{1,0:T(8,128)(2,1)S(1)}, u32[]{:S(2)}, u32[]{:S(2)}) collective-permute-start(bf16[8,2048]{1,0:T(8,128)(2,1)S(1)} %merge.1), channel_id=1, source_target_pairs={{0,12},{1,8},{2,4},{3,0},{4,13},{5,9},{6,5},{7,1},{8,14},{9,10},{1... | collective-permute-start | bytes 98312 | tf_op jit(solution)/shard_map/ppermute | solution.py:41
  65.1 1.8 %collective-permute-start.14 = (f32[16,4096]{1,0:T(8,128)S(1)}, f32[16,4096]{1,0:T(8,128)S(1)}, u32[]{:S(2)}, u32[]{:S(2)}) collective-permute-start(f32[16,4096]{1,0:T(8,128)S(1)} %get-tuple-element.24), channel_id=1, source_target_pairs={{0,1},{1,0},{2,3},{3,2},{4,5},{5,4},{6,7},{7,6},{8,9},{9,8},{10,11... | collective-permute-start | bytes 786440 | tf_op jit(solution)/shard_map/ppermute | solution.py:47
  67.0 9.5 %collective-permute-start.15 = (f32[16,4096]{1,0:T(8,128)S(1)}, f32[16,4096]{1,0:T(8,128)S(1)}, u32[]{:S(2)}, u32[]{:S(2)}) collective-permute-start(f32[16,4096]{1,0:T(8,128)S(1)} %add.13), channel_id=1, source_target_pairs={{0,2},{1,3},{2,0},{3,1},{4,6},{5,7},{6,4},{7,5},{8,10},{9,11},{10,... | collective-permute-start | bytes 786440 | tf_op jit(solution)/shard_map/ppermute | solution.py:47
  76.5 1.4 %collective-permute-start.16 = (bf16[16,4096]{1,0:T(8,128)(2,1)S(1)}, bf16[16,4096]{1,0:T(8,128)(2,1)S(1)}, u32[]{:S(2)}, u32[]{:S(2)}) collective-permute-start(bf16[16,4096]{1,0:T(8,128)(2,1)S(1)} %add_convert_fusion), channel_id=1, source_target_pairs={{0,1},{1,0},{2,3},{3,2},{4,5},{5,4},{6,7},{7,6},{8,9},{9,8},{10,11... | collective-permute-start | bytes 393224 | tf_op jit(solution)/shard_map/ppermute | solution.py:47

commit v4 on v3

--- a/solution.py
+++ b/solution.py
@@ -51,34 +51,27 @@
     return pltpu.CompilerParams(vmem_limit_bytes=mib << 20)
 
 
-def project_kernel(n, residual, gain, smooth, w_query, query_scale, w_keyval, keyval_scale, *rest):
+def project_kernel(n, residual, gain, smooth, w_query, w_keyval, *rest):
     outs = rest[:n]
-    x_buf, g_buf, s_buf, q_buf, k_buf, qs_buf, ks_buf, smoothed, q_sum, k_sum, squares_sum, sems, big_sems = rest[n:]
+    x_buf, g_buf, s_buf, q_buf, k_buf, smoothed, q_sum, k_sum, squares_sum, sems, big_sems = rest[n:]
     rows, width = x_buf.shape
-    steps = big_sems.shape[0] // 2
+    queries = w_query.shape[1]
+    steps = big_sems.shape[0] - 1
     depth = width // steps
     small = [
         pltpu.make_async_copy(source, target, sems.at[i])
-        for i, (source, target) in enumerate(
-            [(residual, x_buf), (gain, g_buf), (smooth, s_buf), (query_scale, qs_buf), (keyval_scale, ks_buf)]
-        )
+        for i, (source, target) in enumerate([(residual, x_buf), (gain, g_buf), (smooth, s_buf)])
     ]
-    for copy in small[:3]:
+    for copy in small:
         copy.start()
     large = []
     for i in range(steps):
         part = pl.ds(i * depth, depth)
-        large.append(
-            (
-                pltpu.make_async_copy(w_keyval.at[part], k_buf.at[part], big_sems.at[2 * i]),
-                pltpu.make_async_copy(w_query.at[part], q_buf.at[part], big_sems.at[2 * i + 1]),
-            )
-        )
-        for copy in large[-1]:
-            copy.start()
-    for copy in small[3:]:
-        copy.start()
-    for copy in small[:3]:
+        large.append(pltpu.make_async_copy(w_query.at[part], q_buf.at[part], big_sems.at[i]))
+    large.append(pltpu.make_async_copy(w_keyval, k_buf, big_sems.at[steps]))
+    for copy in large:
+        copy.start(priority=1)
+    for copy in small:
         copy.wait()
     squares = jnp.zeros((rows, LANES), f32)
     for i in range(width // LANES):
@@ -86,104 +79,92 @@
         x = x_buf[:, lanes].astype(f32)
         squares += x * x
         smoothed[:, lanes] = (x * (g_buf[i : i + 1, :] / s_buf[i : i + 1, :])).astype(bf16)
-    squares = jnp.sum(squares, axis=1, keepdims=True)
+    squares_sum[...] = jnp.broadcast_to(jnp.sum(squares, axis=1, keepdims=True), (rows, LANES))
     for i in range(steps):
         part = slice(i * depth, (i + 1) * depth)
-        large[i][0].wait()
-        k_part = jnp.dot(smoothed[:, part], k_buf[part, :], preferred_element_type=f32)
-        large[i][1].wait()
-        q_part = jnp.dot(smoothed[:, part], q_buf[part, :], preferred_element_type=f32)
+        large[i].wait()
+        term = jnp.dot(smoothed[:, part], q_buf[part, :], preferred_element_type=f32)
         if i == 0:
-            q_sum[...], k_sum[...] = q_part, k_part
+            q_sum[...] = term
         else:
-            q_sum[...] += q_part
-            k_sum[...] += k_part
-    for copy in small[3:]:
-        copy.wait()
+            q_sum[...] += term
+    large[steps].wait()
+    k_sum[...] = jnp.dot(smoothed[...], k_buf[...], preferred_element_type=f32)
     me = lax.axis_index("gx")
     requests = rows // n
-    q_tiles, k_tiles = q_sum.shape[1] // LANES, k_sum.shape[1] // LANES
-    squares_sum[...] = jnp.broadcast_to(squares, (rows, LANES))
+    columns = queries + k_buf.shape[1]
     for k in range(n):
         at = pl.ds(pl.multiple_of((me ^ k) * requests, requests), requests)
-        for t in range(q_tiles):
-            lanes = slice(t * LANES, (t + 1) * LANES)
-            outs[k][:, lanes] = q_sum[at, lanes] * qs_buf[t : t + 1, :]
-        for t in range(k_tiles):
-            lanes = slice(t * LANES, (t + 1) * LANES)
-            outs[k][:, (q_tiles + t) * LANES : (q_tiles + t + 1) * LANES] = k_sum[at, lanes] * ks_buf[t : t + 1, :]
-        outs[k][:, (q_tiles + k_tiles) * LANES :] = squares_sum[at, :]
-
-
-def project(n, residual, gain, smooth, w_query, query_scale, w_keyval, keyval_scale):
+        outs[k][:, :queries] = q_sum[at, :]
+        outs[k][:, queries:columns] = k_sum[at, :]
+        outs[k][:, columns:] = squares_sum[at, :]
+
+
+def project(n, residual, gain, smooth, w_query, w_keyval):
     rows, width = residual.shape
-    queries, keyvals = w_query.shape[1], w_keyval.shape[1]
-    columns = queries + keyvals + LANES
+    columns = w_query.shape[1] + w_keyval.shape[1]
     steps = 8
     return pl.pallas_call(
         functools.partial(project_kernel, n),
-        in_specs=[HBM] * 7,
+        in_specs=[HBM] * 5,
         out_specs=[VMEM] * n,
-        out_shape=[jax.ShapeDtypeStruct((rows // n, columns), f32)] * n,
+        out_shape=[jax.ShapeDtypeStruct((rows // n, columns + LANES), f32)] * n,
         scratch_shapes=[
             pltpu.VMEM((rows, width), bf16),
             pltpu.VMEM((width // LANES, LANES), f32),
             pltpu.VMEM((width // LANES, LANES), f32),
-            pltpu.VMEM((width, queries), bf16),
-            pltpu.VMEM((width, keyvals), bf16),
-            pltpu.VMEM((queries // LANES, LANES), f32),
-            pltpu.VMEM((keyvals // LANES, LANES), f32),
+            pltpu.VMEM(w_query.shape, bf16),
+            pltpu.VMEM(w_keyval.shape, bf16),
             pltpu.VMEM((rows, width), bf16),
-            pltpu.VMEM((rows, queries), f32),
-            pltpu.VMEM((rows, keyvals), f32),
+            pltpu.VMEM((rows, w_query.shape[1]), f32),
+            pltpu.VMEM((rows, w_keyval.shape[1]), f32),
             pltpu.VMEM((rows, LANES), f32),
-            pltpu.SemaphoreType.DMA((5,)),
-            pltpu.SemaphoreType.DMA((2 * steps,)),
+            pltpu.SemaphoreType.DMA((3,)),
+            pltpu.SemaphoreType.DMA((steps + 1,)),
         ],
-        compiler_params=params(50),
+        compiler_params=params(60),
         name="project",
-    )(
-        residual,
-        gain.reshape(-1, LANES),
-        smooth.reshape(-1, LANES),
-        w_query,
-        query_scale.reshape(-1, LANES),
-        w_keyval,
-        keyval_scale.reshape(-1, LANES),
-    )
-
-
-def norm_kernel(*refs):
+    )(residual, gain.reshape(-1, LANES), smooth.reshape(-1, LANES), w_query, w_keyval)
+
+
+def norm_kernel(query_scale, keyval_scale, *refs):
     parts, out = refs[:-1], refs[-1]
     total = parts[0][...]
     for part in parts[1:]:
         total = total + part[...]
     columns = out.shape[1]
-    out[...] = (total[:, :columns] * lax.rsqrt(total[:, columns : columns + 1] / D + EPSILON)).astype(bf16)
-
-
-def norm(parts):
+    row_scale = lax.rsqrt(total[:, columns : columns + 1] / D + EPSILON)
+    tiles = query_scale.shape[0]
+    for t in range(columns // LANES):
+        scale = query_scale[t : t + 1, :] if t < tiles else keyval_scale[t - tiles : t - tiles + 1, :]
+        lanes = slice(t * LANES, (t + 1) * LANES)
+        out[:, lanes] = (row_scale * (total[:, lanes] * scale)).astype(bf16)
+
+
+def norm(parts, query_scale, keyval_scale):
     rows, columns = parts[0].shape
     return pl.pallas_call(
         norm_kernel,
-        in_specs=[VMEM] * len(parts),
+        in_specs=[VMEM] * (2 + len(parts)),
         out_specs=VMEM,
         out_shape=jax.ShapeDtypeStruct((rows, columns - LANES), bf16),
         compiler_params=params(8),
         name="norm",
-    )(*parts)
+    )(query_scale.reshape(-1, LANES), keyval_scale.reshape(-1, LANES), *parts)
 
 
 def attend_kernel(n, *refs):
     pieces = refs[:n]
-    lengths, keys, values, key_scale, value_scale = refs[n : n + 5]
-    outs = refs[n + 5 : 2 * n + 5]
-    placed, k_buf, v_buf, q_rows, logits, messages, fresh, sems = refs[2 * n + 5 :]
+    lengths, keys, values, key_scale, value_scale, w_out = refs[n : n + 6]
+    outs, w_head = refs[n + 6 : 2 * n + 6], refs[2 * n + 6]
+    placed, k_buf, v_buf, q_rows, logits, messages, fresh, sems = refs[2 * n + 7 :]
     requests, _, local, _ = k_buf.shape
     load_keys = pltpu.make_async_copy(keys, k_buf, sems.at[0])
     load_values = pltpu.make_async_copy(values, v_buf, sems.at[1])
+    load_weights = pltpu.make_async_copy(w_out.at[pl.ds(0, w_head.shape[0])], w_head, sems.at[2])
     load_keys.start()
     load_values.start()
+    load_weights.start(priority=1)
     me = lax.axis_index("gx")
     for k in range(n):
         placed[me ^ k] = pieces[k][...].astype(f32)
@@ -241,17 +222,19 @@
         messages[p, count:, :] = jnp.concatenate(rows + [jnp.zeros((spare, LANES), f32)], axis=0)
     for k in range(n):
         outs[k][...] = messages[me ^ k]
-
-
-def attend(n, pieces, lengths, keys, values, key_scale, value_scale):
+    load_weights.wait()
+
+
+def attend(n, pieces, lengths, keys, values, key_scale, value_scale, w_out):
     requests, _, local, _ = keys.shape
     count = requests * GROUP
     height = count + -(-2 * count // LANES // 8) * 8
     return pl.pallas_call(
         functools.partial(attend_kernel, n),
-        in_specs=[VMEM] * n + [SMEM, ANY, ANY, VMEM, VMEM],
-        out_specs=[VMEM] * n,
-        out_shape=[jax.ShapeDtypeStruct((height, LANES), f32)] * n,
+        in_specs=[VMEM] * n + [SMEM, HBM, HBM, VMEM, VMEM, HBM],
+        out_specs=[VMEM] * (n + 1),
+        out_shape=[jax.ShapeDtypeStruct((height, LANES), f32)] * n
+        + [jax.ShapeDtypeStruct((w_out.shape[0] // 2, w_out.shape[1]), bf16)],
         scratch_shapes=[
             pltpu.VMEM((n,) + pieces[0].shape, f32),
             pltpu.VMEM(keys.shape, bf16),
@@ -260,11 +243,11 @@
             pltpu.VMEM((requests * HEADS, local), f32),
             pltpu.VMEM((n, height, LANES), f32),
             pltpu.VMEM((requests * 2 * KV_HEADS, HEAD_DIM), f32),
-            pltpu.SemaphoreType.DMA((2,)),
+            pltpu.SemaphoreType.DMA((3,)),
         ],
-        compiler_params=params(32),
+        compiler_params=params(30),
         name="attend",
-    )(*pieces, lengths, keys, values, key_scale.reshape(-1, local), value_scale.reshape(-1, local))
+    )(*pieces, lengths, keys, values, key_scale.reshape(-1, local), value_scale.reshape(-1, local), w_out)
 
 
 def merge_kernel(*refs):
@@ -310,29 +293,27 @@
 
 def output_kernel(n, *refs):
     pieces = refs[:n]
-    w_out, out_scale, ffn, kept, given, w_buf, ffn_buf, total, placed, sems = refs[n:]
-    depth_all, width = w_buf.shape
+    w_head, w_out, out_scale, ffn, kept, given, w_buf, ffn_buf, total, placed, sems = refs[n:]
+    rest, width = w_buf.shape
     steps = sems.shape[0] - 1
-    depth = depth_all // steps
+    depth, head = rest // steps, w_head.shape[0]
     copies = []
     for i in range(steps):
         part = pl.ds(i * depth, depth)
-        copies.append(pltpu.make_async_copy(w_out.at[part], w_buf.at[part], sems.at[i]))
-        copies[-1].start()
+        source = w_out.at[pl.ds(head + i * depth, depth)]
+        copies.append(pltpu.make_async_copy(source, w_buf.at[part], sems.at[i]))
+        copies[-1].start(priority=1)
     load = pltpu.make_async_copy(ffn, ffn_buf, sems.at[steps])
     load.start()
     me = lax.axis_index("gx")
     for k in range(n):
         placed[me ^ k] = pieces[k][...].astype(f32)
+    attended = placed[...].reshape(total.shape[0], head + rest).astype(bf16)
+    total[...] = jnp.dot(attended[:, :head], w_head[...], preferred_element_type=f32)
     for i in range(steps):
         part = slice(i * depth, (i + 1) * depth)
         copies[i].wait()
-        attended = placed[:, :, part].reshape(total.shape[0], depth).astype(bf16)
-        term = jnp.dot(attended, w_buf[part, :], preferred_element_type=f32)
-        if i == 0:
-            total[...] = term
-        else:
-            total[...] += term
+        total[...] += jnp.dot(attended[:, head:][:, part], w_buf[part, :], preferred_element_type=f32)
     load.wait()
     for t in range(width // LANES):
         lanes = slice(t * LANES, (t + 1) * LANES)
@@ -343,26 +324,26 @@
     given[...] = total[pl.ds(pl.multiple_of((1 - core) * rows, rows), rows), :]
 
 
-def output(pieces, w_out, out_scale, ffn):
+def output(pieces, w_head, w_out, out_scale, ffn):
     n = len(pieces)
     rows = ffn.shape[0]
     width = w_out.shape[1]
-    steps = 8
+    steps = 4
     return pl.pallas_call(
         functools.partial(output_kernel, n),
-        in_specs=[VMEM] * n + [HBM, VMEM, HBM],
+        in_specs=[VMEM] * (n + 1) + [HBM, VMEM, HBM],
         out_specs=[VMEM] * 2,
         out_shape=[jax.ShapeDtypeStruct((rows // 2, width), f32)] * 2,
         scratch_shapes=[
-            pltpu.VMEM(w_out.shape, bf16),
+            pltpu.VMEM((w_out.shape[0] - w_head.shape[0], width), bf16),
             pltpu.VMEM((rows, width), f32),
             pltpu.VMEM((rows, width), f32),
             pltpu.VMEM((n,) + pieces[0].shape, f32),
             pltpu.SemaphoreType.DMA((steps + 1,)),
         ],
-        compiler_params=params(50),
+        compiler_params=params(30),
         name="output",
-    )(*pieces, w_out, out_scale.reshape(-1, LANES), ffn)
+    )(*pieces, w_head, w_out, out_scale.reshape(-1, LANES), ffn)
 
 
 def body(n_gx, n_gy, residual, ffn_partial, norm_gain, smooth_scale, w_query, query_scale, w_keyval, keyval_scale,
@@ -370,11 +351,11 @@
     gy = lax.axis_index("gy")
     rows = residual.shape[0]
     requests = rows // n_gy
-    parts = project(n_gx, residual, norm_gain, smooth_scale, w_query, query_scale, w_keyval, keyval_scale)
-    pieces = spread(norm(trade(parts, "gx", n_gx)), n_gx)
-    parts = attend(n_gx, pieces, lengths, key_cache, value_cache, key_scale, value_scale)
+    parts = project(n_gx, residual, norm_gain, smooth_scale, w_query, w_keyval)
+    pieces = spread(norm(trade(parts, "gx", n_gx), query_scale, keyval_scale), n_gx)
+    *parts, w_head = attend(n_gx, pieces, lengths, key_cache, value_cache, key_scale, value_scale, w_out)
     pieces = spread(merge(trade(parts, "gx", n_gx), requests), n_gx)
-    kept, given = output(pieces, w_out, out_scale, ffn_partial[0])
+    kept, given = output(pieces, w_head, w_out, out_scale, ffn_partial[0])
     core = gy & 1
     chip = kept + swap(given, "gy", n_gy, 1)
     whole = chip + swap(chip, "gy", n_gy, 2)

time: 79.1 us -> 74.2 us (0.938)
  local copies, waits for them, and re-layouts: 5.39 us -> 0.93 us
    unnamed x28 -> x22, local copies, waits for them, and re-layouts: 5.39 us -> 0.93 us
    pallas_call x3, Pallas kernels: 13.4 us -> 12.3 us  [the longest x1 8.15 us: project(): pl.pallas_call(functools.partial(project_kernel, n), in_specs=[HBM] * 5,...]
where the time goes in v4:
time: 74.2 us; the launch traced here: 74 us
  starting transfers between devices  28.9 us (39%)
  waiting for transfers between devices  26.6 us (36%)
  Pallas kernels  16.6 us (22%)
  local copies, waits for them, and re-layouts  0.93 us (1%)
  other arithmetic  0.81 us (1%)
    ppermute x8, starting transfers between devices, spread(): lax.ppermute(value, ('gx', 'gy'), [(a * n + b, (b ^ k) * n + a) for a in...  13.2 us
    ppermute x6, starting transfers between devices, trade(): lax.ppermute(chunks[k], axis, partners(n, k))  12.3 us
    ppermute x6, waiting for transfers between devices, trade(): lax.ppermute(chunks[k], axis, partners(n, k))  11.9 us
    ppermute x3, waiting for transfers between devices, swap(): return lax.ppermute(value, axis, partners(n, offset))  9.32 us
    pallas_call x1, Pallas kernels, project(): pl.pallas_call(functools.partial(project_kernel, n), in_specs=[HBM] * 5,...  8.15 us
    ppermute x8, waiting for transfers between devices, spread(): lax.ppermute(value, ('gx', 'gy'), [(a * n + b, (b ^ k) * n + a) for a in...  5.42 us
    pallas_call x1, Pallas kernels, attend(): pl.pallas_call(functools.partial(attend_kernel, n), in_specs=[VMEM] * n +...  4.09 us
    pallas_call x1, Pallas kernels, output(): pl.pallas_call(functools.partial(output_kernel, n), in_specs=[VMEM] * (n...  4.08 us
  transfers between devices with their start and end apart: 17, of which 11 were waited for; matrix products, arithmetic and copies ran while one was open for 0% of the time, Pallas kernels for 0%

profile of v4, /device:TPU:0, one launch (start us, length us, event | category | flops | bytes accessed | tf_op | source)
XLA Modules:
  0.0 74.0 jit_solution(1883337051294593999)
XLA Ops:
  0.1 8.1 %project.1 = (f32[8,2432]{1,0:T(8,128)}, f32[8,2432]{1,0:T(8,128)}, f32[8,2432]{1,0:T(8,128)}, f32[8,2432]{1,0:T(8,128)}) custom-call(bf16[32,4096]{1,0:T(8,128)(2,1)} %residual.1, f32[32,128]{1,0:T(8,128)} %bitcast.14, f32[32,128]{1,0:T(8,128)} %bitcast.15, bf16[4096,2048]{1,0:T(8,128)(2,1)} %w_query.1, bf16[4096,256]{1,0:T(8,128)(2,1)} %w_keyval.1), custom_call_target="tpu_custom_call" | custom-call | tf_op jit(solution)/shard_map/project/pallas_call | solution.py:107
  8.2 3.1 %collective-permute-start = (f32[8,2432]{1,0:T(8,128)}, f32[8,2432]{1,0:T(8,128)S(1)}, u32[]{:S(2)}, u32[]{:S(2)}) collective-permute-start(f32[8,2432]{1,0:T(8,128)} %get-tuple-element.17), channel_id=1, source_target_pairs={{0,4},{4,0},{8,12},{12,8},{1,5},{5,1},{9,13},{13,9},{2,6},{6,2},{1... | collective-permute-start | bytes 233480 | tf_op jit(solution)/shard_map/ppermute | solution.py:36
  11.3 2.6 %collective-permute-start.1 = (f32[8,2432]{1,0:T(8,128)}, f32[8,2432]{1,0:T(8,128)S(1)}, u32[]{:S(2)}, u32[]{:S(2)}) collective-permute-start(f32[8,2432]{1,0:T(8,128)} %get-tuple-element.18), channel_id=1, source_target_pairs={{0,8},{4,12},{8,0},{12,4},{1,9},{5,13},{9,1},{13,5},{2,10},{6,14},... | collective-permute-start | bytes 233480 | tf_op jit(solution)/shard_map/ppermute | solution.py:36
  13.9 5.7 %collective-permute-done.1.refs_2_ = f32[8,2432]{1,0:T(8,128)S(1)} collective-permute-done((f32[8,2432]{1,0:T(8,128)}, f32[8,2432]{1,0:T(8,128)S(1)}, u32[]{:S(2)}, u32[]{:S(2)}) %collective-permute-start.1) | collective-permute-done | bytes 77856 | tf_op jit(solution)/shard_map/ppermute | solution.py:36
  19.6 0.8 %collective-permute-done.2.refs_3_ = f32[8,2432]{1,0:T(8,128)S(1)} collective-permute-done((f32[8,2432]{1,0:T(8,128)}, f32[8,2432]{1,0:T(8,128)S(1)}, u32[]{:S(2)}, u32[]{:S(2)}) %collective-permute-start.2) | collective-permute-done | bytes 77856 | tf_op jit(solution)/shard_map/ppermute | solution.py:36
  20.4 0.9 %copy-done.3 = f32[8,2432]{1,0:T(8,128)S(1)} copy-done((f32[8,2432]{1,0:T(8,128)S(1)}, f32[8,2432]{1,0:T(8,128)}, u32[]{:S(2)}) %copy-start.3) | copy-done | bytes 77848
  21.3 0.1 norm.1
  21.4 0.7 collective-permute-start.3
  22.1 2.7 %collective-permute-start.4 = (bf16[8,2304]{1,0:T(8,128)(2,1)S(1)}, bf16[8,2304]{1,0:T(8,128)(2,1)S(1)}, u32[]{:S(2)}, u32[]{:S(2)}) collective-permute-start(bf16[8,2304]{1,0:T(8,128)(2,1)S(1)} %norm.1), channel_id=1, source_target_pairs={{0,4},{1,0},{2,12},{3,8},{4,5},{5,1},{6,13},{7,9},{8,6},{9,2},{10,... | collective-permute-start | bytes 110600 | tf_op jit(solution)/shard_map/ppermute | solution.py:41
  24.8 2.5 %collective-permute-start.5 = (bf16[8,2304]{1,0:T(8,128)(2,1)S(1)}, bf16[8,2304]{1,0:T(8,128)(2,1)S(1)}, u32[]{:S(2)}, u32[]{:S(2)}) collective-permute-start(bf16[8,2304]{1,0:T(8,128)(2,1)S(1)} %norm.1), channel_id=1, source_target_pairs={{0,8},{1,12},{2,0},{3,4},{4,9},{5,13},{6,1},{7,5},{8,10},{9,14},{1... | collective-permute-start | bytes 110600 | tf_op jit(solution)/shard_map/ppermute | solution.py:41
  27.3 1.3 %collective-permute-start.6 = (bf16[8,2304]{1,0:T(8,128)(2,1)S(1)}, bf16[8,2304]{1,0:T(8,128)(2,1)S(1)}, u32[]{:S(2)}, u32[]{:S(2)}) collective-permute-start(bf16[8,2304]{1,0:T(8,128)(2,1)S(1)} %norm.1), channel_id=1, source_target_pairs={{0,12},{1,8},{2,4},{3,0},{4,13},{5,9},{6,5},{7,1},{8,14},{9,10},{1... | collective-permute-start | bytes 110600 | tf_op jit(solution)/shard_map/ppermute | solution.py:41
  28.6 1.5 %collective-permute-done.5.refs_2_ = bf16[8,2304]{1,0:T(8,128)(2,1)S(1)} collective-permute-done((bf16[8,2304]{1,0:T(8,128)(2,1)S(1)}, bf16[8,2304]{1,0:T(8,128)(2,1)S(1)}, u32[]{:S(2)}, u32[]{:S(2)}) %collective-permute-start.5) | collective-permute-done | bytes 36896 | tf_op jit(solution)/shard_map/ppermute | solution.py:41
  30.0 0.6 collective-permute-done.6.refs_3_
  30.7 4.1 %attend.1 = (f32[136,128]{1,0:T(8,128)S(1)}, f32[136,128]{1,0:T(8,128)S(1)}, f32[136,128]{1,0:T(8,128)S(1)}, f32[136,128]{1,0:T(8,128)S(1)}, bf16[1024,4096]{1,0:T(8,128)(2,1)S(1)}) custom-call(bf16[8,2304]{1,0:T(8,128)(2,1)S(1)} %collective-permute-done.3.refs_0_, bf16[8,2304]{1,0:T(8,128)(2,1)S(1)} %collective-permute-done.4.refs_1_, ...), custom_call_target="tpu_custom_call" | custom-call | tf_op jit(solution)/shard_map/attend/pallas_call | solution.py:232
  34.8 4.1 %collective-permute-start.7 = (f32[136,128]{1,0:T(8,128)S(1)}, f32[136,128]{1,0:T(8,128)S(1)}, u32[]{:S(2)}, u32[]{:S(2)}) collective-permute-start(f32[136,128]{1,0:T(8,128)S(1)} %get-tuple-element.21), channel_id=1, source_target_pairs={{0,4},{4,0},{8,12},{12,8},{1,5},{5,1},{9,13},{13,9},{2,6},{6,2},{1... | collective-permute-start | bytes 208904 | tf_op jit(solution)/shard_map/ppermute | solution.py:36
  38.9 0.3 collective-permute-start.8
  39.2 2.2 %collective-permute-start.9 = (f32[136,128]{1,0:T(8,128)S(1)}, f32[136,128]{1,0:T(8,128)S(1)}, u32[]{:S(2)}, u32[]{:S(2)}) collective-permute-start(f32[136,128]{1,0:T(8,128)S(1)} %get-tuple-element.23), channel_id=1, source_target_pairs={{0,12},{4,8},{8,4},{12,0},{1,13},{5,9},{9,5},{13,1},{2,14},{6,10},... | collective-permute-start | bytes 208904 | tf_op jit(solution)/shard_map/ppermute | solution.py:36
  41.4 0.1 collective-permute-done.7.refs_1_
  41.5 5.3 %collective-permute-done.8.refs_2_ = f32[136,128]{1,0:T(8,128)S(1)} collective-permute-done((f32[136,128]{1,0:T(8,128)S(1)}, f32[136,128]{1,0:T(8,128)S(1)}, u32[]{:S(2)}, u32[]{:S(2)}) %collective-permute-start.8) | collective-permute-done | bytes 69664 | tf_op jit(solution)/shard_map/ppermute | solution.py:36
  46.8 0.2 merge.1
  47.0 0.7 collective-permute-start.10
  47.6 2.6 %collective-permute-start.11 = (bf16[8,2048]{1,0:T(8,128)(2,1)S(1)}, bf16[8,2048]{1,0:T(8,128)(2,1)S(1)}, u32[]{:S(2)}, u32[]{:S(2)}) collective-permute-start(bf16[8,2048]{1,0:T(8,128)(2,1)S(1)} %merge.1), channel_id=1, source_target_pairs={{0,4},{1,0},{2,12},{3,8},{4,5},{5,1},{6,13},{7,9},{8,6},{9,2},{10,... | collective-permute-start | bytes 98312 | tf_op jit(solution)/shard_map/ppermute | solution.py:41
  50.3 2.8 %collective-permute-start.12 = (bf16[8,2048]{1,0:T(8,128)(2,1)S(1)}, bf16[8,2048]{1,0:T(8,128)(2,1)S(1)}, u32[]{:S(2)}, u32[]{:S(2)}) collective-permute-start(bf16[8,2048]{1,0:T(8,128)(2,1)S(1)} %merge.1), channel_id=1, source_target_pairs={{0,8},{1,12},{2,0},{3,4},{4,9},{5,13},{6,1},{7,5},{8,10},{9,14},{1... | collective-permute-start | bytes 98312 | tf_op jit(solution)/shard_map/ppermute | solution.py:41
  53.0 1.6 %collective-permute-done.12.refs_2_ = bf16[8,2048]{1,0:T(8,128)(2,1)S(1)} collective-permute-done((bf16[8,2048]{1,0:T(8,128)(2,1)S(1)}, bf16[8,2048]{1,0:T(8,128)(2,1)S(1)}, u32[]{:S(2)}, u32[]{:S(2)}) %collective-permute-start.12) | collective-permute-done | bytes 32800 | tf_op jit(solution)/shard_map/ppermute | solution.py:41
  54.6 1.7 %collective-permute-done.13.refs_3_ = bf16[8,2048]{1,0:T(8,128)(2,1)S(1)} collective-permute-done((bf16[8,2048]{1,0:T(8,128)(2,1)S(1)}, bf16[8,2048]{1,0:T(8,128)(2,1)S(1)}, u32[]{:S(2)}, u32[]{:S(2)}) %collective-permute-start.13) | collective-permute-done | bytes 32800 | tf_op jit(solution)/shard_map/ppermute | solution.py:41
  56.4 4.1 %output.1 = (f32[16,4096]{1,0:T(8,128)S(1)}, f32[16,4096]{1,0:T(8,128)S(1)}) custom-call(bf16[8,2048]{1,0:T(8,128)(2,1)S(1)} %collective-permute-done.10.refs_0_, bf16[8,2048]{1,0:T(8,128)(2,1)S(1)} %collective-permute-done.11.refs_1_, bf16[8,2048]{1,0:T(8,128)(2,1)S(1)} %collective-permute-done.12.refs_2_, ...), custom_call_target="tpu_custom_call" | custom-call | tf_op jit(solution)/shard_map/output/pallas_call | solution.py:332
  60.4 0.6 collective-permute-start.14
  61.1 1.2 %collective-permute-done.14 = f32[16,4096]{1,0:T(8,128)S(1)} collective-permute-done((f32[16,4096]{1,0:T(8,128)S(1)}, f32[16,4096]{1,0:T(8,128)S(1)}, u32[]{:S(2)}, u32[]{:S(2)}) %collective-permute-start.14) | collective-permute-done | bytes 262176 | tf_op jit(solution)/shard_map/ppermute | solution.py:47
  62.3 2.7 %collective-permute-start.15 = (f32[16,4096]{1,0:T(8,128)S(1)}, f32[16,4096]{1,0:T(8,128)S(1)}, u32[]{:S(2)}, u32[]{:S(2)}) collective-permute-start(f32[16,4096]{1,0:T(8,128)S(1)} %add.13), channel_id=1, source_target_pairs={{0,2},{1,3},{2,0},{3,1},{4,6},{5,7},{6,4},{7,5},{8,10},{9,11},{10,... | collective-permute-start | bytes 786440 | tf_op jit(solution)/shard_map/ppermute | solution.py:47
  65.0 6.8 %collective-permute-done.15 = f32[16,4096]{1,0:T(8,128)S(1)} collective-permute-done((f32[16,4096]{1,0:T(8,128)S(1)}, f32[16,4096]{1,0:T(8,128)S(1)}, u32[]{:S(2)}, u32[]{:S(2)}) %collective-permute-start.15) | collective-permute-done | bytes 262176 | tf_op jit(solution)/shard_map/ppermute | solution.py:47
  71.9 1.3 %collective-permute-done.16 = bf16[16,4096]{1,0:T(8,128)(2,1)S(1)} collective-permute-done((bf16[16,4096]{1,0:T(8,128)(2,1)S(1)}, bf16[16,4096]{1,0:T(8,128)(2,1)S(1)}, u32[]{:S(2)}, u32[]{:S(2)}) %collective-permute-start.16) | collective-permute-done | bytes 131104 | tf_op jit(solution)/shard_map/ppermute | solution.py:47
  73.3 0.7 pad_maximum_fusion
  (33 shorter events, 0.2 us)
Async XLA Ops:
  0.0 20.4 %copy-start.7 = (f32[2048]{0:T(1024)S(1)}, f32[2048]{0:T(1024)}, u32[]{:S(2)}) copy-start(f32[2048]{0:T(1024)} %param.20) | copy-start | bytes 24580
  0.0 20.4 %copy-start.8 = (f32[256]{0:T(256)S(1)}, f32[256]{0:T(256)}, u32[]{:S(2)}) copy-start(f32[256]{0:T(256)} %param.22) | copy-start | bytes 3076
  0.0 30.7 %copy-start.4 = (f32[8,4,128]{2,1,0:T(4,128)S(1)}, f32[8,4,128]{2,1,0:T(4,128)}, u32[]{:S(2)}) copy-start(f32[8,4,128]{2,1,0:T(4,128)} %param.25) | copy-start | bytes 49156
  0.0 30.7 %copy-start.5 = (f32[8,4,128]{2,1,0:T(4,128)S(1)}, f32[8,4,128]{2,1,0:T(4,128)}, u32[]{:S(2)}) copy-start(f32[8,4,128]{2,1,0:T(4,128)} %param.26) | copy-start | bytes 49156
  0.0 30.7 %copy-start = (bf16[8,4,128,128]{3,2,1,0:T(8,128)(2,1)S(1)}, bf16[8,4,128,128]{3,2,1,0:T(8,128)(2,1)}, u32[]{:S(2)}) copy-start(bf16[8,4,128,128]{3,2,1,0:T(8,128)(2,1)} %refs_5_.2) | copy-start | bytes 3145732
  0.0 30.7 %copy-start.1 = (bf16[8,4,128,128]{3,2,1,0:T(8,128)(2,1)S(1)}, bf16[8,4,128,128]{3,2,1,0:T(8,128)(2,1)}, u32[]{:S(2)}) copy-start(bf16[8,4,128,128]{3,2,1,0:T(8,128)(2,1)} %refs_6_.1) | copy-start | bytes 3145732
  0.0 30.7 %copy-start.9 = (s32[8]{0:T(128)S(1)}, s32[8]{0:T(128)}, u32[]{:S(2)}) copy-start(s32[8]{0:T(128)} %refs_4_.1) | copy-start | bytes 100
  0.0 56.3 %copy-start.2 = (f32[1,32,4096]{2,1,0:T(8,128)S(1)}, f32[1,32,4096]{2,1,0:T(8,128)}, u32[]{:S(2)}) copy-start(f32[1,32,4096]{2,1,0:T(8,128)} %param.16) | copy-start | bytes 1572868
  0.0 56.3 %copy-start.6 = (f32[4096]{0:T(1024)S(1)}, f32[4096]{0:T(1024)}, u32[]{:S(2)}) copy-start(f32[4096]{0:T(1024)} %param.29) | copy-start | bytes 49156
  8.2 5.7 %collective-permute-start = (f32[8,2432]{1,0:T(8,128)}, f32[8,2432]{1,0:T(8,128)S(1)}, u32[]{:S(2)}, u32[]{:S(2)}) collective-permute-start(f32[8,2432]{1,0:T(8,128)} %get-tuple-element.17), channel_id=1, source_target_pairs={{0,4},{4,0},{8,12},{12,8},{1,5},{5,1},{9,13},{13,9},{2,6},{6,2},{1... | collective-permute-start | bytes 233480 | tf_op jit(solution)/shard_map/ppermute | solution.py:36
  11.3 8.3 %collective-permute-start.1 = (f32[8,2432]{1,0:T(8,128)}, f32[8,2432]{1,0:T(8,128)S(1)}, u32[]{:S(2)}, u32[]{:S(2)}) collective-permute-start(f32[8,2432]{1,0:T(8,128)} %get-tuple-element.18), channel_id=1, source_target_pairs={{0,8},{4,12},{8,0},{12,4},{1,9},{5,13},{9,1},{13,5},{2,10},{6,14},... | collective-permute-start | bytes 233480 | tf_op jit(solution)/shard_map/ppermute | solution.py:36
  13.9 6.5 %collective-permute-start.2 = (f32[8,2432]{1,0:T(8,128)}, f32[8,2432]{1,0:T(8,128)S(1)}, u32[]{:S(2)}, u32[]{:S(2)}) collective-permute-start(f32[8,2432]{1,0:T(8,128)} %get-tuple-element.19), channel_id=1, source_target_pairs={{0,12},{4,8},{8,4},{12,0},{1,13},{5,9},{9,5},{13,1},{2,14},{6,10},... | collective-permute-start | bytes 233480 | tf_op jit(solution)/shard_map/ppermute | solution.py:36
  20.4 0.9 %copy-start.3 = (f32[8,2432]{1,0:T(8,128)S(1)}, f32[8,2432]{1,0:T(8,128)}, u32[]{:S(2)}) copy-start(f32[8,2432]{1,0:T(8,128)} %get-tuple-element.16.refs_0_) | copy-start | bytes 233476
  21.4 7.2 %collective-permute-start.3 = (bf16[8,2304]{1,0:T(8,128)(2,1)S(1)}, bf16[8,2304]{1,0:T(8,128)(2,1)S(1)}, u32[]{:S(2)}, u32[]{:S(2)}) collective-permute-start(bf16[8,2304]{1,0:T(8,128)(2,1)S(1)} %norm.1), channel_id=1, source_target_pairs={{0,0},{1,4},{2,8},{3,12},{4,1},{5,5},{6,9},{7,13},{8,2},{9,6},{10,... | collective-permute-start | bytes 110600 | tf_op jit(solution)/shard_map/ppermute | solution.py:41
  22.1 6.5 %collective-permute-start.4 = (bf16[8,2304]{1,0:T(8,128)(2,1)S(1)}, bf16[8,2304]{1,0:T(8,128)(2,1)S(1)}, u32[]{:S(2)}, u32[]{:S(2)}) collective-permute-start(bf16[8,2304]{1,0:T(8,128)(2,1)S(1)} %norm.1), channel_id=1, source_target_pairs={{0,4},{1,0},{2,12},{3,8},{4,5},{5,1},{6,13},{7,9},{8,6},{9,2},{10,... | collective-permute-start | bytes 110600 | tf_op jit(solution)/shard_map/ppermute | solution.py:41
  24.8 5.3 %collective-permute-start.5 = (bf16[8,2304]{1,0:T(8,128)(2,1)S(1)}, bf16[8,2304]{1,0:T(8,128)(2,1)S(1)}, u32[]{:S(2)}, u32[]{:S(2)}) collective-permute-start(bf16[8,2304]{1,0:T(8,128)(2,1)S(1)} %norm.1), channel_id=1, source_target_pairs={{0,8},{1,12},{2,0},{3,4},{4,9},{5,13},{6,1},{7,5},{8,10},{9,14},{1... | collective-permute-start | bytes 110600 | tf_op jit(solution)/shard_map/ppermute | solution.py:41
  27.3 3.4 %collective-permute-start.6 = (bf16[8,2304]{1,0:T(8,128)(2,1)S(1)}, bf16[8,2304]{1,0:T(8,128)(2,1)S(1)}, u32[]{:S(2)}, u32[]{:S(2)}) collective-permute-start(bf16[8,2304]{1,0:T(8,128)(2,1)S(1)} %norm.1), channel_id=1, source_target_pairs={{0,12},{1,8},{2,4},{3,0},{4,13},{5,9},{6,5},{7,1},{8,14},{9,10},{1... | collective-permute-start | bytes 110600 | tf_op jit(solution)/shard_map/ppermute | solution.py:41
  34.8 37.0 %copy-start.10 = (bf16[32,4096]{1,0:T(8,128)(2,1)S(1)}, bf16[32,4096]{1,0:T(8,128)(2,1)}, u32[]{:S(2)}) copy-start(bf16[32,4096]{1,0:T(8,128)(2,1)} %residual.1) | copy-start | bytes 786436
  34.8 6.7 %collective-permute-start.7 = (f32[136,128]{1,0:T(8,128)S(1)}, f32[136,128]{1,0:T(8,128)S(1)}, u32[]{:S(2)}, u32[]{:S(2)}) collective-permute-start(f32[136,128]{1,0:T(8,128)S(1)} %get-tuple-element.21), channel_id=1, source_target_pairs={{0,4},{4,0},{8,12},{12,8},{1,5},{5,1},{9,13},{13,9},{2,6},{6,2},{1... | collective-permute-start | bytes 208904 | tf_op jit(solution)/shard_map/ppermute | solution.py:36
  38.9 7.8 %collective-permute-start.8 = (f32[136,128]{1,0:T(8,128)S(1)}, f32[136,128]{1,0:T(8,128)S(1)}, u32[]{:S(2)}, u32[]{:S(2)}) collective-permute-start(f32[136,128]{1,0:T(8,128)S(1)} %get-tuple-element.22), channel_id=1, source_target_pairs={{0,8},{4,12},{8,0},{12,4},{1,9},{5,13},{9,1},{13,5},{2,10},{6,14},... | collective-permute-start | bytes 208904 | tf_op jit(solution)/shard_map/ppermute | solution.py:36
  39.2 7.5 %collective-permute-start.9 = (f32[136,128]{1,0:T(8,128)S(1)}, f32[136,128]{1,0:T(8,128)S(1)}, u32[]{:S(2)}, u32[]{:S(2)}) collective-permute-start(f32[136,128]{1,0:T(8,128)S(1)} %get-tuple-element.23), channel_id=1, source_target_pairs={{0,12},{4,8},{8,4},{12,0},{1,13},{5,9},{9,5},{13,1},{2,14},{6,10},... | collective-permute-start | bytes 208904 | tf_op jit(solution)/shard_map/ppermute | solution.py:36
  47.0 6.1 %collective-permute-start.10 = (bf16[8,2048]{1,0:T(8,128)(2,1)S(1)}, bf16[8,2048]{1,0:T(8,128)(2,1)S(1)}, u32[]{:S(2)}, u32[]{:S(2)}) collective-permute-start(bf16[8,2048]{1,0:T(8,128)(2,1)S(1)} %merge.1), channel_id=1, source_target_pairs={{0,0},{1,4},{2,8},{3,12},{4,1},{5,5},{6,9},{7,13},{8,2},{9,6},{10,... | collective-permute-start | bytes 98312 | tf_op jit(solution)/shard_map/ppermute | solution.py:41
  47.6 5.4 %collective-permute-start.11 = (bf16[8,2048]{1,0:T(8,128)(2,1)S(1)}, bf16[8,2048]{1,0:T(8,128)(2,1)S(1)}, u32[]{:S(2)}, u32[]{:S(2)}) collective-permute-start(bf16[8,2048]{1,0:T(8,128)(2,1)S(1)} %merge.1), channel_id=1, source_target_pairs={{0,4},{1,0},{2,12},{3,8},{4,5},{5,1},{6,13},{7,9},{8,6},{9,2},{10,... | collective-permute-start | bytes 98312 | tf_op jit(solution)/shard_map/ppermute | solution.py:41
  50.3 4.4 %collective-permute-start.12 = (bf16[8,2048]{1,0:T(8,128)(2,1)S(1)}, bf16[8,2048]{1,0:T(8,128)(2,1)S(1)}, u32[]{:S(2)}, u32[]{:S(2)}) collective-permute-start(bf16[8,2048]{1,0:T(8,128)(2,1)S(1)} %merge.1), channel_id=1, source_target_pairs={{0,8},{1,12},{2,0},{3,4},{4,9},{5,13},{6,1},{7,5},{8,10},{9,14},{1... | collective-permute-start | bytes 98312 | tf_op jit(solution)/shard_map/ppermute | solution.py:41
  53.0 3.3 %collective-permute-start.13 = (bf16[8,2048]{1,0:T(8,128)(2,1)S(1)}, bf16[8,2048]{1,0:T(8,128)(2,1)S(1)}, u32[]{:S(2)}, u32[]{:S(2)}) collective-permute-start(bf16[8,2048]{1,0:T(8,128)(2,1)S(1)} %merge.1), channel_id=1, source_target_pairs={{0,12},{1,8},{2,4},{3,0},{4,13},{5,9},{6,5},{7,1},{8,14},{9,10},{1... | collective-permute-start | bytes 98312 | tf_op jit(solution)/shard_map/ppermute | solution.py:41
  60.4 1.8 %collective-permute-start.14 = (f32[16,4096]{1,0:T(8,128)S(1)}, f32[16,4096]{1,0:T(8,128)S(1)}, u32[]{:S(2)}, u32[]{:S(2)}) collective-permute-start(f32[16,4096]{1,0:T(8,128)S(1)} %get-tuple-element.26), channel_id=1, source_target_pairs={{0,1},{1,0},{2,3},{3,2},{4,5},{5,4},{6,7},{7,6},{8,9},{9,8},{10,11... | collective-permute-start | bytes 786440 | tf_op jit(solution)/shard_map/ppermute | solution.py:47
  62.3 9.5 %collective-permute-start.15 = (f32[16,4096]{1,0:T(8,128)S(1)}, f32[16,4096]{1,0:T(8,128)S(1)}, u32[]{:S(2)}, u32[]{:S(2)}) collective-permute-start(f32[16,4096]{1,0:T(8,128)S(1)} %add.13), channel_id=1, source_target_pairs={{0,2},{1,3},{2,0},{3,1},{4,6},{5,7},{6,4},{7,5},{8,10},{9,11},{10,... | collective-permute-start | bytes 786440 | tf_op jit(solution)/shard_map/ppermute | solution.py:47
  71.9 1.4 %collective-permute-start.16 = (bf16[16,4096]{1,0:T(8,128)(2,1)S(1)}, bf16[16,4096]{1,0:T(8,128)(2,1)S(1)}, u32[]{:S(2)}, u32[]{:S(2)}) collective-permute-start(bf16[16,4096]{1,0:T(8,128)(2,1)S(1)} %add_convert_fusion), channel_id=1, source_target_pairs={{0,1},{1,0},{2,3},{3,2},{4,5},{5,4},{6,7},{7,6},{8,9},{9,8},{10,11... | collective-permute-start | bytes 393224 | tf_op jit(solution)/shard_map/ppermute | solution.py:47

commit v5 on v4

--- a/solution.py
+++ b/solution.py
@@ -15,6 +15,7 @@
 EPSILON = 1e-05
 NEGATIVE = -1e30
 LANES = 128
+SHRINK = 32.0
 f32 = jnp.float32
 bf16 = jnp.bfloat16
 VMEM = pl.BlockSpec(memory_space=pltpu.VMEM)
@@ -36,11 +37,22 @@
     return [chunks[0]] + [lax.ppermute(chunks[k], axis, partners(n, k)) for k in range(1, n)]
 
 
+def place(placed, pieces, n):
+    me = lax.axis_index("gx")
+    for k in range(n):
+        placed[me ^ k] = pieces[k][...].astype(f32)
+
+    @pl.when(me == lax.axis_index("gy"))
+    def _():
+        placed[me] = pieces[n][...].astype(f32)
+
+
 def spread(value, n):
-    return [
-        lax.ppermute(value, ("gx", "gy"), [(a * n + b, (b ^ k) * n + a) for a in range(n) for b in range(n)])
-        for k in range(n)
-    ]
+    pieces = []
+    for k in range(n):
+        pairs = [(a * n + b, (b ^ k) * n + a) for a in range(n) for b in range(n)]
+        pieces.append(lax.ppermute(value, ("gx", "gy"), [pair for pair in pairs if pair[0] != pair[1]]))
+    return pieces + [value]
 
 
 def swap(value, axis, n, offset):
@@ -153,21 +165,38 @@
     )(query_scale.reshape(-1, LANES), keyval_scale.reshape(-1, LANES), *parts)
 
 
+def fetch_kernel(n, *refs):
+    sources, targets, sems = refs[1 : n + 1], refs[n + 1 : 2 * n + 1], refs[-1]
+    copies = [pltpu.make_async_copy(a, b, sems.at[i]) for i, (a, b) in enumerate(zip(sources, targets))]
+    for copy in copies:
+        copy.start()
+    for copy in copies:
+        copy.wait()
+
+
+def fetch(after, *arrays):
+    n = len(arrays)
+    size = sum(array.size * array.dtype.itemsize for array in arrays)
+    return pl.pallas_call(
+        functools.partial(fetch_kernel, n),
+        in_specs=[ANY] + [HBM] * n,
+        out_specs=[VMEM] * n,
+        out_shape=[jax.ShapeDtypeStruct(array.shape, array.dtype) for array in arrays],
+        scratch_shapes=[pltpu.SemaphoreType.DMA((n,))],
+        compiler_params=params(24),
+        cost_estimate=pl.CostEstimate(flops=0, bytes_accessed=2 * size, transcendentals=0),
+        name="fetch",
+    )(after, *arrays)
+
+
 def attend_kernel(n, *refs):
-    pieces = refs[:n]
-    lengths, keys, values, key_scale, value_scale, w_out = refs[n : n + 6]
-    outs, w_head = refs[n + 6 : 2 * n + 6], refs[2 * n + 6]
-    placed, k_buf, v_buf, q_rows, logits, messages, fresh, sems = refs[2 * n + 7 :]
-    requests, _, local, _ = k_buf.shape
-    load_keys = pltpu.make_async_copy(keys, k_buf, sems.at[0])
-    load_values = pltpu.make_async_copy(values, v_buf, sems.at[1])
-    load_weights = pltpu.make_async_copy(w_out.at[pl.ds(0, w_head.shape[0])], w_head, sems.at[2])
-    load_keys.start()
-    load_values.start()
-    load_weights.start(priority=1)
+    pieces, refs = refs[: n + 1], refs[n + 1 :]
+    lengths, keys, values, key_scale, value_scale = refs[:5]
+    outs = refs[5 : n + 5]
+    placed, q_rows, logits, messages, fresh = refs[n + 5 :]
+    requests, _, local, _ = keys.shape
     me = lax.axis_index("gx")
-    for k in range(n):
-        placed[me ^ k] = pieces[k][...].astype(f32)
+    place(placed, pieces, n)
     queries = HEADS * HEAD_DIM // n
     per = queries // LANES
     for h in range(HEADS):
@@ -178,14 +207,12 @@
         start = queries + c % share * LANES
         fresh[pl.ds(c, requests, stride=2 * KV_HEADS), :] = placed[c // share, :, start : start + LANES]
     multiplier = HEAD_DIM ** (-0.5)
-    load_keys.wait()
     for r in range(requests):
         for g in range(KV_HEADS):
             at = slice(r * HEADS + g * GROUP, r * HEADS + (g + 1) * GROUP)
             logits[at, :] = lax.dot_general(
-                q_rows[at, :].astype(bf16), k_buf[r, g], (((1,), (1,)), ((), ())), preferred_element_type=f32
+                q_rows[at, :].astype(bf16), keys[r, g], (((1,), (1,)), ((), ())), preferred_element_type=f32
             )
-    load_values.wait()
     position = lax.broadcasted_iota(jnp.int32, (GROUP, local), 1) + me * local
     first = me == 0
     count = requests * GROUP
@@ -208,7 +235,7 @@
             totals[g].append(jnp.sum(weights, axis=1, keepdims=True) + own_weight)
             tops[g].append(top)
             scaled = (weights * value_scale[scale_at : scale_at + 1, :]).astype(bf16)
-            mixed = jnp.dot(scaled, v_buf[r, g], preferred_element_type=f32) + own_weight * new_value
+            mixed = jnp.dot(scaled, values[r, g], preferred_element_type=f32) + own_weight * new_value
             messages[g, r * GROUP : (r + 1) * GROUP, :] = mixed
     diagonal = lax.broadcasted_iota(jnp.int32, (LANES, LANES), 0) == lax.broadcasted_iota(jnp.int32, (LANES, LANES), 1)
     wide = LANES // GROUP
@@ -222,32 +249,27 @@
         messages[p, count:, :] = jnp.concatenate(rows + [jnp.zeros((spare, LANES), f32)], axis=0)
     for k in range(n):
         outs[k][...] = messages[me ^ k]
-    load_weights.wait()
-
-
-def attend(n, pieces, lengths, keys, values, key_scale, value_scale, w_out):
+
+
+def attend(n, pieces, lengths, keys, values, key_scale, value_scale):
     requests, _, local, _ = keys.shape
     count = requests * GROUP
     height = count + -(-2 * count // LANES // 8) * 8
     return pl.pallas_call(
         functools.partial(attend_kernel, n),
-        in_specs=[VMEM] * n + [SMEM, HBM, HBM, VMEM, VMEM, HBM],
-        out_specs=[VMEM] * (n + 1),
-        out_shape=[jax.ShapeDtypeStruct((height, LANES), f32)] * n
-        + [jax.ShapeDtypeStruct((w_out.shape[0] // 2, w_out.shape[1]), bf16)],
+        in_specs=[VMEM] * (n + 1) + [SMEM, VMEM, VMEM, VMEM, VMEM],
+        out_specs=[VMEM] * n,
+        out_shape=[jax.ShapeDtypeStruct((height, LANES), f32)] * n,
         scratch_shapes=[
             pltpu.VMEM((n,) + pieces[0].shape, f32),
-            pltpu.VMEM(keys.shape, bf16),
-            pltpu.VMEM(values.shape, bf16),
             pltpu.VMEM((requests * HEADS, HEAD_DIM), f32),
             pltpu.VMEM((requests * HEADS, local), f32),
             pltpu.VMEM((n, height, LANES), f32),
             pltpu.VMEM((requests * 2 * KV_HEADS, HEAD_DIM), f32),
-            pltpu.SemaphoreType.DMA((3,)),
         ],
-        compiler_params=params(30),
+        compiler_params=params(24),
         name="attend",
-    )(*pieces, lengths, keys, values, key_scale.reshape(-1, local), value_scale.reshape(-1, local), w_out)
+    )(*pieces, lengths, keys, values, key_scale.reshape(-1, local), value_scale.reshape(-1, local))
 
 
 def merge_kernel(*refs):
@@ -292,58 +314,36 @@
 
 
 def output_kernel(n, *refs):
-    pieces = refs[:n]
-    w_head, w_out, out_scale, ffn, kept, given, w_buf, ffn_buf, total, placed, sems = refs[n:]
-    rest, width = w_buf.shape
-    steps = sems.shape[0] - 1
-    depth, head = rest // steps, w_head.shape[0]
-    copies = []
-    for i in range(steps):
-        part = pl.ds(i * depth, depth)
-        source = w_out.at[pl.ds(head + i * depth, depth)]
-        copies.append(pltpu.make_async_copy(source, w_buf.at[part], sems.at[i]))
-        copies[-1].start(priority=1)
-    load = pltpu.make_async_copy(ffn, ffn_buf, sems.at[steps])
-    load.start()
-    me = lax.axis_index("gx")
-    for k in range(n):
-        placed[me ^ k] = pieces[k][...].astype(f32)
-    attended = placed[...].reshape(total.shape[0], head + rest).astype(bf16)
-    total[...] = jnp.dot(attended[:, :head], w_head[...], preferred_element_type=f32)
-    for i in range(steps):
-        part = slice(i * depth, (i + 1) * depth)
-        copies[i].wait()
-        total[...] += jnp.dot(attended[:, head:][:, part], w_buf[part, :], preferred_element_type=f32)
-    load.wait()
+    pieces = refs[: n + 1]
+    w_out, out_scale, ffn, kept, given, total, placed = refs[n + 1 :]
+    width = w_out.shape[1]
+    place(placed, pieces, n)
+    attended = placed[...].reshape(total.shape[0], w_out.shape[0]).astype(bf16)
+    span = width // 4
+    for i in range(4):
+        part = slice(i * span, (i + 1) * span)
+        total[:, part] = jnp.dot(attended, w_out[:, part], preferred_element_type=f32)
     for t in range(width // LANES):
         lanes = slice(t * LANES, (t + 1) * LANES)
-        total[:, lanes] = total[:, lanes] * out_scale[t : t + 1, :] + ffn_buf[:, lanes]
+        total[:, lanes] = total[:, lanes] * out_scale[t : t + 1, :] + ffn[:, lanes]
     rows = total.shape[0] // 2
     core = lax.axis_index("gy") & 1
     kept[...] = total[pl.ds(pl.multiple_of(core * rows, rows), rows), :]
     given[...] = total[pl.ds(pl.multiple_of((1 - core) * rows, rows), rows), :]
 
 
-def output(pieces, w_head, w_out, out_scale, ffn):
-    n = len(pieces)
-    rows = ffn.shape[0]
-    width = w_out.shape[1]
-    steps = 4
+def output(pieces, w_out, out_scale, ffn):
+    n = len(pieces) - 1
+    rows, width = ffn.shape
     return pl.pallas_call(
         functools.partial(output_kernel, n),
-        in_specs=[VMEM] * (n + 1) + [HBM, VMEM, HBM],
+        in_specs=[VMEM] * (n + 4),
         out_specs=[VMEM] * 2,
         out_shape=[jax.ShapeDtypeStruct((rows // 2, width), f32)] * 2,
-        scratch_shapes=[
-            pltpu.VMEM((w_out.shape[0] - w_head.shape[0], width), bf16),
-            pltpu.VMEM((rows, width), f32),
-            pltpu.VMEM((rows, width), f32),
-            pltpu.VMEM((n,) + pieces[0].shape, f32),
-            pltpu.SemaphoreType.DMA((steps + 1,)),
-        ],
-        compiler_params=params(30),
+        scratch_shapes=[pltpu.VMEM((rows, width), f32), pltpu.VMEM((n,) + pieces[0].shape, f32)],
+        compiler_params=params(20),
         name="output",
-    )(*pieces, w_head, w_out, out_scale.reshape(-1, LANES), ffn)
+    )(*pieces, w_out, out_scale.reshape(-1, LANES), ffn)
 
 
 def body(n_gx, n_gy, residual, ffn_partial, norm_gain, smooth_scale, w_query, query_scale, w_keyval, keyval_scale,
@@ -352,13 +352,17 @@
     rows = residual.shape[0]
     requests = rows // n_gy
     parts = project(n_gx, residual, norm_gain, smooth_scale, w_query, w_keyval)
-    pieces = spread(norm(trade(parts, "gx", n_gx), query_scale, keyval_scale), n_gx)
-    *parts, w_head = attend(n_gx, pieces, lengths, key_cache, value_cache, key_scale, value_scale, w_out)
+    (w_near,) = fetch(parts[0], w_out)
+    total = trade(parts, "gx", n_gx)
+    total[0], w_near = lax.optimization_barrier((total[0], w_near))
+    pieces = spread(norm(total, query_scale, keyval_scale), n_gx)
+    parts = attend(n_gx, pieces, lengths, key_cache, value_cache, key_scale, value_scale)
     pieces = spread(merge(trade(parts, "gx", n_gx), requests), n_gx)
-    kept, given = output(pieces, w_head, w_out, out_scale, ffn_partial[0])
+    kept, given = output(pieces, w_near, out_scale, ffn_partial[0])
     core = gy & 1
     chip = kept + swap(given, "gy", n_gy, 1)
-    whole = chip + swap(chip, "gy", n_gy, 2)
+    other = swap((chip * (1 / SHRINK)).astype(jnp.float16), "gy", n_gy, 2)
+    whole = chip + other.astype(f32) * SHRINK
     mine = lax.dynamic_slice_in_dim(residual, core * (rows // 2), rows // 2, 0)
     mine = (mine.astype(f32) + whole).astype(bf16)
     return jnp.concatenate(ordered([mine, swap(mine, "gy", n_gy, 1)], core))

time: 74.2 us -> 68.5 us (0.923)
  waiting for transfers between devices: 26.6 us -> 17.9 us
  Pallas kernels: 16.6 us -> 19.3 us
    ppermute x6, waiting for transfers between devices: 11.9 us -> 6.5 us  [trade(): lax.ppermute(chunks[k], axis, partners(n, k))]
    pallas_call x1 -> x2, Pallas kernels: 4.09 us -> 7.93 us  [the longest x1 5.93 us: fetch(): pl.pallas_call(functools.partial(fetch_kernel, n), in_specs=[ANY] + [HBM]...]
    ppermute x3, waiting for transfers between devices: 9.32 us -> 6.51 us  [swap(): return lax.ppermute(value, axis, partners(n, offset))]
    ppermute x8, starting transfers between devices: 13.2 us -> 15.1 us  [spread(): lax.ppermute(value, ('gx', 'gy'), [pair for pair in pairs if pair[0] != p...]
    ppermute x6, starting transfers between devices: 12.3 us -> 10.9 us  [trade(): lax.ppermute(chunks[k], axis, partners(n, k))]
    pallas_call x1, Pallas kernels: 4.08 us -> 3.05 us  [output(): pl.pallas_call(functools.partial(output_kernel, n), in_specs=[VMEM] * (n...]
  transfers between devices with their start and end apart: 17 -> 17, of which waited for: 11 -> 8; matrix products, arithmetic and copies ran while one was open for 0% -> 0% of each run, Pallas kernels for 0% -> 9%
where the time goes in v5:
time: 68.5 us; the launch traced here: 68.3 us
  starting transfers between devices  29.2 us (43%)
  Pallas kernels  19.3 us (28%)
  waiting for transfers between devices  17.9 us (26%)
  local copies, waits for them, and re-layouts  0.94 us (1%)
  other arithmetic  0.83 us (1%)
    ppermute x8, starting transfers between devices, spread(): lax.ppermute(value, ('gx', 'gy'), [pair for pair in pairs if pair[0] != p...  15.1 us
    ppermute x6, starting transfers between devices, trade(): lax.ppermute(chunks[k], axis, partners(n, k))  10.9 us
    pallas_call x1, Pallas kernels, project(): pl.pallas_call(functools.partial(project_kernel, n), in_specs=[HBM] * 5,...  7.99 us
    ppermute x3, waiting for transfers between devices, swap(): return lax.ppermute(value, axis, partners(n, offset))  6.51 us
    ppermute x6, waiting for transfers between devices, trade(): lax.ppermute(chunks[k], axis, partners(n, k))  6.5 us
    pallas_call x1, Pallas kernels, fetch(): pl.pallas_call(functools.partial(fetch_kernel, n), in_specs=[ANY] + [HBM]...  5.93 us
    ppermute x8, waiting for transfers between devices, spread(): lax.ppermute(value, ('gx', 'gy'), [pair for pair in pairs if pair[0] != p...  4.91 us
    ppermute x3, starting transfers between devices, swap(): return lax.ppermute(value, axis, partners(n, offset))  3.14 us
  transfers between devices with their start and end apart: 17, of which 8 were waited for; matrix products, arithmetic and copies ran while one was open for 0% of the time, Pallas kernels for 9%

profile of v5, /device:TPU:0, one launch (start us, length us, event | category | flops | bytes accessed | tf_op | source)
XLA Modules:
  0.0 68.3 jit_solution(11339409541752333407)
XLA Ops:
  0.0 8.0 %project.1 = (f32[8,2432]{1,0:T(8,128)}, f32[8,2432]{1,0:T(8,128)}, f32[8,2432]{1,0:T(8,128)}, f32[8,2432]{1,0:T(8,128)}) custom-call(bf16[32,4096]{1,0:T(8,128)(2,1)} %residual.1, f32[32,128]{1,0:T(8,128)} %bitcast.14, f32[32,128]{1,0:T(8,128)} %bitcast.15, bf16[4096,2048]{1,0:T(8,128)(2,1)} %w_query.1, bf16[4096,256]{1,0:T(8,128)(2,1)} %w_keyval.1), custom_call_target="tpu_custom_call" | custom-call | tf_op jit(solution)/shard_map/project/pallas_call | solution.py:119
  8.0 3.1 %collective-permute-start = (f32[8,2432]{1,0:T(8,128)}, f32[8,2432]{1,0:T(8,128)S(1)}, u32[]{:S(2)}, u32[]{:S(2)}) collective-permute-start(f32[8,2432]{1,0:T(8,128)} %get-tuple-element.19), channel_id=1, source_target_pairs={{0,4},{4,0},{8,12},{12,8},{1,5},{5,1},{9,13},{13,9},{2,6},{6,2},{1... | collective-permute-start | bytes 233480 | tf_op jit(solution)/shard_map/ppermute | solution.py:37
  11.1 2.6 %collective-permute-start.1 = (f32[8,2432]{1,0:T(8,128)}, f32[8,2432]{1,0:T(8,128)S(1)}, u32[]{:S(2)}, u32[]{:S(2)}) collective-permute-start(f32[8,2432]{1,0:T(8,128)} %get-tuple-element.20), channel_id=1, source_target_pairs={{0,8},{4,12},{8,0},{12,4},{1,9},{5,13},{9,1},{13,5},{2,10},{6,14},... | collective-permute-start | bytes 233480 | tf_op jit(solution)/shard_map/ppermute | solution.py:37
  13.7 0.9 %copy-done.3 = f32[8,2432]{1,0:T(8,128)S(1)} copy-done((f32[8,2432]{1,0:T(8,128)S(1)}, f32[8,2432]{1,0:T(8,128)}, u32[]{:S(2)}) %copy-start.3) | copy-done | bytes 77848
  14.6 5.9 %fetch.1.refs_5_ = bf16[2048,4096]{1,0:T(8,128)(2,1)S(1)} custom-call(f32[8,2432]{1,0:T(8,128)S(1)} %copy-done.3, bf16[2048,4096]{1,0:T(8,128)(2,1)} %refs_1_.1), custom_call_target="tpu_custom_call" | custom-call | bytes 33554432 | tf_op jit(solution)/shard_map/fetch/pallas_call | solution.py:180
  20.6 0.1 norm.1.refs_4_
  20.7 0.7 collective-permute-start.3
  21.4 2.3 %collective-permute-start.4 = (bf16[8,2304]{1,0:T(8,128)(2,1)S(1)}, bf16[8,2304]{1,0:T(8,128)(2,1)S(1)}, u32[]{:S(2)}, u32[]{:S(2)}) collective-permute-start(bf16[8,2304]{1,0:T(8,128)(2,1)S(1)} %norm.1.refs_4_), channel_id=1, source_target_pairs={{0,4},{1,0},{2,12},{3,8},{4,5},{5,1},{6,13},{7,9},{8,6},{9,2},{10,... | collective-permute-start | bytes 110600 | tf_op jit(solution)/shard_map/ppermute | solution.py:54
  23.7 3.2 %collective-permute-start.5 = (bf16[8,2304]{1,0:T(8,128)(2,1)S(1)}, bf16[8,2304]{1,0:T(8,128)(2,1)S(1)}, u32[]{:S(2)}, u32[]{:S(2)}) collective-permute-start(bf16[8,2304]{1,0:T(8,128)(2,1)S(1)} %norm.1.refs_4_), channel_id=1, source_target_pairs={{0,8},{1,12},{2,0},{3,4},{4,9},{5,13},{6,1},{7,5},{8,10},{9,14},{1... | collective-permute-start | bytes 110600 | tf_op jit(solution)/shard_map/ppermute | solution.py:54
  26.8 2.4 %collective-permute-start.6 = (bf16[8,2304]{1,0:T(8,128)(2,1)S(1)}, bf16[8,2304]{1,0:T(8,128)(2,1)S(1)}, u32[]{:S(2)}, u32[]{:S(2)}) collective-permute-start(bf16[8,2304]{1,0:T(8,128)(2,1)S(1)} %norm.1.refs_4_), channel_id=1, source_target_pairs={{0,12},{1,8},{2,4},{3,0},{4,13},{5,9},{6,5},{7,1},{8,14},{9,10},{1... | collective-permute-start | bytes 110600 | tf_op jit(solution)/shard_map/ppermute | solution.py:54
  29.3 0.8 %collective-permute-done.5.refs_2_ = bf16[8,2304]{1,0:T(8,128)(2,1)S(1)} collective-permute-done((bf16[8,2304]{1,0:T(8,128)(2,1)S(1)}, bf16[8,2304]{1,0:T(8,128)(2,1)S(1)}, u32[]{:S(2)}, u32[]{:S(2)}) %collective-permute-start.5) | collective-permute-done | bytes 36896 | tf_op jit(solution)/shard_map/ppermute | solution.py:54
  30.0 0.9 %collective-permute-done.6.refs_3_ = bf16[8,2304]{1,0:T(8,128)(2,1)S(1)} collective-permute-done((bf16[8,2304]{1,0:T(8,128)(2,1)S(1)}, bf16[8,2304]{1,0:T(8,128)(2,1)S(1)}, u32[]{:S(2)}, u32[]{:S(2)}) %collective-permute-start.6) | collective-permute-done | bytes 36896 | tf_op jit(solution)/shard_map/ppermute | solution.py:54
  30.9 2.0 %attend.1 = (f32[136,128]{1,0:T(8,128)S(1)}, f32[136,128]{1,0:T(8,128)S(1)}, f32[136,128]{1,0:T(8,128)S(1)}, f32[136,128]{1,0:T(8,128)S(1)}) custom-call(bf16[8,2304]{1,0:T(8,128)(2,1)S(1)} %collective-permute-done.3.refs_0_, bf16[8,2304]{1,0:T(8,128)(2,1)S(1)} %collective-permute-done.4.refs_1_, bf16[8,2304]{1,0:T(8,128)(2,1)S(1)} %collective-permute-done.5.refs_2_, ...), custom_call_target="tpu_custom_call" | custom-call | tf_op jit(solution)/shard_map/attend/pallas_call | solution.py:258
  32.9 2.8 %collective-permute-start.7 = (f32[136,128]{1,0:T(8,128)S(1)}, f32[136,128]{1,0:T(8,128)S(1)}, u32[]{:S(2)}, u32[]{:S(2)}) collective-permute-start(f32[136,128]{1,0:T(8,128)S(1)} %get-tuple-element.23), channel_id=1, source_target_pairs={{0,4},{4,0},{8,12},{12,8},{1,5},{5,1},{9,13},{13,9},{2,6},{6,2},{1... | collective-permute-start | bytes 208904 | tf_op jit(solution)/shard_map/ppermute | solution.py:37
  35.7 2.1 %collective-permute-start.8 = (f32[136,128]{1,0:T(8,128)S(1)}, f32[136,128]{1,0:T(8,128)S(1)}, u32[]{:S(2)}, u32[]{:S(2)}) collective-permute-start(f32[136,128]{1,0:T(8,128)S(1)} %get-tuple-element.24), channel_id=1, source_target_pairs={{0,8},{4,12},{8,0},{12,4},{1,9},{5,13},{9,1},{13,5},{2,10},{6,14},... | collective-permute-start | bytes 208904 | tf_op jit(solution)/shard_map/ppermute | solution.py:37
  37.8 0.3 collective-permute-start.9
  38.2 6.5 %collective-permute-done.8.refs_2_ = f32[136,128]{1,0:T(8,128)S(1)} collective-permute-done((f32[136,128]{1,0:T(8,128)S(1)}, f32[136,128]{1,0:T(8,128)S(1)}, u32[]{:S(2)}, u32[]{:S(2)}) %collective-permute-start.8) | collective-permute-done | bytes 69664 | tf_op jit(solution)/shard_map/ppermute | solution.py:37
  44.7 0.2 merge.1.refs_4_
  44.9 0.7 collective-permute-start.10
  45.5 3.3 %collective-permute-start.11 = (bf16[8,2048]{1,0:T(8,128)(2,1)S(1)}, bf16[8,2048]{1,0:T(8,128)(2,1)S(1)}, u32[]{:S(2)}, u32[]{:S(2)}) collective-permute-start(bf16[8,2048]{1,0:T(8,128)(2,1)S(1)} %merge.1.refs_4_), channel_id=1, source_target_pairs={{0,4},{1,0},{2,12},{3,8},{4,5},{5,1},{6,13},{7,9},{8,6},{9,2},{10,... | collective-permute-start | bytes 98312 | tf_op jit(solution)/shard_map/ppermute | solution.py:54
  48.8 2.6 %collective-permute-start.12 = (bf16[8,2048]{1,0:T(8,128)(2,1)S(1)}, bf16[8,2048]{1,0:T(8,128)(2,1)S(1)}, u32[]{:S(2)}, u32[]{:S(2)}) collective-permute-start(bf16[8,2048]{1,0:T(8,128)(2,1)S(1)} %merge.1.refs_4_), channel_id=1, source_target_pairs={{0,8},{1,12},{2,0},{3,4},{4,9},{5,13},{6,1},{7,5},{8,10},{9,14},{1... | collective-permute-start | bytes 98312 | tf_op jit(solution)/shard_map/ppermute | solution.py:54
  51.4 0.1 collective-permute-start.13
  51.5 1.5 %collective-permute-done.12.refs_2_ = bf16[8,2048]{1,0:T(8,128)(2,1)S(1)} collective-permute-done((bf16[8,2048]{1,0:T(8,128)(2,1)S(1)}, bf16[8,2048]{1,0:T(8,128)(2,1)S(1)}, u32[]{:S(2)}, u32[]{:S(2)}) %collective-permute-start.12) | collective-permute-done | bytes 32800 | tf_op jit(solution)/shard_map/ppermute | solution.py:54
  53.0 1.7 %collective-permute-done.13.refs_3_ = bf16[8,2048]{1,0:T(8,128)(2,1)S(1)} collective-permute-done((bf16[8,2048]{1,0:T(8,128)(2,1)S(1)}, bf16[8,2048]{1,0:T(8,128)(2,1)S(1)}, u32[]{:S(2)}, u32[]{:S(2)}) %collective-permute-start.13) | collective-permute-done | bytes 32800 | tf_op jit(solution)/shard_map/ppermute | solution.py:54
  54.7 3.0 %output.1 = (f32[16,4096]{1,0:T(8,128)S(1)}, f32[16,4096]{1,0:T(8,128)S(1)}) custom-call(bf16[8,2048]{1,0:T(8,128)(2,1)S(1)} %collective-permute-done.10.refs_0_, bf16[8,2048]{1,0:T(8,128)(2,1)S(1)} %collective-permute-done.11.refs_1_, bf16[8,2048]{1,0:T(8,128)(2,1)S(1)} %collective-permute-done.12.refs_2_, ...), custom_call_target="tpu_custom_call" | custom-call | tf_op jit(solution)/shard_map/output/pallas_call | solution.py:338
  57.8 0.5 collective-permute-start.14
  58.3 1.2 %collective-permute-done.14 = f32[16,4096]{1,0:T(8,128)S(1)} collective-permute-done((f32[16,4096]{1,0:T(8,128)S(1)}, f32[16,4096]{1,0:T(8,128)S(1)}, u32[]{:S(2)}, u32[]{:S(2)}) %collective-permute-start.14) | collective-permute-done | bytes 262176 | tf_op jit(solution)/shard_map/ppermute | solution.py:59
  59.5 2.5 %collective-permute-start.15 = (f16[16,4096]{1,0:T(8,128)(2,1)S(1)}, f16[16,4096]{1,0:T(8,128)(2,1)S(1)}, u32[]{:S(2)}, u32[]{:S(2)}) collective-permute-start(f16[16,4096]{1,0:T(8,128)(2,1)S(1)} %get-tuple-element.29), channel_id=1, source_target_pairs={{0,2},{1,3},{2,0},{3,1},{4,6},{5,7},{6,4},{7,5},{8,10},{9,11},{10,... | collective-permute-start | bytes 393224 | tf_op jit(solution)/shard_map/ppermute | solution.py:59
  62.1 4.0 %collective-permute-done.15 = f16[16,4096]{1,0:T(8,128)(2,1)S(1)} collective-permute-done((f16[16,4096]{1,0:T(8,128)(2,1)S(1)}, f16[16,4096]{1,0:T(8,128)(2,1)S(1)}, u32[]{:S(2)}, u32[]{:S(2)}) %collective-permute-start.15) | collective-permute-done | bytes 131104 | tf_op jit(solution)/shard_map/ppermute | solution.py:59
  66.1 0.1 collective-permute-start.16
  66.2 1.3 %collective-permute-done.16 = bf16[16,4096]{1,0:T(8,128)(2,1)S(1)} collective-permute-done((bf16[16,4096]{1,0:T(8,128)(2,1)S(1)}, bf16[16,4096]{1,0:T(8,128)(2,1)S(1)}, u32[]{:S(2)}, u32[]{:S(2)}) %collective-permute-start.16) | collective-permute-done | bytes 131104 | tf_op jit(solution)/shard_map/ppermute | solution.py:59
  67.6 0.7 %pad_maximum_fusion = bf16[32,4096]{1,0:T(8,128)(2,1)} fusion(bf16[16,4096]{1,0:T(8,128)(2,1)S(1)} %get-tuple-element.32, bf16[16,4096]{1,0:T(8,128)(2,1)S(1)} %get-tuple-element.31), kind=kLoop, calls=%fused_computation | loop fusion | flops 524288 | bytes 524288 | tf_op jit(solution)/shard_map/concatenate | solution.py:368
  (34 shorter events, 0.2 us)
Async XLA Ops:
  8.0 12.6 %collective-permute-start = (f32[8,2432]{1,0:T(8,128)}, f32[8,2432]{1,0:T(8,128)S(1)}, u32[]{:S(2)}, u32[]{:S(2)}) collective-permute-start(f32[8,2432]{1,0:T(8,128)} %get-tuple-element.19), channel_id=1, source_target_pairs={{0,4},{4,0},{8,12},{12,8},{1,5},{5,1},{9,13},{13,9},{2,6},{6,2},{1... | collective-permute-start | bytes 233480 | tf_op jit(solution)/shard_map/ppermute | solution.py:37
  11.1 9.5 %collective-permute-start.1 = (f32[8,2432]{1,0:T(8,128)}, f32[8,2432]{1,0:T(8,128)S(1)}, u32[]{:S(2)}, u32[]{:S(2)}) collective-permute-start(f32[8,2432]{1,0:T(8,128)} %get-tuple-element.20), channel_id=1, source_target_pairs={{0,8},{4,12},{8,0},{12,4},{1,9},{5,13},{9,1},{13,5},{2,10},{6,14},... | collective-permute-start | bytes 233480 | tf_op jit(solution)/shard_map/ppermute | solution.py:37
  13.7 6.9 %collective-permute-start.2 = (f32[8,2432]{1,0:T(8,128)}, f32[8,2432]{1,0:T(8,128)S(1)}, u32[]{:S(2)}, u32[]{:S(2)}) collective-permute-start(f32[8,2432]{1,0:T(8,128)} %get-tuple-element.21), channel_id=1, source_target_pairs={{0,12},{4,8},{8,4},{12,0},{1,13},{5,9},{9,5},{13,1},{2,14},{6,10},... | collective-permute-start | bytes 233480 | tf_op jit(solution)/shard_map/ppermute | solution.py:37
  13.7 0.9 %copy-start.3 = (f32[8,2432]{1,0:T(8,128)S(1)}, f32[8,2432]{1,0:T(8,128)}, u32[]{:S(2)}) copy-start(f32[8,2432]{1,0:T(8,128)} %get-tuple-element.18.refs_0_) | copy-start | bytes 233476
  14.6 6.1 %copy-start.7 = (f32[2048]{0:T(1024)S(1)}, f32[2048]{0:T(1024)}, u32[]{:S(2)}) copy-start(f32[2048]{0:T(1024)} %param.20) | copy-start | bytes 24580
  14.6 6.1 %copy-start.8 = (f32[256]{0:T(256)S(1)}, f32[256]{0:T(256)}, u32[]{:S(2)}) copy-start(f32[256]{0:T(256)} %param.22) | copy-start | bytes 3076
  14.6 16.3 %copy-start = (bf16[8,4,128,128]{3,2,1,0:T(8,128)(2,1)S(1)}, bf16[8,4,128,128]{3,2,1,0:T(8,128)(2,1)}, u32[]{:S(2)}) copy-start(bf16[8,4,128,128]{3,2,1,0:T(8,128)(2,1)} %refs_6_.1) | copy-start | bytes 3145732
  14.6 16.3 %copy-start.1 = (bf16[8,4,128,128]{3,2,1,0:T(8,128)(2,1)S(1)}, bf16[8,4,128,128]{3,2,1,0:T(8,128)(2,1)}, u32[]{:S(2)}) copy-start(bf16[8,4,128,128]{3,2,1,0:T(8,128)(2,1)} %refs_7_.1) | copy-start | bytes 3145732
  14.6 16.3 %copy-start.4 = (f32[8,4,128]{2,1,0:T(4,128)S(1)}, f32[8,4,128]{2,1,0:T(4,128)}, u32[]{:S(2)}) copy-start(f32[8,4,128]{2,1,0:T(4,128)} %param.25) | copy-start | bytes 49156
  14.6 16.3 %copy-start.5 = (f32[8,4,128]{2,1,0:T(4,128)S(1)}, f32[8,4,128]{2,1,0:T(4,128)}, u32[]{:S(2)}) copy-start(f32[8,4,128]{2,1,0:T(4,128)} %param.26) | copy-start | bytes 49156
  14.6 16.3 %copy-start.9 = (s32[8]{0:T(128)S(1)}, s32[8]{0:T(128)}, u32[]{:S(2)}) copy-start(s32[8]{0:T(128)} %refs_5_.1) | copy-start | bytes 100
  14.6 40.1 %copy-start.2 = (f32[1,32,4096]{2,1,0:T(8,128)S(1)}, f32[1,32,4096]{2,1,0:T(8,128)}, u32[]{:S(2)}) copy-start(f32[1,32,4096]{2,1,0:T(8,128)} %param.16) | copy-start | bytes 1572868
  14.6 40.1 %copy-start.6 = (f32[4096]{0:T(1024)S(1)}, f32[4096]{0:T(1024)}, u32[]{:S(2)}) copy-start(f32[4096]{0:T(1024)} %param.29) | copy-start | bytes 49156
  20.6 45.5 %copy-start.10 = (bf16[32,4096]{1,0:T(8,128)(2,1)S(1)}, bf16[32,4096]{1,0:T(8,128)(2,1)}, u32[]{:S(2)}) copy-start(bf16[32,4096]{1,0:T(8,128)(2,1)} %residual.1) | copy-start | bytes 786436
  20.7 8.5 %collective-permute-start.3 = (bf16[8,2304]{1,0:T(8,128)(2,1)S(1)}, bf16[8,2304]{1,0:T(8,128)(2,1)S(1)}, u32[]{:S(2)}, u32[]{:S(2)}) collective-permute-start(bf16[8,2304]{1,0:T(8,128)(2,1)S(1)} %norm.1.refs_4_), channel_id=1, source_target_pairs={{1,4},{2,8},{3,12},{4,1},{6,9},{7,13},{8,2},{9,6},{11,14},{12,3},{... | collective-permute-start | bytes 110600 | tf_op jit(solution)/shard_map/ppermute | solution.py:54
  21.4 7.9 %collective-permute-start.4 = (bf16[8,2304]{1,0:T(8,128)(2,1)S(1)}, bf16[8,2304]{1,0:T(8,128)(2,1)S(1)}, u32[]{:S(2)}, u32[]{:S(2)}) collective-permute-start(bf16[8,2304]{1,0:T(8,128)(2,1)S(1)} %norm.1.refs_4_), channel_id=1, source_target_pairs={{0,4},{1,0},{2,12},{3,8},{4,5},{5,1},{6,13},{7,9},{8,6},{9,2},{10,... | collective-permute-start | bytes 110600 | tf_op jit(solution)/shard_map/ppermute | solution.py:54
  23.7 6.4 %collective-permute-start.5 = (bf16[8,2304]{1,0:T(8,128)(2,1)S(1)}, bf16[8,2304]{1,0:T(8,128)(2,1)S(1)}, u32[]{:S(2)}, u32[]{:S(2)}) collective-permute-start(bf16[8,2304]{1,0:T(8,128)(2,1)S(1)} %norm.1.refs_4_), channel_id=1, source_target_pairs={{0,8},{1,12},{2,0},{3,4},{4,9},{5,13},{6,1},{7,5},{8,10},{9,14},{1... | collective-permute-start | bytes 110600 | tf_op jit(solution)/shard_map/ppermute | solution.py:54
  26.8 4.1 %collective-permute-start.6 = (bf16[8,2304]{1,0:T(8,128)(2,1)S(1)}, bf16[8,2304]{1,0:T(8,128)(2,1)S(1)}, u32[]{:S(2)}, u32[]{:S(2)}) collective-permute-start(bf16[8,2304]{1,0:T(8,128)(2,1)S(1)} %norm.1.refs_4_), channel_id=1, source_target_pairs={{0,12},{1,8},{2,4},{3,0},{4,13},{5,9},{6,5},{7,1},{8,14},{9,10},{1... | collective-permute-start | bytes 110600 | tf_op jit(solution)/shard_map/ppermute | solution.py:54
  32.9 5.2 %collective-permute-start.7 = (f32[136,128]{1,0:T(8,128)S(1)}, f32[136,128]{1,0:T(8,128)S(1)}, u32[]{:S(2)}, u32[]{:S(2)}) collective-permute-start(f32[136,128]{1,0:T(8,128)S(1)} %get-tuple-element.23), channel_id=1, source_target_pairs={{0,4},{4,0},{8,12},{12,8},{1,5},{5,1},{9,13},{13,9},{2,6},{6,2},{1... | collective-permute-start | bytes 208904 | tf_op jit(solution)/shard_map/ppermute | solution.py:37
  35.7 8.9 %collective-permute-start.8 = (f32[136,128]{1,0:T(8,128)S(1)}, f32[136,128]{1,0:T(8,128)S(1)}, u32[]{:S(2)}, u32[]{:S(2)}) collective-permute-start(f32[136,128]{1,0:T(8,128)S(1)} %get-tuple-element.24), channel_id=1, source_target_pairs={{0,8},{4,12},{8,0},{12,4},{1,9},{5,13},{9,1},{13,5},{2,10},{6,14},... | collective-permute-start | bytes 208904 | tf_op jit(solution)/shard_map/ppermute | solution.py:37
  37.8 6.8 %collective-permute-start.9 = (f32[136,128]{1,0:T(8,128)S(1)}, f32[136,128]{1,0:T(8,128)S(1)}, u32[]{:S(2)}, u32[]{:S(2)}) collective-permute-start(f32[136,128]{1,0:T(8,128)S(1)} %get-tuple-element.25), channel_id=1, source_target_pairs={{0,12},{4,8},{8,4},{12,0},{1,13},{5,9},{9,5},{13,1},{2,14},{6,10},... | collective-permute-start | bytes 208904 | tf_op jit(solution)/shard_map/ppermute | solution.py:37
  44.9 6.6 %collective-permute-start.10 = (bf16[8,2048]{1,0:T(8,128)(2,1)S(1)}, bf16[8,2048]{1,0:T(8,128)(2,1)S(1)}, u32[]{:S(2)}, u32[]{:S(2)}) collective-permute-start(bf16[8,2048]{1,0:T(8,128)(2,1)S(1)} %merge.1.refs_4_), channel_id=1, source_target_pairs={{1,4},{2,8},{3,12},{4,1},{6,9},{7,13},{8,2},{9,6},{11,14},{12,3},{... | collective-permute-start | bytes 98312 | tf_op jit(solution)/shard_map/ppermute | solution.py:54
  45.5 5.9 %collective-permute-start.11 = (bf16[8,2048]{1,0:T(8,128)(2,1)S(1)}, bf16[8,2048]{1,0:T(8,128)(2,1)S(1)}, u32[]{:S(2)}, u32[]{:S(2)}) collective-permute-start(bf16[8,2048]{1,0:T(8,128)(2,1)S(1)} %merge.1.refs_4_), channel_id=1, source_target_pairs={{0,4},{1,0},{2,12},{3,8},{4,5},{5,1},{6,13},{7,9},{8,6},{9,2},{10,... | collective-permute-start | bytes 98312 | tf_op jit(solution)/shard_map/ppermute | solution.py:54
  48.8 4.2 %collective-permute-start.12 = (bf16[8,2048]{1,0:T(8,128)(2,1)S(1)}, bf16[8,2048]{1,0:T(8,128)(2,1)S(1)}, u32[]{:S(2)}, u32[]{:S(2)}) collective-permute-start(bf16[8,2048]{1,0:T(8,128)(2,1)S(1)} %merge.1.refs_4_), channel_id=1, source_target_pairs={{0,8},{1,12},{2,0},{3,4},{4,9},{5,13},{6,1},{7,5},{8,10},{9,14},{1... | collective-permute-start | bytes 98312 | tf_op jit(solution)/shard_map/ppermute | solution.py:54
  51.4 3.3 %collective-permute-start.13 = (bf16[8,2048]{1,0:T(8,128)(2,1)S(1)}, bf16[8,2048]{1,0:T(8,128)(2,1)S(1)}, u32[]{:S(2)}, u32[]{:S(2)}) collective-permute-start(bf16[8,2048]{1,0:T(8,128)(2,1)S(1)} %merge.1.refs_4_), channel_id=1, source_target_pairs={{0,12},{1,8},{2,4},{3,0},{4,13},{5,9},{6,5},{7,1},{8,14},{9,10},{1... | collective-permute-start | bytes 98312 | tf_op jit(solution)/shard_map/ppermute | solution.py:54
  57.8 1.7 %collective-permute-start.14 = (f32[16,4096]{1,0:T(8,128)S(1)}, f32[16,4096]{1,0:T(8,128)S(1)}, u32[]{:S(2)}, u32[]{:S(2)}) collective-permute-start(f32[16,4096]{1,0:T(8,128)S(1)} %get-tuple-element.28), channel_id=1, source_target_pairs={{0,1},{1,0},{2,3},{3,2},{4,5},{5,4},{6,7},{7,6},{8,9},{9,8},{10,11... | collective-permute-start | bytes 786440 | tf_op jit(solution)/shard_map/ppermute | solution.py:59
  59.5 6.6 %collective-permute-start.15 = (f16[16,4096]{1,0:T(8,128)(2,1)S(1)}, f16[16,4096]{1,0:T(8,128)(2,1)S(1)}, u32[]{:S(2)}, u32[]{:S(2)}) collective-permute-start(f16[16,4096]{1,0:T(8,128)(2,1)S(1)} %get-tuple-element.29), channel_id=1, source_target_pairs={{0,2},{1,3},{2,0},{3,1},{4,6},{5,7},{6,4},{7,5},{8,10},{9,11},{10,... | collective-permute-start | bytes 393224 | tf_op jit(solution)/shard_map/ppermute | solution.py:59
  66.1 1.4 %collective-permute-start.16 = (bf16[16,4096]{1,0:T(8,128)(2,1)S(1)}, bf16[16,4096]{1,0:T(8,128)(2,1)S(1)}, u32[]{:S(2)}, u32[]{:S(2)}) collective-permute-start(bf16[16,4096]{1,0:T(8,128)(2,1)S(1)} %add_convert_fusion), channel_id=1, source_target_pairs={{0,1},{1,0},{2,3},{3,2},{4,5},{5,4},{6,7},{7,6},{8,9},{9,8},{10,11... | collective-permute-start | bytes 393224 | tf_op jit(solution)/shard_map/ppermute | solution.py:59

commit v6 on v5

--- a/solution.py
+++ b/solution.py
@@ -15,6 +15,8 @@
 EPSILON = 1e-05
 NEGATIVE = -1e30
 LANES = 128
+LOWEST = -4e7
+UNITS = (32768.0, 16.0, 0.0078125)
 SHRINK = 32.0
 f32 = jnp.float32
 bf16 = jnp.bfloat16
@@ -34,25 +36,41 @@
 
 
 def trade(chunks, axis, n):
-    return [chunks[0]] + [lax.ppermute(chunks[k], axis, partners(n, k)) for k in range(1, n)]
+    return [chunks[0]] + [lax.ppermute(chunks[k], axis, partners(n, k)) for k in (3, 1, 2)]
 
 
 def place(placed, pieces, n):
-    me = lax.axis_index("gx")
-    for k in range(n):
-        placed[me ^ k] = pieces[k][...].astype(f32)
-
-    @pl.when(me == lax.axis_index("gy"))
+    gx = lax.axis_index("gx")
+    for k in range(n // 2):
+        for core in range(2):
+            placed[2 * ((gx // 2) ^ k) + core] = pieces[k][core].astype(f32)
+
+    @pl.when(gx == lax.axis_index("gy"))
     def _():
-        placed[me] = pieces[n][...].astype(f32)
+        for core in range(2):
+            placed[2 * (gx // 2) + core] = pieces[n // 2][core].astype(f32)
+
+
+def pair_kernel(mine, other, out):
+    core = lax.axis_index("gy") & 1
+    out[core] = mine[...]
+    out[1 - core] = other[...]
 
 
 def spread(value, n):
+    pair = pl.pallas_call(
+        pair_kernel,
+        in_specs=[VMEM] * 2,
+        out_specs=VMEM,
+        out_shape=jax.ShapeDtypeStruct((2,) + value.shape, value.dtype),
+        compiler_params=params(4),
+        name="pair",
+    )(value, swap(value, "gy", n, 1))
     pieces = []
-    for k in range(n):
-        pairs = [(a * n + b, (b ^ k) * n + a) for a in range(n) for b in range(n)]
-        pieces.append(lax.ppermute(value, ("gx", "gy"), [pair for pair in pairs if pair[0] != pair[1]]))
-    return pieces + [value]
+    for k in range(n // 2):
+        pairs = [(a * n + b, (b % 2 + 2 * ((b // 2) ^ k)) * n + a) for a in range(n) for b in range(n)]
+        pieces.append(lax.ppermute(pair, ("gx", "gy"), [p for p in pairs if p[0] != p[1]]))
+    return pieces + [pair]
 
 
 def swap(value, axis, n, offset):
@@ -165,32 +183,44 @@
     )(query_scale.reshape(-1, LANES), keyval_scale.reshape(-1, LANES), *parts)
 
 
-def fetch_kernel(n, *refs):
-    sources, targets, sems = refs[1 : n + 1], refs[n + 1 : 2 * n + 1], refs[-1]
-    copies = [pltpu.make_async_copy(a, b, sems.at[i]) for i, (a, b) in enumerate(zip(sources, targets))]
-    for copy in copies:
-        copy.start()
-    for copy in copies:
-        copy.wait()
-
-
-def fetch(after, *arrays):
-    n = len(arrays)
-    size = sum(array.size * array.dtype.itemsize for array in arrays)
+def fetch_kernel(first, _, source, target, sem):
+    copy = pltpu.make_async_copy(source.at[pl.ds(first, target.shape[0])], target, sem)
+    copy.start()
+    copy.wait()
+
+
+def fetch(after, array, first, count):
+    shape = (count,) + array.shape[1:]
+    size = count * (array.size // array.shape[0]) * array.dtype.itemsize
     return pl.pallas_call(
-        functools.partial(fetch_kernel, n),
-        in_specs=[ANY] + [HBM] * n,
-        out_specs=[VMEM] * n,
-        out_shape=[jax.ShapeDtypeStruct(array.shape, array.dtype) for array in arrays],
-        scratch_shapes=[pltpu.SemaphoreType.DMA((n,))],
-        compiler_params=params(24),
+        functools.partial(fetch_kernel, first),
+        in_specs=[ANY, HBM],
+        out_specs=VMEM,
+        out_shape=jax.ShapeDtypeStruct(shape, array.dtype),
+        scratch_shapes=[pltpu.SemaphoreType.DMA],
+        compiler_params=params(40),
         cost_estimate=pl.CostEstimate(flops=0, bytes_accessed=2 * size, transcendentals=0),
         name="fetch",
-    )(after, *arrays)
+    )(after, array)
+
+
+def digits(value, units):
+    rows = []
+    for unit in units:
+        rows.append(jnp.floor(value * (1 / unit) + 0.5))
+        value = value - rows[-1] * unit
+    return rows + [value]
+
+
+def joined_digits(rows, units):
+    value = rows[0] * units[0]
+    for row, unit in zip(rows[1:], units[1:] + (1.0,)):
+        value = value + row * unit
+    return value
 
 
 def attend_kernel(n, *refs):
-    pieces, refs = refs[: n + 1], refs[n + 1 :]
+    pieces, refs = refs[: n // 2 + 1], refs[n // 2 + 1 :]
     lengths, keys, values, key_scale, value_scale = refs[:5]
     outs = refs[5 : n + 5]
     placed, q_rows, logits, messages, fresh = refs[n + 5 :]
@@ -241,10 +271,12 @@
     wide = LANES // GROUP
     for p in range(n):
         rows = []
-        for kind in (tops, totals):
-            for b in range(count // LANES):
-                column = jnp.concatenate(kind[p][b * wide : (b + 1) * wide], axis=0)
-                rows.append(jnp.sum(jnp.where(diagonal, column, 0.0), axis=0, keepdims=True))
+        for b in range(count // LANES):
+            top, total = [
+                jnp.sum(jnp.where(diagonal, jnp.concatenate(kind[p][b * wide : (b + 1) * wide], axis=0), 0.0), axis=0, keepdims=True)
+                for kind in (tops, totals)
+            ]
+            rows += digits(jnp.maximum(top, LOWEST), UNITS) + digits(total, (1.0,))
         spare = messages.shape[1] - count - len(rows)
         messages[p, count:, :] = jnp.concatenate(rows + [jnp.zeros((spare, LANES), f32)], axis=0)
     for k in range(n):
@@ -254,14 +286,14 @@
 def attend(n, pieces, lengths, keys, values, key_scale, value_scale):
     requests, _, local, _ = keys.shape
     count = requests * GROUP
-    height = count + -(-2 * count // LANES // 8) * 8
+    height = count + -(-(len(UNITS) + 3) * (count // LANES) // 8) * 8
     return pl.pallas_call(
         functools.partial(attend_kernel, n),
-        in_specs=[VMEM] * (n + 1) + [SMEM, VMEM, VMEM, VMEM, VMEM],
+        in_specs=[VMEM] * len(pieces) + [SMEM, VMEM, VMEM, VMEM, VMEM],
         out_specs=[VMEM] * n,
         out_shape=[jax.ShapeDtypeStruct((height, LANES), f32)] * n,
         scratch_shapes=[
-            pltpu.VMEM((n,) + pieces[0].shape, f32),
+            pltpu.VMEM((n,) + pieces[0].shape[1:], f32),
             pltpu.VMEM((requests * HEADS, HEAD_DIM), f32),
             pltpu.VMEM((requests * HEADS, local), f32),
             pltpu.VMEM((n, height, LANES), f32),
@@ -280,8 +312,10 @@
     blocks = count // LANES
     for b in range(blocks):
         at = slice(b * LANES, (b + 1) * LANES)
-        tops = [part[count + b : count + b + 1, :] for part in parts]
-        totals = [part[count + blocks + b : count + blocks + b + 1, :] for part in parts]
+        first, size = count + b * (len(UNITS) + 3), len(UNITS) + 1
+        rows = [[part[first + i : first + i + 1, :] for i in range(size + 2)] for part in parts]
+        tops = [joined_digits(row[:size], UNITS) for row in rows]
+        totals = [joined_digits(row[size:], (1.0,)) for row in rows]
         largest = tops[0]
         for top in tops[1:]:
             largest = jnp.maximum(largest, top)
@@ -314,15 +348,17 @@
 
 
 def output_kernel(n, *refs):
-    pieces = refs[: n + 1]
-    w_out, out_scale, ffn, kept, given, total, placed = refs[n + 1 :]
-    width = w_out.shape[1]
+    pieces, refs = refs[: n // 2 + 1], refs[n // 2 + 1 :]
+    upper, lower, out_scale, ffn, kept, given, total, placed = refs
+    head, width = upper.shape
     place(placed, pieces, n)
-    attended = placed[...].reshape(total.shape[0], w_out.shape[0]).astype(bf16)
+    attended = placed[...].reshape(total.shape[0], head + lower.shape[0]).astype(bf16)
     span = width // 4
     for i in range(4):
         part = slice(i * span, (i + 1) * span)
-        total[:, part] = jnp.dot(attended, w_out[:, part], preferred_element_type=f32)
+        total[:, part] = jnp.dot(attended[:, :head], upper[:, part], preferred_element_type=f32) + jnp.dot(
+            attended[:, head:], lower[:, part], preferred_element_type=f32
+        )
     for t in range(width // LANES):
         lanes = slice(t * LANES, (t + 1) * LANES)
         total[:, lanes] = total[:, lanes] * out_scale[t : t + 1, :] + ffn[:, lanes]
@@ -332,18 +368,18 @@
     given[...] = total[pl.ds(pl.multiple_of((1 - core) * rows, rows), rows), :]
 
 
-def output(pieces, w_out, out_scale, ffn):
-    n = len(pieces) - 1
+def output(pieces, upper, lower, out_scale, ffn):
+    n = 2 * (len(pieces) - 1)
     rows, width = ffn.shape
     return pl.pallas_call(
         functools.partial(output_kernel, n),
-        in_specs=[VMEM] * (n + 4),
+        in_specs=[VMEM] * (len(pieces) + 4),
         out_specs=[VMEM] * 2,
         out_shape=[jax.ShapeDtypeStruct((rows // 2, width), f32)] * 2,
-        scratch_shapes=[pltpu.VMEM((rows, width), f32), pltpu.VMEM((n,) + pieces[0].shape, f32)],
+        scratch_shapes=[pltpu.VMEM((rows, width), f32), pltpu.VMEM((n,) + pieces[0].shape[1:], f32)],
         compiler_params=params(20),
         name="output",
-    )(*pieces, w_out, out_scale.reshape(-1, LANES), ffn)
+    )(*pieces, upper, lower, out_scale.reshape(-1, LANES), ffn)
 
 
 def body(n_gx, n_gy, residual, ffn_partial, norm_gain, smooth_scale, w_query, query_scale, w_keyval, keyval_scale,
@@ -352,13 +388,18 @@
     rows = residual.shape[0]
     requests = rows // n_gy
     parts = project(n_gx, residual, norm_gain, smooth_scale, w_query, w_keyval)
-    (w_near,) = fetch(parts[0], w_out)
+    head = w_out.shape[0] * 6 // 8
+    upper = fetch(parts[0], w_out, 0, head)
     total = trade(parts, "gx", n_gx)
-    total[0], w_near = lax.optimization_barrier((total[0], w_near))
+    total[0], upper = lax.optimization_barrier((total[0], upper))
     pieces = spread(norm(total, query_scale, keyval_scale), n_gx)
     parts = attend(n_gx, pieces, lengths, key_cache, value_cache, key_scale, value_scale)
-    pieces = spread(merge(trade(parts, "gx", n_gx), requests), n_gx)
-    kept, given = output(pieces, w_near, out_scale, ffn_partial[0])
+    lower = fetch(parts[0], w_out, head, w_out.shape[0] - head)
+    total = trade([part.astype(jnp.float16) for part in parts], "gx", n_gx)
+    total = [parts[0]] + [part.astype(f32) for part in total[1:]]
+    total[0], lower = lax.optimization_barrier((total[0], lower))
+    pieces = spread(merge(total, requests), n_gx)
+    kept, given = output(pieces, upper, lower, out_scale, ffn_partial[0])
     core = gy & 1
     chip = kept + swap(given, "gy", n_gy, 1)
     other = swap((chip * (1 / SHRINK)).astype(jnp.float16), "gy", n_gy, 2)

time: 68.5 us -> 64.2 us (0.937)
  starting transfers between devices: 29.2 us -> 25.1 us
  waiting for transfers between devices: 17.9 us -> 16.5 us
  Pallas kernels: 19.3 us -> 20.3 us
    ppermute x8 -> x4, starting transfers between devices: 15.1 us -> 10.5 us  [spread(): lax.ppermute(pair, ('gx', 'gy'), [p for p in pairs if p[0] != p[1]])]
    ppermute x6, waiting for transfers between devices: 6.5 us -> 2.38 us  [trade(): lax.ppermute(chunks[k], axis, partners(n, k))]
    ppermute x3 -> x5, waiting for transfers between devices: 6.51 us -> 8.91 us  [swap(): return lax.ppermute(value, axis, partners(n, offset))]
    pallas_call x3 -> x6, Pallas kernels: 11 us -> 12 us  [the longest x2 6.93 us: fetch(): pl.pallas_call(functools.partial(fetch_kernel, first), in_specs=[ANY, HBM...]
    ppermute x3 -> x5, starting transfers between devices: 3.14 us -> 3.92 us  [swap(): return lax.ppermute(value, axis, partners(n, offset))]
    ppermute x8 -> x4, waiting for transfers between devices: 4.91 us -> 5.2 us  [spread(): lax.ppermute(pair, ('gx', 'gy'), [p for p in pairs if p[0] != p[1]])]
  transfers between devices with their start and end apart: 17 -> 15, of which waited for: 8 -> 9; matrix products, arithmetic and copies ran while one was open for 0% -> 0% of each run, Pallas kernels for 9% -> 11%
where the time goes in v6:
time: 64.2 us; the launch traced here: 64 us
  starting transfers between devices  25.1 us (39%)
  Pallas kernels  20.3 us (32%)
  waiting for transfers between devices  16.5 us (26%)
  local copies, waits for them, and re-layouts  0.94 us (1%)
  other arithmetic  0.88 us (1%)
    ppermute x6, starting transfers between devices, trade(): lax.ppermute(chunks[k], axis, partners(n, k))  10.7 us
    ppermute x4, starting transfers between devices, spread(): lax.ppermute(pair, ('gx', 'gy'), [p for p in pairs if p[0] != p[1]])  10.5 us
    ppermute x5, waiting for transfers between devices, swap(): return lax.ppermute(value, axis, partners(n, offset))  8.91 us
    pallas_call x1, Pallas kernels, project(): pl.pallas_call(functools.partial(project_kernel, n), in_specs=[HBM] * 5,...  8.01 us
    pallas_call x2, Pallas kernels, fetch(): pl.pallas_call(functools.partial(fetch_kernel, first), in_specs=[ANY, HBM...  6.93 us
    ppermute x4, waiting for transfers between devices, spread(): lax.ppermute(pair, ('gx', 'gy'), [p for p in pairs if p[0] != p[1]])  5.2 us
    ppermute x5, starting transfers between devices, swap(): return lax.ppermute(value, axis, partners(n, offset))  3.92 us
    pallas_call x1, Pallas kernels, output(): pl.pallas_call(functools.partial(output_kernel, n), in_specs=[VMEM] * (le...  3.05 us
  transfers between devices with their start and end apart: 15, of which 9 were waited for; matrix products, arithmetic and copies ran while one was open for 0% of the time, Pallas kernels for 11%

profile of v6, /device:TPU:0, one launch (start us, length us, event | category | flops | bytes accessed | tf_op | source)
XLA Modules:
  0.0 64.0 jit_solution(5918565429381833088)
XLA Ops:
  0.0 8.0 %project.1 = (f32[8,2432]{1,0:T(8,128)}, f32[8,2432]{1,0:T(8,128)}, f32[8,2432]{1,0:T(8,128)}, f32[8,2432]{1,0:T(8,128)}) custom-call(bf16[32,4096]{1,0:T(8,128)(2,1)} %residual.1, f32[32,128]{1,0:T(8,128)} %bitcast.14, f32[32,128]{1,0:T(8,128)} %bitcast.15, bf16[4096,2048]{1,0:T(8,128)(2,1)} %w_query.1, bf16[4096,256]{1,0:T(8,128)(2,1)} %w_keyval.1), custom_call_target="tpu_custom_call" | custom-call | tf_op jit(solution)/shard_map/project/pallas_call | solution.py:137
  8.0 5.1 %collective-permute-start = (f32[8,2432]{1,0:T(8,128)}, f32[8,2432]{1,0:T(8,128)S(1)}, u32[]{:S(2)}, u32[]{:S(2)}) collective-permute-start(f32[8,2432]{1,0:T(8,128)} %get-tuple-element.21), channel_id=1, source_target_pairs={{0,12},{4,8},{8,4},{12,0},{1,13},{5,9},{9,5},{13,1},{2,14},{6,10},... | collective-permute-start | bytes 233480 | tf_op jit(solution)/shard_map/ppermute | solution.py:39
  13.1 0.6 collective-permute-start.2
  13.8 0.9 %copy-done.3 = f32[8,2432]{1,0:T(8,128)S(1)} copy-done((f32[8,2432]{1,0:T(8,128)S(1)}, f32[8,2432]{1,0:T(8,128)}, u32[]{:S(2)}) %copy-start.3) | copy-done | bytes 77848
  14.7 4.7 %fetch.2.refs_3_ = bf16[1536,4096]{1,0:T(8,128)(2,1)S(1)} custom-call(f32[8,2432]{1,0:T(8,128)S(1)} %copy-done.3, bf16[2048,4096]{1,0:T(8,128)(2,1)} %source.3), custom_call_target="tpu_custom_call" | custom-call | bytes 25165824 | tf_op jit(solution)/shard_map/fetch/pallas_call | solution.py:195
  19.5 0.1 norm.1.mine
  19.7 1.2 %collective-permute-done.3.other = bf16[8,2304]{1,0:T(8,128)(2,1)S(1)} collective-permute-done((bf16[8,2304]{1,0:T(8,128)(2,1)S(1)}, bf16[8,2304]{1,0:T(8,128)(2,1)S(1)}, u32[]{:S(2)}, u32[]{:S(2)}) %collective-permute-start.3) | collective-permute-done | bytes 36896 | tf_op jit(solution)/shard_map/ppermute | solution.py:77
  20.9 0.7 %collective-permute-start.4 = (bf16[2,8,2304]{2,1,0:T(8,128)(2,1)S(1)}, bf16[2,8,2304]{2,1,0:T(8,128)(2,1)S(1)}, u32[]{:S(2)}, u32[]{:S(2)}) collective-permute-start(bf16[2,8,2304]{2,1,0:T(8,128)(2,1)S(1)} %pair.2.refs_2_), channel_id=1, source_target_pairs={{1,4},{2,8},{3,12},{4,1},{6,9},{7,13},{8,2},{9,6},{11,14},{12,3},{... | collective-permute-start | bytes 221192 | tf_op jit(solution)/shard_map/ppermute | solution.py:72
  21.5 5.3 %collective-permute-start.5 = (bf16[2,8,2304]{2,1,0:T(8,128)(2,1)S(1)}, bf16[2,8,2304]{2,1,0:T(8,128)(2,1)S(1)}, u32[]{:S(2)}, u32[]{:S(2)}) collective-permute-start(bf16[2,8,2304]{2,1,0:T(8,128)(2,1)S(1)} %pair.2.refs_2_), channel_id=1, source_target_pairs={{0,8},{1,12},{2,0},{3,4},{4,9},{5,13},{6,1},{7,5},{8,10},{9,14},{1... | collective-permute-start | bytes 221192 | tf_op jit(solution)/shard_map/ppermute | solution.py:72
  26.8 2.9 %collective-permute-done.5.refs_1_ = bf16[2,8,2304]{2,1,0:T(8,128)(2,1)S(1)} collective-permute-done((bf16[2,8,2304]{2,1,0:T(8,128)(2,1)S(1)}, bf16[2,8,2304]{2,1,0:T(8,128)(2,1)S(1)}, u32[]{:S(2)}, u32[]{:S(2)}) %collective-permute-start.5) | collective-permute-done | bytes 73760 | tf_op jit(solution)/shard_map/ppermute | solution.py:72
  29.7 2.0 %attend.1 = (f32[136,128]{1,0:T(8,128)S(1)}, f32[136,128]{1,0:T(8,128)S(1)}, f32[136,128]{1,0:T(8,128)S(1)}, f32[136,128]{1,0:T(8,128)S(1)}) custom-call(bf16[2,8,2304]{2,1,0:T(8,128)(2,1)S(1)} %collective-permute-done.4.refs_0_, bf16[2,8,2304]{2,1,0:T(8,128)(2,1)S(1)} %collective-permute-done.5.refs_1_, bf16[2,8,2304]{2,1,0:T(8,128)(2,1)S(1)} %pair.2.refs_2_, ...), custom_call_target="tpu_custom_call" | custom-call | tf_op jit(solution)/shard_map/attend/pallas_call | solution.py:290
  31.8 4.2 %collective-permute-start.6 = (f16[136,128]{1,0:T(8,128)(2,1)S(1)}, f16[136,128]{1,0:T(8,128)(2,1)S(1)}, u32[]{:S(2)}, u32[]{:S(2)}) collective-permute-start(f16[136,128]{1,0:T(8,128)(2,1)S(1)} %convert_element_type.31), channel_id=1, source_target_pairs={{0,12},{4,8},{8,4},{12,0},{1,13},{5,9},{9,5},{13,1},{2,14},{6,10},... | collective-permute-start | bytes 104456 | tf_op jit(solution)/shard_map/ppermute | solution.py:39
  36.0 0.1 collective-permute-start.7
  36.1 0.6 collective-permute-start.8
  36.7 2.2 %fetch.3.refs_4_ = bf16[512,4096]{1,0:T(8,128)(2,1)S(1)} custom-call(f32[136,128]{1,0:T(8,128)S(1)} %get-tuple-element.25._.refs_0_, bf16[2048,4096]{1,0:T(8,128)(2,1)} %source.3), custom_call_target="tpu_custom_call" | custom-call | bytes 8388608 | tf_op jit(solution)/shard_map/fetch/pallas_call | solution.py:195
  39.0 1.2 %collective-permute-done.7 = f16[136,128]{1,0:T(8,128)(2,1)S(1)} collective-permute-done((f16[136,128]{1,0:T(8,128)(2,1)S(1)}, f16[136,128]{1,0:T(8,128)(2,1)S(1)}, u32[]{:S(2)}, u32[]{:S(2)}) %collective-permute-start.7) | collective-permute-done | bytes 34848 | tf_op jit(solution)/shard_map/ppermute | solution.py:39
  40.2 1.2 %collective-permute-done.8 = f16[136,128]{1,0:T(8,128)(2,1)S(1)} collective-permute-done((f16[136,128]{1,0:T(8,128)(2,1)S(1)}, f16[136,128]{1,0:T(8,128)(2,1)S(1)}, u32[]{:S(2)}, u32[]{:S(2)}) %collective-permute-start.8) | collective-permute-done | bytes 34848 | tf_op jit(solution)/shard_map/ppermute | solution.py:39
  41.4 0.2 merge.1.mine
  41.6 0.1 collective-permute-start.9
  41.6 1.2 %collective-permute-done.9.other = bf16[8,2048]{1,0:T(8,128)(2,1)S(1)} collective-permute-done((bf16[8,2048]{1,0:T(8,128)(2,1)S(1)}, bf16[8,2048]{1,0:T(8,128)(2,1)S(1)}, u32[]{:S(2)}, u32[]{:S(2)}) %collective-permute-start.9) | collective-permute-done | bytes 32800 | tf_op jit(solution)/shard_map/ppermute | solution.py:77
  42.9 0.7 %collective-permute-start.10 = (bf16[2,8,2048]{2,1,0:T(8,128)(2,1)S(1)}, bf16[2,8,2048]{2,1,0:T(8,128)(2,1)S(1)}, u32[]{:S(2)}, u32[]{:S(2)}) collective-permute-start(bf16[2,8,2048]{2,1,0:T(8,128)(2,1)S(1)} %pair.3.refs_2_), channel_id=1, source_target_pairs={{1,4},{2,8},{3,12},{4,1},{6,9},{7,13},{8,2},{9,6},{11,14},{12,3},{... | collective-permute-start | bytes 196616 | tf_op jit(solution)/shard_map/ppermute | solution.py:72
  43.5 3.9 %collective-permute-start.11 = (bf16[2,8,2048]{2,1,0:T(8,128)(2,1)S(1)}, bf16[2,8,2048]{2,1,0:T(8,128)(2,1)S(1)}, u32[]{:S(2)}, u32[]{:S(2)}) collective-permute-start(bf16[2,8,2048]{2,1,0:T(8,128)(2,1)S(1)} %pair.3.refs_2_), channel_id=1, source_target_pairs={{0,8},{1,12},{2,0},{3,4},{4,9},{5,13},{6,1},{7,5},{8,10},{9,14},{1... | collective-permute-start | bytes 196616 | tf_op jit(solution)/shard_map/ppermute | solution.py:72
  47.4 2.3 %collective-permute-done.11.refs_1_ = bf16[2,8,2048]{2,1,0:T(8,128)(2,1)S(1)} collective-permute-done((bf16[2,8,2048]{2,1,0:T(8,128)(2,1)S(1)}, bf16[2,8,2048]{2,1,0:T(8,128)(2,1)S(1)}, u32[]{:S(2)}, u32[]{:S(2)}) %collective-permute-start.11) | collective-permute-done | bytes 65568 | tf_op jit(solution)/shard_map/ppermute | solution.py:72
  49.8 3.0 %output.1 = (f32[16,4096]{1,0:T(8,128)S(1)}, f32[16,4096]{1,0:T(8,128)S(1)}) custom-call(bf16[2,8,2048]{2,1,0:T(8,128)(2,1)S(1)} %collective-permute-done.10.refs_0_, bf16[2,8,2048]{2,1,0:T(8,128)(2,1)S(1)} %collective-permute-done.11.refs_1_, bf16[2,8,2048]{2,1,0:T(8,128)(2,1)S(1)} %pair.3.refs_2_, bf16[1536,4096]{1,0:T(8,128)(2,1)S(1)} %fetch.2.refs_3_, ...), custom_call_target="tpu_custom_call" | custom-call | tf_op jit(solution)/shard_map/output/pallas_call | solution.py:374
  52.8 1.6 %collective-permute-start.12 = (f32[16,4096]{1,0:T(8,128)S(1)}, f32[16,4096]{1,0:T(8,128)S(1)}, u32[]{:S(2)}, u32[]{:S(2)}) collective-permute-start(f32[16,4096]{1,0:T(8,128)S(1)} %get-tuple-element.32), channel_id=1, source_target_pairs={{0,1},{1,0},{2,3},{3,2},{4,5},{5,4},{6,7},{7,6},{8,9},{9,8},{10,11... | collective-permute-start | bytes 786440 | tf_op jit(solution)/shard_map/ppermute | solution.py:77
  54.4 1.2 %collective-permute-done.12 = f32[16,4096]{1,0:T(8,128)S(1)} collective-permute-done((f32[16,4096]{1,0:T(8,128)S(1)}, f32[16,4096]{1,0:T(8,128)S(1)}, u32[]{:S(2)}, u32[]{:S(2)}) %collective-permute-start.12) | collective-permute-done | bytes 262176 | tf_op jit(solution)/shard_map/ppermute | solution.py:77
  55.6 2.2 %collective-permute-start.13 = (f16[16,4096]{1,0:T(8,128)(2,1)S(1)}, f16[16,4096]{1,0:T(8,128)(2,1)S(1)}, u32[]{:S(2)}, u32[]{:S(2)}) collective-permute-start(f16[16,4096]{1,0:T(8,128)(2,1)S(1)} %get-tuple-element.33), channel_id=1, source_target_pairs={{0,2},{1,3},{2,0},{3,1},{4,6},{5,7},{6,4},{7,5},{8,10},{9,11},{10,... | collective-permute-start | bytes 393224 | tf_op jit(solution)/shard_map/ppermute | solution.py:77
  57.8 4.0 %collective-permute-done.13 = f16[16,4096]{1,0:T(8,128)(2,1)S(1)} collective-permute-done((f16[16,4096]{1,0:T(8,128)(2,1)S(1)}, f16[16,4096]{1,0:T(8,128)(2,1)S(1)}, u32[]{:S(2)}, u32[]{:S(2)}) %collective-permute-start.13) | collective-permute-done | bytes 131104 | tf_op jit(solution)/shard_map/ppermute | solution.py:77
  61.8 0.1 add_convert_fusion
  61.8 0.1 collective-permute-start.14
  61.9 1.3 %collective-permute-done.14 = bf16[16,4096]{1,0:T(8,128)(2,1)S(1)} collective-permute-done((bf16[16,4096]{1,0:T(8,128)(2,1)S(1)}, bf16[16,4096]{1,0:T(8,128)(2,1)S(1)}, u32[]{:S(2)}, u32[]{:S(2)}) %collective-permute-start.14) | collective-permute-done | bytes 131104 | tf_op jit(solution)/shard_map/ppermute | solution.py:77
  63.3 0.7 %pad_maximum_fusion = bf16[32,4096]{1,0:T(8,128)(2,1)} fusion(bf16[16,4096]{1,0:T(8,128)(2,1)S(1)} %get-tuple-element.36, bf16[16,4096]{1,0:T(8,128)(2,1)S(1)} %get-tuple-element.35), kind=kLoop, calls=%fused_computation | loop fusion | flops 524288 | bytes 524288 | tf_op jit(solution)/shard_map/concatenate | solution.py:409
  (39 shorter events, 0.2 us)
Async XLA Ops:
  8.0 11.5 %collective-permute-start = (f32[8,2432]{1,0:T(8,128)}, f32[8,2432]{1,0:T(8,128)S(1)}, u32[]{:S(2)}, u32[]{:S(2)}) collective-permute-start(f32[8,2432]{1,0:T(8,128)} %get-tuple-element.21), channel_id=1, source_target_pairs={{0,12},{4,8},{8,4},{12,0},{1,13},{5,9},{9,5},{13,1},{2,14},{6,10},... | collective-permute-start | bytes 233480 | tf_op jit(solution)/shard_map/ppermute | solution.py:39
  13.1 6.4 %collective-permute-start.1 = (f32[8,2432]{1,0:T(8,128)}, f32[8,2432]{1,0:T(8,128)S(1)}, u32[]{:S(2)}, u32[]{:S(2)}) collective-permute-start(f32[8,2432]{1,0:T(8,128)} %get-tuple-element.22), channel_id=1, source_target_pairs={{0,4},{4,0},{8,12},{12,8},{1,5},{5,1},{9,13},{13,9},{2,6},{6,2},{1... | collective-permute-start | bytes 233480 | tf_op jit(solution)/shard_map/ppermute | solution.py:39
  13.1 6.4 %collective-permute-start.2 = (f32[8,2432]{1,0:T(8,128)}, f32[8,2432]{1,0:T(8,128)S(1)}, u32[]{:S(2)}, u32[]{:S(2)}) collective-permute-start(f32[8,2432]{1,0:T(8,128)} %get-tuple-element.23), channel_id=1, source_target_pairs={{0,8},{4,12},{8,0},{12,4},{1,9},{5,13},{9,1},{13,5},{2,10},{6,14},... | collective-permute-start | bytes 233480 | tf_op jit(solution)/shard_map/ppermute | solution.py:39
  13.8 0.9 %copy-start.3 = (f32[8,2432]{1,0:T(8,128)S(1)}, f32[8,2432]{1,0:T(8,128)}, u32[]{:S(2)}) copy-start(f32[8,2432]{1,0:T(8,128)} %get-tuple-element.20._.refs_0_) | copy-start | bytes 233476
  14.7 4.8 %copy-start.7 = (f32[2048]{0:T(1024)S(1)}, f32[2048]{0:T(1024)}, u32[]{:S(2)}) copy-start(f32[2048]{0:T(1024)} %param.20) | copy-start | bytes 24580
  14.7 4.9 %copy-start.8 = (f32[256]{0:T(256)S(1)}, f32[256]{0:T(256)}, u32[]{:S(2)}) copy-start(f32[256]{0:T(256)} %param.22) | copy-start | bytes 3076
  14.7 15.0 %copy-start = (bf16[8,4,128,128]{3,2,1,0:T(8,128)(2,1)S(1)}, bf16[8,4,128,128]{3,2,1,0:T(8,128)(2,1)}, u32[]{:S(2)}) copy-start(bf16[8,4,128,128]{3,2,1,0:T(8,128)(2,1)} %refs_4_.1) | copy-start | bytes 3145732
  14.7 15.0 %copy-start.1 = (bf16[8,4,128,128]{3,2,1,0:T(8,128)(2,1)S(1)}, bf16[8,4,128,128]{3,2,1,0:T(8,128)(2,1)}, u32[]{:S(2)}) copy-start(bf16[8,4,128,128]{3,2,1,0:T(8,128)(2,1)} %refs_5_.1) | copy-start | bytes 3145732
  14.7 15.0 %copy-start.4 = (f32[8,4,128]{2,1,0:T(4,128)S(1)}, f32[8,4,128]{2,1,0:T(4,128)}, u32[]{:S(2)}) copy-start(f32[8,4,128]{2,1,0:T(4,128)} %param.25) | copy-start | bytes 49156
  14.7 15.0 %copy-start.5 = (f32[8,4,128]{2,1,0:T(4,128)S(1)}, f32[8,4,128]{2,1,0:T(4,128)}, u32[]{:S(2)}) copy-start(f32[8,4,128]{2,1,0:T(4,128)} %param.26) | copy-start | bytes 49156
  14.7 15.0 %copy-start.9 = (s32[8]{0:T(128)S(1)}, s32[8]{0:T(128)}, u32[]{:S(2)}) copy-start(s32[8]{0:T(128)} %refs_3_.1) | copy-start | bytes 100
  19.4 30.3 %copy-start.2 = (f32[1,32,4096]{2,1,0:T(8,128)S(1)}, f32[1,32,4096]{2,1,0:T(8,128)}, u32[]{:S(2)}) copy-start(f32[1,32,4096]{2,1,0:T(8,128)} %param.16) | copy-start | bytes 1572868
  19.5 30.3 %copy-start.6 = (f32[4096]{0:T(1024)S(1)}, f32[4096]{0:T(1024)}, u32[]{:S(2)}) copy-start(f32[4096]{0:T(1024)} %param.29) | copy-start | bytes 49156
  19.6 1.2 %collective-permute-start.3 = (bf16[8,2304]{1,0:T(8,128)(2,1)S(1)}, bf16[8,2304]{1,0:T(8,128)(2,1)S(1)}, u32[]{:S(2)}, u32[]{:S(2)}) collective-permute-start(bf16[8,2304]{1,0:T(8,128)(2,1)S(1)} %norm.1.mine), channel_id=1, source_target_pairs={{0,1},{1,0},{2,3},{3,2},{4,5},{5,4},{6,7},{7,6},{8,9},{9,8},{10,11... | collective-permute-start | bytes 110600 | tf_op jit(solution)/shard_map/ppermute | solution.py:77
  20.9 6.0 %collective-permute-start.4 = (bf16[2,8,2304]{2,1,0:T(8,128)(2,1)S(1)}, bf16[2,8,2304]{2,1,0:T(8,128)(2,1)S(1)}, u32[]{:S(2)}, u32[]{:S(2)}) collective-permute-start(bf16[2,8,2304]{2,1,0:T(8,128)(2,1)S(1)} %pair.2.refs_2_), channel_id=1, source_target_pairs={{1,4},{2,8},{3,12},{4,1},{6,9},{7,13},{8,2},{9,6},{11,14},{12,3},{... | collective-permute-start | bytes 221192 | tf_op jit(solution)/shard_map/ppermute | solution.py:72
  21.5 8.2 %collective-permute-start.5 = (bf16[2,8,2304]{2,1,0:T(8,128)(2,1)S(1)}, bf16[2,8,2304]{2,1,0:T(8,128)(2,1)S(1)}, u32[]{:S(2)}, u32[]{:S(2)}) collective-permute-start(bf16[2,8,2304]{2,1,0:T(8,128)(2,1)S(1)} %pair.2.refs_2_), channel_id=1, source_target_pairs={{0,8},{1,12},{2,0},{3,4},{4,9},{5,13},{6,1},{7,5},{8,10},{9,14},{1... | collective-permute-start | bytes 221192 | tf_op jit(solution)/shard_map/ppermute | solution.py:72
  31.8 7.2 %collective-permute-start.6 = (f16[136,128]{1,0:T(8,128)(2,1)S(1)}, f16[136,128]{1,0:T(8,128)(2,1)S(1)}, u32[]{:S(2)}, u32[]{:S(2)}) collective-permute-start(f16[136,128]{1,0:T(8,128)(2,1)S(1)} %convert_element_type.31), channel_id=1, source_target_pairs={{0,12},{4,8},{8,4},{12,0},{1,13},{5,9},{9,5},{13,1},{2,14},{6,10},... | collective-permute-start | bytes 104456 | tf_op jit(solution)/shard_map/ppermute | solution.py:39
  36.0 4.2 %collective-permute-start.7 = (f16[136,128]{1,0:T(8,128)(2,1)S(1)}, f16[136,128]{1,0:T(8,128)(2,1)S(1)}, u32[]{:S(2)}, u32[]{:S(2)}) collective-permute-start(f16[136,128]{1,0:T(8,128)(2,1)S(1)} %convert_element_type.33), channel_id=1, source_target_pairs={{0,4},{4,0},{8,12},{12,8},{1,5},{5,1},{9,13},{13,9},{2,6},{6,2},{1... | collective-permute-start | bytes 104456 | tf_op jit(solution)/shard_map/ppermute | solution.py:39
  36.1 5.2 %collective-permute-start.8 = (f16[136,128]{1,0:T(8,128)(2,1)S(1)}, f16[136,128]{1,0:T(8,128)(2,1)S(1)}, u32[]{:S(2)}, u32[]{:S(2)}) collective-permute-start(f16[136,128]{1,0:T(8,128)(2,1)S(1)} %convert_element_type.35), channel_id=1, source_target_pairs={{0,8},{4,12},{8,0},{12,4},{1,9},{5,13},{9,1},{13,5},{2,10},{6,14},... | collective-permute-start | bytes 104456 | tf_op jit(solution)/shard_map/ppermute | solution.py:39
  38.9 22.9 %copy-start.10 = (bf16[32,4096]{1,0:T(8,128)(2,1)S(1)}, bf16[32,4096]{1,0:T(8,128)(2,1)}, u32[]{:S(2)}) copy-start(bf16[32,4096]{1,0:T(8,128)(2,1)} %residual.1) | copy-start | bytes 786436
  41.6 1.3 %collective-permute-start.9 = (bf16[8,2048]{1,0:T(8,128)(2,1)S(1)}, bf16[8,2048]{1,0:T(8,128)(2,1)S(1)}, u32[]{:S(2)}, u32[]{:S(2)}) collective-permute-start(bf16[8,2048]{1,0:T(8,128)(2,1)S(1)} %merge.1.mine), channel_id=1, source_target_pairs={{0,1},{1,0},{2,3},{3,2},{4,5},{5,4},{6,7},{7,6},{8,9},{9,8},{10,11... | collective-permute-start | bytes 98312 | tf_op jit(solution)/shard_map/ppermute | solution.py:77
  42.9 4.6 %collective-permute-start.10 = (bf16[2,8,2048]{2,1,0:T(8,128)(2,1)S(1)}, bf16[2,8,2048]{2,1,0:T(8,128)(2,1)S(1)}, u32[]{:S(2)}, u32[]{:S(2)}) collective-permute-start(bf16[2,8,2048]{2,1,0:T(8,128)(2,1)S(1)} %pair.3.refs_2_), channel_id=1, source_target_pairs={{1,4},{2,8},{3,12},{4,1},{6,9},{7,13},{8,2},{9,6},{11,14},{12,3},{... | collective-permute-start | bytes 196616 | tf_op jit(solution)/shard_map/ppermute | solution.py:72
  43.5 6.2 %collective-permute-start.11 = (bf16[2,8,2048]{2,1,0:T(8,128)(2,1)S(1)}, bf16[2,8,2048]{2,1,0:T(8,128)(2,1)S(1)}, u32[]{:S(2)}, u32[]{:S(2)}) collective-permute-start(bf16[2,8,2048]{2,1,0:T(8,128)(2,1)S(1)} %pair.3.refs_2_), channel_id=1, source_target_pairs={{0,8},{1,12},{2,0},{3,4},{4,9},{5,13},{6,1},{7,5},{8,10},{9,14},{1... | collective-permute-start | bytes 196616 | tf_op jit(solution)/shard_map/ppermute | solution.py:72
  52.8 2.7 %collective-permute-start.12 = (f32[16,4096]{1,0:T(8,128)S(1)}, f32[16,4096]{1,0:T(8,128)S(1)}, u32[]{:S(2)}, u32[]{:S(2)}) collective-permute-start(f32[16,4096]{1,0:T(8,128)S(1)} %get-tuple-element.32), channel_id=1, source_target_pairs={{0,1},{1,0},{2,3},{3,2},{4,5},{5,4},{6,7},{7,6},{8,9},{9,8},{10,11... | collective-permute-start | bytes 786440 | tf_op jit(solution)/shard_map/ppermute | solution.py:77
  55.6 6.2 %collective-permute-start.13 = (f16[16,4096]{1,0:T(8,128)(2,1)S(1)}, f16[16,4096]{1,0:T(8,128)(2,1)S(1)}, u32[]{:S(2)}, u32[]{:S(2)}) collective-permute-start(f16[16,4096]{1,0:T(8,128)(2,1)S(1)} %get-tuple-element.33), channel_id=1, source_target_pairs={{0,2},{1,3},{2,0},{3,1},{4,6},{5,7},{6,4},{7,5},{8,10},{9,11},{10,... | collective-permute-start | bytes 393224 | tf_op jit(solution)/shard_map/ppermute | solution.py:77
  61.8 1.4 %collective-permute-start.14 = (bf16[16,4096]{1,0:T(8,128)(2,1)S(1)}, bf16[16,4096]{1,0:T(8,128)(2,1)S(1)}, u32[]{:S(2)}, u32[]{:S(2)}) collective-permute-start(bf16[16,4096]{1,0:T(8,128)(2,1)S(1)} %add_convert_fusion), channel_id=1, source_target_pairs={{0,1},{1,0},{2,3},{3,2},{4,5},{5,4},{6,7},{7,6},{8,9},{9,8},{10,11... | collective-permute-start | bytes 393224 | tf_op jit(solution)/shard_map/ppermute | solution.py:77

commit v7 on v6

--- a/solution.py
+++ b/solution.py
@@ -16,7 +16,9 @@
 NEGATIVE = -1e30
 LANES = 128
 LOWEST = -4e7
-UNITS = (32768.0, 16.0, 0.0078125)
+TOP_UNITS = (32768.0, 16.0, 0.0078125)
+TOTAL_UNITS = (1.0, 0.0009765625)
+STATISTICS = len(TOP_UNITS) + len(TOTAL_UNITS) + 2
 SHRINK = 32.0
 f32 = jnp.float32
 bf16 = jnp.bfloat16
@@ -36,16 +38,16 @@
 
 
 def trade(chunks, axis, n):
-    return [chunks[0]] + [lax.ppermute(chunks[k], axis, partners(n, k)) for k in (3, 1, 2)]
+    return [chunks[0]] + [lax.ppermute(chunks[k], axis, partners(n, k)) for k in [n - 1, *range(1, n - 1)]]
 
 
 def place(placed, pieces, n):
     gx = lax.axis_index("gx")
     for k in range(n // 2):
         for core in range(2):
-            placed[2 * ((gx // 2) ^ k) + core] = pieces[k][core].astype(f32)
-
-    @pl.when(gx == lax.axis_index("gy"))
+            placed[2 * ((gx & 1) ^ k) + core] = pieces[k][core].astype(f32)
+
+    @pl.when((gx == lax.axis_index("gy")) & (gx // 2 == (gx & 1)))
     def _():
         for core in range(2):
             placed[2 * (gx // 2) + core] = pieces[n // 2][core].astype(f32)
@@ -68,7 +70,7 @@
     )(value, swap(value, "gy", n, 1))
     pieces = []
     for k in range(n // 2):
-        pairs = [(a * n + b, (b % 2 + 2 * ((b // 2) ^ k)) * n + a) for a in range(n) for b in range(n)]
+        pairs = [(a * n + b, (2 * (b % 2) + ((b // 2) ^ k)) * n + a) for a in range(n) for b in range(n)]
         pieces.append(lax.ppermute(pair, ("gx", "gy"), [p for p in pairs if p[0] != p[1]]))
     return pieces + [pair]
 
@@ -276,7 +278,7 @@
                 jnp.sum(jnp.where(diagonal, jnp.concatenate(kind[p][b * wide : (b + 1) * wide], axis=0), 0.0), axis=0, keepdims=True)
                 for kind in (tops, totals)
             ]
-            rows += digits(jnp.maximum(top, LOWEST), UNITS) + digits(total, (1.0,))
+            rows += digits(jnp.maximum(top, LOWEST), TOP_UNITS) + digits(total, TOTAL_UNITS)
         spare = messages.shape[1] - count - len(rows)
         messages[p, count:, :] = jnp.concatenate(rows + [jnp.zeros((spare, LANES), f32)], axis=0)
     for k in range(n):
@@ -286,7 +288,7 @@
 def attend(n, pieces, lengths, keys, values, key_scale, value_scale):
     requests, _, local, _ = keys.shape
     count = requests * GROUP
-    height = count + -(-(len(UNITS) + 3) * (count // LANES) // 8) * 8
+    height = count + -(-STATISTICS * (count // LANES) // 8) * 8
     return pl.pallas_call(
         functools.partial(attend_kernel, n),
         in_specs=[VMEM] * len(pieces) + [SMEM, VMEM, VMEM, VMEM, VMEM],
@@ -312,10 +314,10 @@
     blocks = count // LANES
     for b in range(blocks):
         at = slice(b * LANES, (b + 1) * LANES)
-        first, size = count + b * (len(UNITS) + 3), len(UNITS) + 1
-        rows = [[part[first + i : first + i + 1, :] for i in range(size + 2)] for part in parts]
-        tops = [joined_digits(row[:size], UNITS) for row in rows]
-        totals = [joined_digits(row[size:], (1.0,)) for row in rows]
+        first, size = count + b * STATISTICS, len(TOP_UNITS) + 1
+        rows = [[part[first + i : first + i + 1, :] for i in range(STATISTICS)] for part in parts]
+        tops = [joined_digits(row[:size], TOP_UNITS) for row in rows]
+        totals = [joined_digits(row[size:], TOTAL_UNITS) for row in rows]
         largest = tops[0]
         for top in tops[1:]:
             largest = jnp.maximum(largest, top)
@@ -388,7 +390,7 @@
     rows = residual.shape[0]
     requests = rows // n_gy
     parts = project(n_gx, residual, norm_gain, smooth_scale, w_query, w_keyval)
-    head = w_out.shape[0] * 6 // 8
+    head = w_out.shape[0] * 11 // 16
     upper = fetch(parts[0], w_out, 0, head)
     total = trade(parts, "gx", n_gx)
     total[0], upper = lax.optimization_barrier((total[0], upper))

time: 64.2 us -> 63.6 us (level)
  starting transfers between devices: 25.1 us -> 21.9 us
  waiting for transfers between devices: 16.5 us -> 19.1 us
    ppermute x4, starting transfers between devices: 10.5 us -> 7.51 us  [spread(): lax.ppermute(pair, ('gx', 'gy'), [p for p in pairs if p[0] != p[1]])]
    ppermute x4, waiting for transfers between devices: 5.2 us -> 7.64 us  [spread(): lax.ppermute(pair, ('gx', 'gy'), [p for p in pairs if p[0] != p[1]])]
    ppermute x5, starting transfers between devices: 3.92 us -> 2.77 us  [swap(): return lax.ppermute(value, axis, partners(n, offset))]
    ppermute x6, starting transfers between devices: 10.7 us -> 11.6 us  [trade(): lax.ppermute(chunks[k], axis, partners(n, k))]
  transfers between devices with their start and end apart: 15 -> 15, of which waited for: 9 -> 10; matrix products, arithmetic and copies ran while one was open for 0% -> 0% of each run, Pallas kernels for 11% -> 11%
where the time goes in v7:
time: 63.6 us; the launch traced here: 63.4 us
  starting transfers between devices  21.9 us (34%)
  Pallas kernels  20.3 us (32%)
  waiting for transfers between devices  19.1 us (30%)
  local copies, waits for them, and re-layouts  0.94 us (1%)
  other arithmetic  0.88 us (1%)
    ppermute x6, starting transfers between devices, trade(): lax.ppermute(chunks[k], axis, partners(n, k))  11.6 us
    ppermute x5, waiting for transfers between devices, swap(): return lax.ppermute(value, axis, partners(n, offset))  9.27 us
    pallas_call x1, Pallas kernels, project(): pl.pallas_call(functools.partial(project_kernel, n), in_specs=[HBM] * 5,...  8.01 us
    ppermute x4, waiting for transfers between devices, spread(): lax.ppermute(pair, ('gx', 'gy'), [p for p in pairs if p[0] != p[1]])  7.64 us
    ppermute x4, starting transfers between devices, spread(): lax.ppermute(pair, ('gx', 'gy'), [p for p in pairs if p[0] != p[1]])  7.51 us
    pallas_call x2, Pallas kernels, fetch(): pl.pallas_call(functools.partial(fetch_kernel, first), in_specs=[ANY, HBM...  6.93 us
    pallas_call x1, Pallas kernels, output(): pl.pallas_call(functools.partial(output_kernel, n), in_specs=[VMEM] * (le...  3.04 us
    ppermute x5, starting transfers between devices, swap(): return lax.ppermute(value, axis, partners(n, offset))  2.77 us
  transfers between devices with their start and end apart: 15, of which 10 were waited for; matrix products, arithmetic and copies ran while one was open for 0% of the time, Pallas kernels for 11%

profile of v7, /device:TPU:0, one launch (start us, length us, event | category | flops | bytes accessed | tf_op | source)
XLA Modules:
  0.0 63.4 jit_solution(15376223920110663647)
XLA Ops:
  0.0 8.0 %project.1 = (f32[8,2432]{1,0:T(8,128)}, f32[8,2432]{1,0:T(8,128)}, f32[8,2432]{1,0:T(8,128)}, f32[8,2432]{1,0:T(8,128)}) custom-call(bf16[32,4096]{1,0:T(8,128)(2,1)} %residual.1, f32[32,128]{1,0:T(8,128)} %bitcast.14, f32[32,128]{1,0:T(8,128)} %bitcast.15, bf16[4096,2048]{1,0:T(8,128)(2,1)} %w_query.1, bf16[4096,256]{1,0:T(8,128)(2,1)} %w_keyval.1), custom_call_target="tpu_custom_call" | custom-call | tf_op jit(solution)/shard_map/project/pallas_call | solution.py:139
  8.0 5.1 %collective-permute-start = (f32[8,2432]{1,0:T(8,128)}, f32[8,2432]{1,0:T(8,128)S(1)}, u32[]{:S(2)}, u32[]{:S(2)}) collective-permute-start(f32[8,2432]{1,0:T(8,128)} %get-tuple-element.21), channel_id=1, source_target_pairs={{0,12},{4,8},{8,4},{12,0},{1,13},{5,9},{9,5},{13,1},{2,14},{6,10},... | collective-permute-start | bytes 233480 | tf_op jit(solution)/shard_map/ppermute | solution.py:41
  13.1 0.6 %collective-permute-start.2 = (f32[8,2432]{1,0:T(8,128)}, f32[8,2432]{1,0:T(8,128)S(1)}, u32[]{:S(2)}, u32[]{:S(2)}) collective-permute-start(f32[8,2432]{1,0:T(8,128)} %get-tuple-element.23), channel_id=1, source_target_pairs={{0,8},{4,12},{8,0},{12,4},{1,9},{5,13},{9,1},{13,5},{2,10},{6,14},... | collective-permute-start | bytes 233480 | tf_op jit(solution)/shard_map/ppermute | solution.py:41
  13.8 0.9 %copy-done.3 = f32[8,2432]{1,0:T(8,128)S(1)} copy-done((f32[8,2432]{1,0:T(8,128)S(1)}, f32[8,2432]{1,0:T(8,128)}, u32[]{:S(2)}) %copy-start.3) | copy-done | bytes 77848
  14.7 4.4 %fetch.2.refs_3_ = bf16[1408,4096]{1,0:T(8,128)(2,1)S(1)} custom-call(f32[8,2432]{1,0:T(8,128)S(1)} %copy-done.3, bf16[2048,4096]{1,0:T(8,128)(2,1)} %source.3), custom_call_target="tpu_custom_call" | custom-call | bytes 23068672 | tf_op jit(solution)/shard_map/fetch/pallas_call | solution.py:197
  19.2 0.2 collective-permute-done.1.refs_2_
  19.4 0.1 norm.1.mine
  19.5 1.2 %collective-permute-done.3.other = bf16[8,2304]{1,0:T(8,128)(2,1)S(1)} collective-permute-done((bf16[8,2304]{1,0:T(8,128)(2,1)S(1)}, bf16[8,2304]{1,0:T(8,128)(2,1)S(1)}, u32[]{:S(2)}, u32[]{:S(2)}) %collective-permute-start.3) | collective-permute-done | bytes 36896 | tf_op jit(solution)/shard_map/ppermute | solution.py:79
  20.7 0.7 %collective-permute-start.4 = (bf16[2,8,2304]{2,1,0:T(8,128)(2,1)S(1)}, bf16[2,8,2304]{2,1,0:T(8,128)(2,1)S(1)}, u32[]{:S(2)}, u32[]{:S(2)}) collective-permute-start(bf16[2,8,2304]{2,1,0:T(8,128)(2,1)S(1)} %pair.2.refs_2_), channel_id=1, source_target_pairs={{1,8},{2,4},{3,12},{4,1},{5,9},{6,5},{7,13},{8,2},{9,10},{10,6},{1... | collective-permute-start | bytes 221192 | tf_op jit(solution)/shard_map/ppermute | solution.py:74
  21.4 3.1 %collective-permute-start.5 = (bf16[2,8,2304]{2,1,0:T(8,128)(2,1)S(1)}, bf16[2,8,2304]{2,1,0:T(8,128)(2,1)S(1)}, u32[]{:S(2)}, u32[]{:S(2)}) collective-permute-start(bf16[2,8,2304]{2,1,0:T(8,128)(2,1)S(1)} %pair.2.refs_2_), channel_id=1, source_target_pairs={{0,4},{1,12},{2,0},{3,8},{4,5},{5,13},{6,1},{7,9},{8,6},{9,14},{10... | collective-permute-start | bytes 221192 | tf_op jit(solution)/shard_map/ppermute | solution.py:74
  24.5 3.3 %collective-permute-done.5.refs_1_ = bf16[2,8,2304]{2,1,0:T(8,128)(2,1)S(1)} collective-permute-done((bf16[2,8,2304]{2,1,0:T(8,128)(2,1)S(1)}, bf16[2,8,2304]{2,1,0:T(8,128)(2,1)S(1)}, u32[]{:S(2)}, u32[]{:S(2)}) %collective-permute-start.5) | collective-permute-done | bytes 73760 | tf_op jit(solution)/shard_map/ppermute | solution.py:74
  27.8 2.0 %attend.1 = (f32[136,128]{1,0:T(8,128)S(1)}, f32[136,128]{1,0:T(8,128)S(1)}, f32[136,128]{1,0:T(8,128)S(1)}, f32[136,128]{1,0:T(8,128)S(1)}) custom-call(bf16[2,8,2304]{2,1,0:T(8,128)(2,1)S(1)} %collective-permute-done.4.refs_0_, bf16[2,8,2304]{2,1,0:T(8,128)(2,1)S(1)} %collective-permute-done.5.refs_1_, bf16[2,8,2304]{2,1,0:T(8,128)(2,1)S(1)} %pair.2.refs_2_, ...), custom_call_target="tpu_custom_call" | custom-call | tf_op jit(solution)/shard_map/attend/pallas_call | solution.py:292
  29.9 5.2 %collective-permute-start.6 = (f16[136,128]{1,0:T(8,128)(2,1)S(1)}, f16[136,128]{1,0:T(8,128)(2,1)S(1)}, u32[]{:S(2)}, u32[]{:S(2)}) collective-permute-start(f16[136,128]{1,0:T(8,128)(2,1)S(1)} %convert_element_type.31), channel_id=1, source_target_pairs={{0,12},{4,8},{8,4},{12,0},{1,13},{5,9},{9,5},{13,1},{2,14},{6,10},... | collective-permute-start | bytes 104456 | tf_op jit(solution)/shard_map/ppermute | solution.py:41
  35.1 0.4 collective-permute-start.7
  35.5 0.3 collective-permute-start.8
  35.8 2.5 %fetch.3.refs_4_ = bf16[640,4096]{1,0:T(8,128)(2,1)S(1)} custom-call(f32[136,128]{1,0:T(8,128)S(1)} %get-tuple-element.25._.refs_0_, bf16[2048,4096]{1,0:T(8,128)(2,1)} %source.3), custom_call_target="tpu_custom_call" | custom-call | bytes 10485760 | tf_op jit(solution)/shard_map/fetch/pallas_call | solution.py:197
  38.3 1.1 %collective-permute-done.7 = f16[136,128]{1,0:T(8,128)(2,1)S(1)} collective-permute-done((f16[136,128]{1,0:T(8,128)(2,1)S(1)}, f16[136,128]{1,0:T(8,128)(2,1)S(1)}, u32[]{:S(2)}, u32[]{:S(2)}) %collective-permute-start.7) | collective-permute-done | bytes 34848 | tf_op jit(solution)/shard_map/ppermute | solution.py:41
  39.4 0.9 %collective-permute-done.8 = f16[136,128]{1,0:T(8,128)(2,1)S(1)} collective-permute-done((f16[136,128]{1,0:T(8,128)(2,1)S(1)}, f16[136,128]{1,0:T(8,128)(2,1)S(1)}, u32[]{:S(2)}, u32[]{:S(2)}) %collective-permute-start.8) | collective-permute-done | bytes 34848 | tf_op jit(solution)/shard_map/ppermute | solution.py:41
  40.4 0.2 merge.1.mine
  40.6 0.1 collective-permute-start.9
  40.6 1.2 %collective-permute-done.9.other = bf16[8,2048]{1,0:T(8,128)(2,1)S(1)} collective-permute-done((bf16[8,2048]{1,0:T(8,128)(2,1)S(1)}, bf16[8,2048]{1,0:T(8,128)(2,1)S(1)}, u32[]{:S(2)}, u32[]{:S(2)}) %collective-permute-start.9) | collective-permute-done | bytes 32800 | tf_op jit(solution)/shard_map/ppermute | solution.py:79
  41.9 0.7 %collective-permute-start.10 = (bf16[2,8,2048]{2,1,0:T(8,128)(2,1)S(1)}, bf16[2,8,2048]{2,1,0:T(8,128)(2,1)S(1)}, u32[]{:S(2)}, u32[]{:S(2)}) collective-permute-start(bf16[2,8,2048]{2,1,0:T(8,128)(2,1)S(1)} %pair.3.refs_2_), channel_id=1, source_target_pairs={{1,8},{2,4},{3,12},{4,1},{5,9},{6,5},{7,13},{8,2},{9,10},{10,6},{1... | collective-permute-start | bytes 196616 | tf_op jit(solution)/shard_map/ppermute | solution.py:74
  42.5 3.1 %collective-permute-start.11 = (bf16[2,8,2048]{2,1,0:T(8,128)(2,1)S(1)}, bf16[2,8,2048]{2,1,0:T(8,128)(2,1)S(1)}, u32[]{:S(2)}, u32[]{:S(2)}) collective-permute-start(bf16[2,8,2048]{2,1,0:T(8,128)(2,1)S(1)} %pair.3.refs_2_), channel_id=1, source_target_pairs={{0,4},{1,12},{2,0},{3,8},{4,5},{5,13},{6,1},{7,9},{8,6},{9,14},{10... | collective-permute-start | bytes 196616 | tf_op jit(solution)/shard_map/ppermute | solution.py:74
  45.6 4.3 %collective-permute-done.11.refs_1_ = bf16[2,8,2048]{2,1,0:T(8,128)(2,1)S(1)} collective-permute-done((bf16[2,8,2048]{2,1,0:T(8,128)(2,1)S(1)}, bf16[2,8,2048]{2,1,0:T(8,128)(2,1)S(1)}, u32[]{:S(2)}, u32[]{:S(2)}) %collective-permute-start.11) | collective-permute-done | bytes 65568 | tf_op jit(solution)/shard_map/ppermute | solution.py:74
  49.9 3.0 %output.1 = (f32[16,4096]{1,0:T(8,128)S(1)}, f32[16,4096]{1,0:T(8,128)S(1)}) custom-call(bf16[2,8,2048]{2,1,0:T(8,128)(2,1)S(1)} %collective-permute-done.10.refs_0_, bf16[2,8,2048]{2,1,0:T(8,128)(2,1)S(1)} %collective-permute-done.11.refs_1_, bf16[2,8,2048]{2,1,0:T(8,128)(2,1)S(1)} %pair.3.refs_2_, bf16[1408,4096]{1,0:T(8,128)(2,1)S(1)} %fetch.2.refs_3_, ...), custom_call_target="tpu_custom_call" | custom-call | tf_op jit(solution)/shard_map/output/pallas_call | solution.py:376
  53.0 0.1 collective-permute-start.12
  53.1 1.5 %collective-permute-done.12 = f32[16,4096]{1,0:T(8,128)S(1)} collective-permute-done((f32[16,4096]{1,0:T(8,128)S(1)}, f32[16,4096]{1,0:T(8,128)S(1)}, u32[]{:S(2)}, u32[]{:S(2)}) %collective-permute-start.12) | collective-permute-done | bytes 262176 | tf_op jit(solution)/shard_map/ppermute | solution.py:79
  54.6 2.5 %collective-permute-start.13 = (f16[16,4096]{1,0:T(8,128)(2,1)S(1)}, f16[16,4096]{1,0:T(8,128)(2,1)S(1)}, u32[]{:S(2)}, u32[]{:S(2)}) collective-permute-start(f16[16,4096]{1,0:T(8,128)(2,1)S(1)} %get-tuple-element.33), channel_id=1, source_target_pairs={{0,2},{1,3},{2,0},{3,1},{4,6},{5,7},{6,4},{7,5},{8,10},{9,11},{10,... | collective-permute-start | bytes 393224 | tf_op jit(solution)/shard_map/ppermute | solution.py:79
  57.2 4.0 %collective-permute-done.13 = f16[16,4096]{1,0:T(8,128)(2,1)S(1)} collective-permute-done((f16[16,4096]{1,0:T(8,128)(2,1)S(1)}, f16[16,4096]{1,0:T(8,128)(2,1)S(1)}, u32[]{:S(2)}, u32[]{:S(2)}) %collective-permute-start.13) | collective-permute-done | bytes 131104 | tf_op jit(solution)/shard_map/ppermute | solution.py:79
  61.2 0.1 collective-permute-start.14
  61.3 1.3 %collective-permute-done.14 = bf16[16,4096]{1,0:T(8,128)(2,1)S(1)} collective-permute-done((bf16[16,4096]{1,0:T(8,128)(2,1)S(1)}, bf16[16,4096]{1,0:T(8,128)(2,1)S(1)}, u32[]{:S(2)}, u32[]{:S(2)}) %collective-permute-start.14) | collective-permute-done | bytes 131104 | tf_op jit(solution)/shard_map/ppermute | solution.py:79
  62.7 0.7 %pad_maximum_fusion = bf16[32,4096]{1,0:T(8,128)(2,1)} fusion(bf16[16,4096]{1,0:T(8,128)(2,1)S(1)} %get-tuple-element.36, bf16[16,4096]{1,0:T(8,128)(2,1)S(1)} %get-tuple-element.35), kind=kLoop, calls=%fused_computation | loop fusion | flops 524288 | bytes 524288 | tf_op jit(solution)/shard_map/concatenate | solution.py:411
  (39 shorter events, 0.3 us)
Async XLA Ops:
  8.0 11.1 %collective-permute-start = (f32[8,2432]{1,0:T(8,128)}, f32[8,2432]{1,0:T(8,128)S(1)}, u32[]{:S(2)}, u32[]{:S(2)}) collective-permute-start(f32[8,2432]{1,0:T(8,128)} %get-tuple-element.21), channel_id=1, source_target_pairs={{0,12},{4,8},{8,4},{12,0},{1,13},{5,9},{9,5},{13,1},{2,14},{6,10},... | collective-permute-start | bytes 233480 | tf_op jit(solution)/shard_map/ppermute | solution.py:41
  13.1 6.2 %collective-permute-start.1 = (f32[8,2432]{1,0:T(8,128)}, f32[8,2432]{1,0:T(8,128)S(1)}, u32[]{:S(2)}, u32[]{:S(2)}) collective-permute-start(f32[8,2432]{1,0:T(8,128)} %get-tuple-element.22), channel_id=1, source_target_pairs={{0,4},{4,0},{8,12},{12,8},{1,5},{5,1},{9,13},{13,9},{2,6},{6,2},{1... | collective-permute-start | bytes 233480 | tf_op jit(solution)/shard_map/ppermute | solution.py:41
  13.1 6.2 %collective-permute-start.2 = (f32[8,2432]{1,0:T(8,128)}, f32[8,2432]{1,0:T(8,128)S(1)}, u32[]{:S(2)}, u32[]{:S(2)}) collective-permute-start(f32[8,2432]{1,0:T(8,128)} %get-tuple-element.23), channel_id=1, source_target_pairs={{0,8},{4,12},{8,0},{12,4},{1,9},{5,13},{9,1},{13,5},{2,10},{6,14},... | collective-permute-start | bytes 233480 | tf_op jit(solution)/shard_map/ppermute | solution.py:41
  13.8 0.9 %copy-start.3 = (f32[8,2432]{1,0:T(8,128)S(1)}, f32[8,2432]{1,0:T(8,128)}, u32[]{:S(2)}) copy-start(f32[8,2432]{1,0:T(8,128)} %get-tuple-element.20._.refs_0_) | copy-start | bytes 233476
  14.7 4.7 %copy-start.7 = (f32[2048]{0:T(1024)S(1)}, f32[2048]{0:T(1024)}, u32[]{:S(2)}) copy-start(f32[2048]{0:T(1024)} %param.20) | copy-start | bytes 24580
  14.7 4.7 %copy-start.8 = (f32[256]{0:T(256)S(1)}, f32[256]{0:T(256)}, u32[]{:S(2)}) copy-start(f32[256]{0:T(256)} %param.22) | copy-start | bytes 3076
  14.7 13.1 %copy-start = (bf16[8,4,128,128]{3,2,1,0:T(8,128)(2,1)S(1)}, bf16[8,4,128,128]{3,2,1,0:T(8,128)(2,1)}, u32[]{:S(2)}) copy-start(bf16[8,4,128,128]{3,2,1,0:T(8,128)(2,1)} %refs_4_.1) | copy-start | bytes 3145732
  14.7 13.1 %copy-start.1 = (bf16[8,4,128,128]{3,2,1,0:T(8,128)(2,1)S(1)}, bf16[8,4,128,128]{3,2,1,0:T(8,128)(2,1)}, u32[]{:S(2)}) copy-start(bf16[8,4,128,128]{3,2,1,0:T(8,128)(2,1)} %refs_5_.1) | copy-start | bytes 3145732
  14.7 13.1 %copy-start.4 = (f32[8,4,128]{2,1,0:T(4,128)S(1)}, f32[8,4,128]{2,1,0:T(4,128)}, u32[]{:S(2)}) copy-start(f32[8,4,128]{2,1,0:T(4,128)} %param.25) | copy-start | bytes 49156
  14.7 13.1 %copy-start.5 = (f32[8,4,128]{2,1,0:T(4,128)S(1)}, f32[8,4,128]{2,1,0:T(4,128)}, u32[]{:S(2)}) copy-start(f32[8,4,128]{2,1,0:T(4,128)} %param.26) | copy-start | bytes 49156
  14.7 13.1 %copy-start.9 = (s32[8]{0:T(128)S(1)}, s32[8]{0:T(128)}, u32[]{:S(2)}) copy-start(s32[8]{0:T(128)} %refs_3_.1) | copy-start | bytes 100
  19.4 1.2 %collective-permute-start.3 = (bf16[8,2304]{1,0:T(8,128)(2,1)S(1)}, bf16[8,2304]{1,0:T(8,128)(2,1)S(1)}, u32[]{:S(2)}, u32[]{:S(2)}) collective-permute-start(bf16[8,2304]{1,0:T(8,128)(2,1)S(1)} %norm.1.mine), channel_id=1, source_target_pairs={{0,1},{1,0},{2,3},{3,2},{4,5},{5,4},{6,7},{7,6},{8,9},{9,8},{10,11... | collective-permute-start | bytes 110600 | tf_op jit(solution)/shard_map/ppermute | solution.py:79
  20.7 3.8 %collective-permute-start.4 = (bf16[2,8,2304]{2,1,0:T(8,128)(2,1)S(1)}, bf16[2,8,2304]{2,1,0:T(8,128)(2,1)S(1)}, u32[]{:S(2)}, u32[]{:S(2)}) collective-permute-start(bf16[2,8,2304]{2,1,0:T(8,128)(2,1)S(1)} %pair.2.refs_2_), channel_id=1, source_target_pairs={{1,8},{2,4},{3,12},{4,1},{5,9},{6,5},{7,13},{8,2},{9,10},{10,6},{1... | collective-permute-start | bytes 221192 | tf_op jit(solution)/shard_map/ppermute | solution.py:74
  21.4 6.4 %collective-permute-start.5 = (bf16[2,8,2304]{2,1,0:T(8,128)(2,1)S(1)}, bf16[2,8,2304]{2,1,0:T(8,128)(2,1)S(1)}, u32[]{:S(2)}, u32[]{:S(2)}) collective-permute-start(bf16[2,8,2304]{2,1,0:T(8,128)(2,1)S(1)} %pair.2.refs_2_), channel_id=1, source_target_pairs={{0,4},{1,12},{2,0},{3,8},{4,5},{5,13},{6,1},{7,9},{8,6},{9,14},{10... | collective-permute-start | bytes 221192 | tf_op jit(solution)/shard_map/ppermute | solution.py:74
  29.8 20.1 %copy-start.2 = (f32[1,32,4096]{2,1,0:T(8,128)S(1)}, f32[1,32,4096]{2,1,0:T(8,128)}, u32[]{:S(2)}) copy-start(f32[1,32,4096]{2,1,0:T(8,128)} %param.16) | copy-start | bytes 1572868
  29.9 20.1 %copy-start.6 = (f32[4096]{0:T(1024)S(1)}, f32[4096]{0:T(1024)}, u32[]{:S(2)}) copy-start(f32[4096]{0:T(1024)} %param.29) | copy-start | bytes 49156
  29.9 8.4 %collective-permute-start.6 = (f16[136,128]{1,0:T(8,128)(2,1)S(1)}, f16[136,128]{1,0:T(8,128)(2,1)S(1)}, u32[]{:S(2)}, u32[]{:S(2)}) collective-permute-start(f16[136,128]{1,0:T(8,128)(2,1)S(1)} %convert_element_type.31), channel_id=1, source_target_pairs={{0,12},{4,8},{8,4},{12,0},{1,13},{5,9},{9,5},{13,1},{2,14},{6,10},... | collective-permute-start | bytes 104456 | tf_op jit(solution)/shard_map/ppermute | solution.py:41
  35.1 4.4 %collective-permute-start.7 = (f16[136,128]{1,0:T(8,128)(2,1)S(1)}, f16[136,128]{1,0:T(8,128)(2,1)S(1)}, u32[]{:S(2)}, u32[]{:S(2)}) collective-permute-start(f16[136,128]{1,0:T(8,128)(2,1)S(1)} %convert_element_type.33), channel_id=1, source_target_pairs={{0,4},{4,0},{8,12},{12,8},{1,5},{5,1},{9,13},{13,9},{2,6},{6,2},{1... | collective-permute-start | bytes 104456 | tf_op jit(solution)/shard_map/ppermute | solution.py:41
  35.5 4.9 %collective-permute-start.8 = (f16[136,128]{1,0:T(8,128)(2,1)S(1)}, f16[136,128]{1,0:T(8,128)(2,1)S(1)}, u32[]{:S(2)}, u32[]{:S(2)}) collective-permute-start(f16[136,128]{1,0:T(8,128)(2,1)S(1)} %convert_element_type.35), channel_id=1, source_target_pairs={{0,8},{4,12},{8,0},{12,4},{1,9},{5,13},{9,1},{13,5},{2,10},{6,14},... | collective-permute-start | bytes 104456 | tf_op jit(solution)/shard_map/ppermute | solution.py:41
  38.3 22.9 %copy-start.10 = (bf16[32,4096]{1,0:T(8,128)(2,1)S(1)}, bf16[32,4096]{1,0:T(8,128)(2,1)}, u32[]{:S(2)}) copy-start(bf16[32,4096]{1,0:T(8,128)(2,1)} %residual.1) | copy-start | bytes 786436
  40.6 1.3 %collective-permute-start.9 = (bf16[8,2048]{1,0:T(8,128)(2,1)S(1)}, bf16[8,2048]{1,0:T(8,128)(2,1)S(1)}, u32[]{:S(2)}, u32[]{:S(2)}) collective-permute-start(bf16[8,2048]{1,0:T(8,128)(2,1)S(1)} %merge.1.mine), channel_id=1, source_target_pairs={{0,1},{1,0},{2,3},{3,2},{4,5},{5,4},{6,7},{7,6},{8,9},{9,8},{10,11... | collective-permute-start | bytes 98312 | tf_op jit(solution)/shard_map/ppermute | solution.py:79
  41.9 3.8 %collective-permute-start.10 = (bf16[2,8,2048]{2,1,0:T(8,128)(2,1)S(1)}, bf16[2,8,2048]{2,1,0:T(8,128)(2,1)S(1)}, u32[]{:S(2)}, u32[]{:S(2)}) collective-permute-start(bf16[2,8,2048]{2,1,0:T(8,128)(2,1)S(1)} %pair.3.refs_2_), channel_id=1, source_target_pairs={{1,8},{2,4},{3,12},{4,1},{5,9},{6,5},{7,13},{8,2},{9,10},{10,6},{1... | collective-permute-start | bytes 196616 | tf_op jit(solution)/shard_map/ppermute | solution.py:74
  42.5 7.4 %collective-permute-start.11 = (bf16[2,8,2048]{2,1,0:T(8,128)(2,1)S(1)}, bf16[2,8,2048]{2,1,0:T(8,128)(2,1)S(1)}, u32[]{:S(2)}, u32[]{:S(2)}) collective-permute-start(bf16[2,8,2048]{2,1,0:T(8,128)(2,1)S(1)} %pair.3.refs_2_), channel_id=1, source_target_pairs={{0,4},{1,12},{2,0},{3,8},{4,5},{5,13},{6,1},{7,9},{8,6},{9,14},{10... | collective-permute-start | bytes 196616 | tf_op jit(solution)/shard_map/ppermute | solution.py:74
  53.0 1.6 %collective-permute-start.12 = (f32[16,4096]{1,0:T(8,128)S(1)}, f32[16,4096]{1,0:T(8,128)S(1)}, u32[]{:S(2)}, u32[]{:S(2)}) collective-permute-start(f32[16,4096]{1,0:T(8,128)S(1)} %get-tuple-element.32), channel_id=1, source_target_pairs={{0,1},{1,0},{2,3},{3,2},{4,5},{5,4},{6,7},{7,6},{8,9},{9,8},{10,11... | collective-permute-start | bytes 786440 | tf_op jit(solution)/shard_map/ppermute | solution.py:79
  54.6 6.6 %collective-permute-start.13 = (f16[16,4096]{1,0:T(8,128)(2,1)S(1)}, f16[16,4096]{1,0:T(8,128)(2,1)S(1)}, u32[]{:S(2)}, u32[]{:S(2)}) collective-permute-start(f16[16,4096]{1,0:T(8,128)(2,1)S(1)} %get-tuple-element.33), channel_id=1, source_target_pairs={{0,2},{1,3},{2,0},{3,1},{4,6},{5,7},{6,4},{7,5},{8,10},{9,11},{10,... | collective-permute-start | bytes 393224 | tf_op jit(solution)/shard_map/ppermute | solution.py:79
  61.2 1.4 %collective-permute-start.14 = (bf16[16,4096]{1,0:T(8,128)(2,1)S(1)}, bf16[16,4096]{1,0:T(8,128)(2,1)S(1)}, u32[]{:S(2)}, u32[]{:S(2)}) collective-permute-start(bf16[16,4096]{1,0:T(8,128)(2,1)S(1)} %add_convert_fusion), channel_id=1, source_target_pairs={{0,1},{1,0},{2,3},{3,2},{4,5},{5,4},{6,7},{7,6},{8,9},{9,8},{10,11... | collective-permute-start | bytes 393224 | tf_op jit(solution)/shard_map/ppermute | solution.py:79

commit v8 on v7

--- a/solution.py
+++ b/solution.py
@@ -19,6 +19,7 @@
 TOP_UNITS = (32768.0, 16.0, 0.0078125)
 TOTAL_UNITS = (1.0, 0.0009765625)
 STATISTICS = len(TOP_UNITS) + len(TOTAL_UNITS) + 2
+PORTIONS = (3, 3, 3, 3, 2, 1, 1)
 SHRINK = 32.0
 f32 = jnp.float32
 bf16 = jnp.bfloat16
@@ -88,8 +89,9 @@
     x_buf, g_buf, s_buf, q_buf, k_buf, smoothed, q_sum, k_sum, squares_sum, sems, big_sems = rest[n:]
     rows, width = x_buf.shape
     queries = w_query.shape[1]
-    steps = big_sems.shape[0] - 1
-    depth = width // steps
+    steps = len(PORTIONS)
+    ends = [sum(PORTIONS[: i + 1]) * width // sum(PORTIONS) for i in range(steps)]
+    starts = [0] + ends[:-1]
     small = [
         pltpu.make_async_copy(source, target, sems.at[i])
         for i, (source, target) in enumerate([(residual, x_buf), (gain, g_buf), (smooth, s_buf)])
@@ -98,10 +100,10 @@
         copy.start()
     large = []
     for i in range(steps):
-        part = pl.ds(i * depth, depth)
+        part = pl.ds(starts[i], ends[i] - starts[i])
         large.append(pltpu.make_async_copy(w_query.at[part], q_buf.at[part], big_sems.at[i]))
-    large.append(pltpu.make_async_copy(w_keyval, k_buf, big_sems.at[steps]))
-    for copy in large:
+    weights = pltpu.make_async_copy(w_keyval, k_buf, big_sems.at[steps])
+    for copy in large[:2] + [weights] + large[2:]:
         copy.start(priority=1)
     for copy in small:
         copy.wait()
@@ -113,15 +115,16 @@
         smoothed[:, lanes] = (x * (g_buf[i : i + 1, :] / s_buf[i : i + 1, :])).astype(bf16)
     squares_sum[...] = jnp.broadcast_to(jnp.sum(squares, axis=1, keepdims=True), (rows, LANES))
     for i in range(steps):
-        part = slice(i * depth, (i + 1) * depth)
+        part = slice(starts[i], ends[i])
+        if i == 2:
+            weights.wait()
+            k_sum[...] = jnp.dot(smoothed[...], k_buf[...], preferred_element_type=f32)
         large[i].wait()
         term = jnp.dot(smoothed[:, part], q_buf[part, :], preferred_element_type=f32)
         if i == 0:
             q_sum[...] = term
         else:
             q_sum[...] += term
-    large[steps].wait()
-    k_sum[...] = jnp.dot(smoothed[...], k_buf[...], preferred_element_type=f32)
     me = lax.axis_index("gx")
     requests = rows // n
     columns = queries + k_buf.shape[1]
@@ -135,7 +138,7 @@
 def project(n, residual, gain, smooth, w_query, w_keyval):
     rows, width = residual.shape
     columns = w_query.shape[1] + w_keyval.shape[1]
-    steps = 8
+    steps = len(PORTIONS)
     return pl.pallas_call(
         functools.partial(project_kernel, n),
         in_specs=[HBM] * 5,

time: 63.6 us -> 63.2 us (level)
  no operation moved by 1% of the time
where the time goes in v8:
time: 63.2 us; the launch traced here: 63 us
  starting transfers between devices  21.9 us (35%)
  Pallas kernels  19.9 us (31%)
  waiting for transfers between devices  19.1 us (30%)
  local copies, waits for them, and re-layouts  0.94 us (1%)
  other arithmetic  0.88 us (1%)
    ppermute x6, starting transfers between devices, trade(): lax.ppermute(chunks[k], axis, partners(n, k))  11.6 us
    ppermute x5, waiting for transfers between devices, swap(): return lax.ppermute(value, axis, partners(n, offset))  9.27 us
    ppermute x4, waiting for transfers between devices, spread(): lax.ppermute(pair, ('gx', 'gy'), [p for p in pairs if p[0] != p[1]])  7.64 us
    pallas_call x1, Pallas kernels, project(): pl.pallas_call(functools.partial(project_kernel, n), in_specs=[HBM] * 5,...  7.59 us
    ppermute x4, starting transfers between devices, spread(): lax.ppermute(pair, ('gx', 'gy'), [p for p in pairs if p[0] != p[1]])  7.51 us
    pallas_call x2, Pallas kernels, fetch(): pl.pallas_call(functools.partial(fetch_kernel, first), in_specs=[ANY, HBM...  6.93 us
    pallas_call x1, Pallas kernels, output(): pl.pallas_call(functools.partial(output_kernel, n), in_specs=[VMEM] * (le...  3.05 us
    ppermute x5, starting transfers between devices, swap(): return lax.ppermute(value, axis, partners(n, offset))  2.77 us
  transfers between devices with their start and end apart: 15, of which 10 were waited for; matrix products, arithmetic and copies ran while one was open for 0% of the time, Pallas kernels for 11%

profile of v8, /device:TPU:0, one launch (start us, length us, event | category | flops | bytes accessed | tf_op | source)
XLA Modules:
  0.0 63.0 jit_solution(14269308163510380845)
XLA Ops:
  0.0 7.6 %project.1 = (f32[8,2432]{1,0:T(8,128)}, f32[8,2432]{1,0:T(8,128)}, f32[8,2432]{1,0:T(8,128)}, f32[8,2432]{1,0:T(8,128)}) custom-call(bf16[32,4096]{1,0:T(8,128)(2,1)} %residual.1, f32[32,128]{1,0:T(8,128)} %bitcast.14, f32[32,128]{1,0:T(8,128)} %bitcast.15, bf16[4096,2048]{1,0:T(8,128)(2,1)} %w_query.1, bf16[4096,256]{1,0:T(8,128)(2,1)} %w_keyval.1), custom_call_target="tpu_custom_call" | custom-call | tf_op jit(solution)/shard_map/project/pallas_call | solution.py:142
  7.6 5.1 %collective-permute-start = (f32[8,2432]{1,0:T(8,128)}, f32[8,2432]{1,0:T(8,128)S(1)}, u32[]{:S(2)}, u32[]{:S(2)}) collective-permute-start(f32[8,2432]{1,0:T(8,128)} %get-tuple-element.21), channel_id=1, source_target_pairs={{0,12},{4,8},{8,4},{12,0},{1,13},{5,9},{9,5},{13,1},{2,14},{6,10},... | collective-permute-start | bytes 233480 | tf_op jit(solution)/shard_map/ppermute | solution.py:42
  12.7 0.6 %collective-permute-start.2 = (f32[8,2432]{1,0:T(8,128)}, f32[8,2432]{1,0:T(8,128)S(1)}, u32[]{:S(2)}, u32[]{:S(2)}) collective-permute-start(f32[8,2432]{1,0:T(8,128)} %get-tuple-element.23), channel_id=1, source_target_pairs={{0,8},{4,12},{8,0},{12,4},{1,9},{5,13},{9,1},{13,5},{2,10},{6,14},... | collective-permute-start | bytes 233480 | tf_op jit(solution)/shard_map/ppermute | solution.py:42
  13.4 0.9 %copy-done.3 = f32[8,2432]{1,0:T(8,128)S(1)} copy-done((f32[8,2432]{1,0:T(8,128)S(1)}, f32[8,2432]{1,0:T(8,128)}, u32[]{:S(2)}) %copy-start.3) | copy-done | bytes 77848
  14.3 4.4 %fetch.2.refs_3_ = bf16[1408,4096]{1,0:T(8,128)(2,1)S(1)} custom-call(f32[8,2432]{1,0:T(8,128)S(1)} %copy-done.3, bf16[2048,4096]{1,0:T(8,128)(2,1)} %source.3), custom_call_target="tpu_custom_call" | custom-call | bytes 23068672 | tf_op jit(solution)/shard_map/fetch/pallas_call | solution.py:200
  18.7 0.2 collective-permute-done.1.refs_2_
  18.9 0.1 norm.1.mine
  19.1 1.2 %collective-permute-done.3.other = bf16[8,2304]{1,0:T(8,128)(2,1)S(1)} collective-permute-done((bf16[8,2304]{1,0:T(8,128)(2,1)S(1)}, bf16[8,2304]{1,0:T(8,128)(2,1)S(1)}, u32[]{:S(2)}, u32[]{:S(2)}) %collective-permute-start.3) | collective-permute-done | bytes 36896 | tf_op jit(solution)/shard_map/ppermute | solution.py:80
  20.3 0.7 %collective-permute-start.4 = (bf16[2,8,2304]{2,1,0:T(8,128)(2,1)S(1)}, bf16[2,8,2304]{2,1,0:T(8,128)(2,1)S(1)}, u32[]{:S(2)}, u32[]{:S(2)}) collective-permute-start(bf16[2,8,2304]{2,1,0:T(8,128)(2,1)S(1)} %pair.2.refs_2_), channel_id=1, source_target_pairs={{1,8},{2,4},{3,12},{4,1},{5,9},{6,5},{7,13},{8,2},{9,10},{10,6},{1... | collective-permute-start | bytes 221192 | tf_op jit(solution)/shard_map/ppermute | solution.py:75
  21.0 3.1 %collective-permute-start.5 = (bf16[2,8,2304]{2,1,0:T(8,128)(2,1)S(1)}, bf16[2,8,2304]{2,1,0:T(8,128)(2,1)S(1)}, u32[]{:S(2)}, u32[]{:S(2)}) collective-permute-start(bf16[2,8,2304]{2,1,0:T(8,128)(2,1)S(1)} %pair.2.refs_2_), channel_id=1, source_target_pairs={{0,4},{1,12},{2,0},{3,8},{4,5},{5,13},{6,1},{7,9},{8,6},{9,14},{10... | collective-permute-start | bytes 221192 | tf_op jit(solution)/shard_map/ppermute | solution.py:75
  24.1 3.3 %collective-permute-done.5.refs_1_ = bf16[2,8,2304]{2,1,0:T(8,128)(2,1)S(1)} collective-permute-done((bf16[2,8,2304]{2,1,0:T(8,128)(2,1)S(1)}, bf16[2,8,2304]{2,1,0:T(8,128)(2,1)S(1)}, u32[]{:S(2)}, u32[]{:S(2)}) %collective-permute-start.5) | collective-permute-done | bytes 73760 | tf_op jit(solution)/shard_map/ppermute | solution.py:75
  27.4 2.0 %attend.1 = (f32[136,128]{1,0:T(8,128)S(1)}, f32[136,128]{1,0:T(8,128)S(1)}, f32[136,128]{1,0:T(8,128)S(1)}, f32[136,128]{1,0:T(8,128)S(1)}) custom-call(bf16[2,8,2304]{2,1,0:T(8,128)(2,1)S(1)} %collective-permute-done.4.refs_0_, bf16[2,8,2304]{2,1,0:T(8,128)(2,1)S(1)} %collective-permute-done.5.refs_1_, bf16[2,8,2304]{2,1,0:T(8,128)(2,1)S(1)} %pair.2.refs_2_, ...), custom_call_target="tpu_custom_call" | custom-call | tf_op jit(solution)/shard_map/attend/pallas_call | solution.py:295
  29.5 5.2 %collective-permute-start.6 = (f16[136,128]{1,0:T(8,128)(2,1)S(1)}, f16[136,128]{1,0:T(8,128)(2,1)S(1)}, u32[]{:S(2)}, u32[]{:S(2)}) collective-permute-start(f16[136,128]{1,0:T(8,128)(2,1)S(1)} %convert_element_type.31), channel_id=1, source_target_pairs={{0,12},{4,8},{8,4},{12,0},{1,13},{5,9},{9,5},{13,1},{2,14},{6,10},... | collective-permute-start | bytes 104456 | tf_op jit(solution)/shard_map/ppermute | solution.py:42
  34.6 0.4 collective-permute-start.7
  35.0 0.3 collective-permute-start.8
  35.4 2.5 %fetch.3.refs_4_ = bf16[640,4096]{1,0:T(8,128)(2,1)S(1)} custom-call(f32[136,128]{1,0:T(8,128)S(1)} %get-tuple-element.25._.refs_0_, bf16[2048,4096]{1,0:T(8,128)(2,1)} %source.3), custom_call_target="tpu_custom_call" | custom-call | bytes 10485760 | tf_op jit(solution)/shard_map/fetch/pallas_call | solution.py:200
  37.9 1.1 %collective-permute-done.7 = f16[136,128]{1,0:T(8,128)(2,1)S(1)} collective-permute-done((f16[136,128]{1,0:T(8,128)(2,1)S(1)}, f16[136,128]{1,0:T(8,128)(2,1)S(1)}, u32[]{:S(2)}, u32[]{:S(2)}) %collective-permute-start.7) | collective-permute-done | bytes 34848 | tf_op jit(solution)/shard_map/ppermute | solution.py:42
  39.0 0.9 %collective-permute-done.8 = f16[136,128]{1,0:T(8,128)(2,1)S(1)} collective-permute-done((f16[136,128]{1,0:T(8,128)(2,1)S(1)}, f16[136,128]{1,0:T(8,128)(2,1)S(1)}, u32[]{:S(2)}, u32[]{:S(2)}) %collective-permute-start.8) | collective-permute-done | bytes 34848 | tf_op jit(solution)/shard_map/ppermute | solution.py:42
  39.9 0.2 merge.1.mine
  40.2 0.1 collective-permute-start.9
  40.2 1.2 %collective-permute-done.9.other = bf16[8,2048]{1,0:T(8,128)(2,1)S(1)} collective-permute-done((bf16[8,2048]{1,0:T(8,128)(2,1)S(1)}, bf16[8,2048]{1,0:T(8,128)(2,1)S(1)}, u32[]{:S(2)}, u32[]{:S(2)}) %collective-permute-start.9) | collective-permute-done | bytes 32800 | tf_op jit(solution)/shard_map/ppermute | solution.py:80
  41.4 0.7 %collective-permute-start.10 = (bf16[2,8,2048]{2,1,0:T(8,128)(2,1)S(1)}, bf16[2,8,2048]{2,1,0:T(8,128)(2,1)S(1)}, u32[]{:S(2)}, u32[]{:S(2)}) collective-permute-start(bf16[2,8,2048]{2,1,0:T(8,128)(2,1)S(1)} %pair.3.refs_2_), channel_id=1, source_target_pairs={{1,8},{2,4},{3,12},{4,1},{5,9},{6,5},{7,13},{8,2},{9,10},{10,6},{1... | collective-permute-start | bytes 196616 | tf_op jit(solution)/shard_map/ppermute | solution.py:75
  42.1 3.1 %collective-permute-start.11 = (bf16[2,8,2048]{2,1,0:T(8,128)(2,1)S(1)}, bf16[2,8,2048]{2,1,0:T(8,128)(2,1)S(1)}, u32[]{:S(2)}, u32[]{:S(2)}) collective-permute-start(bf16[2,8,2048]{2,1,0:T(8,128)(2,1)S(1)} %pair.3.refs_2_), channel_id=1, source_target_pairs={{0,4},{1,12},{2,0},{3,8},{4,5},{5,13},{6,1},{7,9},{8,6},{9,14},{10... | collective-permute-start | bytes 196616 | tf_op jit(solution)/shard_map/ppermute | solution.py:75
  45.2 4.3 %collective-permute-done.11.refs_1_ = bf16[2,8,2048]{2,1,0:T(8,128)(2,1)S(1)} collective-permute-done((bf16[2,8,2048]{2,1,0:T(8,128)(2,1)S(1)}, bf16[2,8,2048]{2,1,0:T(8,128)(2,1)S(1)}, u32[]{:S(2)}, u32[]{:S(2)}) %collective-permute-start.11) | collective-permute-done | bytes 65568 | tf_op jit(solution)/shard_map/ppermute | solution.py:75
  49.5 3.0 %output.1 = (f32[16,4096]{1,0:T(8,128)S(1)}, f32[16,4096]{1,0:T(8,128)S(1)}) custom-call(bf16[2,8,2048]{2,1,0:T(8,128)(2,1)S(1)} %collective-permute-done.10.refs_0_, bf16[2,8,2048]{2,1,0:T(8,128)(2,1)S(1)} %collective-permute-done.11.refs_1_, bf16[2,8,2048]{2,1,0:T(8,128)(2,1)S(1)} %pair.3.refs_2_, bf16[1408,4096]{1,0:T(8,128)(2,1)S(1)} %fetch.2.refs_3_, ...), custom_call_target="tpu_custom_call" | custom-call | tf_op jit(solution)/shard_map/output/pallas_call | solution.py:379
  52.6 0.1 collective-permute-start.12
  52.7 1.5 %collective-permute-done.12 = f32[16,4096]{1,0:T(8,128)S(1)} collective-permute-done((f32[16,4096]{1,0:T(8,128)S(1)}, f32[16,4096]{1,0:T(8,128)S(1)}, u32[]{:S(2)}, u32[]{:S(2)}) %collective-permute-start.12) | collective-permute-done | bytes 262176 | tf_op jit(solution)/shard_map/ppermute | solution.py:80
  54.2 2.5 %collective-permute-start.13 = (f16[16,4096]{1,0:T(8,128)(2,1)S(1)}, f16[16,4096]{1,0:T(8,128)(2,1)S(1)}, u32[]{:S(2)}, u32[]{:S(2)}) collective-permute-start(f16[16,4096]{1,0:T(8,128)(2,1)S(1)} %get-tuple-element.33), channel_id=1, source_target_pairs={{0,2},{1,3},{2,0},{3,1},{4,6},{5,7},{6,4},{7,5},{8,10},{9,11},{10,... | collective-permute-start | bytes 393224 | tf_op jit(solution)/shard_map/ppermute | solution.py:80
  56.8 4.0 %collective-permute-done.13 = f16[16,4096]{1,0:T(8,128)(2,1)S(1)} collective-permute-done((f16[16,4096]{1,0:T(8,128)(2,1)S(1)}, f16[16,4096]{1,0:T(8,128)(2,1)S(1)}, u32[]{:S(2)}, u32[]{:S(2)}) %collective-permute-start.13) | collective-permute-done | bytes 131104 | tf_op jit(solution)/shard_map/ppermute | solution.py:80
  60.8 0.1 collective-permute-start.14
  60.9 1.3 %collective-permute-done.14 = bf16[16,4096]{1,0:T(8,128)(2,1)S(1)} collective-permute-done((bf16[16,4096]{1,0:T(8,128)(2,1)S(1)}, bf16[16,4096]{1,0:T(8,128)(2,1)S(1)}, u32[]{:S(2)}, u32[]{:S(2)}) %collective-permute-start.14) | collective-permute-done | bytes 131104 | tf_op jit(solution)/shard_map/ppermute | solution.py:80
  62.3 0.7 %pad_maximum_fusion = bf16[32,4096]{1,0:T(8,128)(2,1)} fusion(bf16[16,4096]{1,0:T(8,128)(2,1)S(1)} %get-tuple-element.36, bf16[16,4096]{1,0:T(8,128)(2,1)S(1)} %get-tuple-element.35), kind=kLoop, calls=%fused_computation | loop fusion | flops 524288 | bytes 524288 | tf_op jit(solution)/shard_map/concatenate | solution.py:414
  (39 shorter events, 0.3 us)
Async XLA Ops:
  7.6 11.1 %collective-permute-start = (f32[8,2432]{1,0:T(8,128)}, f32[8,2432]{1,0:T(8,128)S(1)}, u32[]{:S(2)}, u32[]{:S(2)}) collective-permute-start(f32[8,2432]{1,0:T(8,128)} %get-tuple-element.21), channel_id=1, source_target_pairs={{0,12},{4,8},{8,4},{12,0},{1,13},{5,9},{9,5},{13,1},{2,14},{6,10},... | collective-permute-start | bytes 233480 | tf_op jit(solution)/shard_map/ppermute | solution.py:42
  12.7 6.2 %collective-permute-start.1 = (f32[8,2432]{1,0:T(8,128)}, f32[8,2432]{1,0:T(8,128)S(1)}, u32[]{:S(2)}, u32[]{:S(2)}) collective-permute-start(f32[8,2432]{1,0:T(8,128)} %get-tuple-element.22), channel_id=1, source_target_pairs={{0,4},{4,0},{8,12},{12,8},{1,5},{5,1},{9,13},{13,9},{2,6},{6,2},{1... | collective-permute-start | bytes 233480 | tf_op jit(solution)/shard_map/ppermute | solution.py:42
  12.7 6.2 %collective-permute-start.2 = (f32[8,2432]{1,0:T(8,128)}, f32[8,2432]{1,0:T(8,128)S(1)}, u32[]{:S(2)}, u32[]{:S(2)}) collective-permute-start(f32[8,2432]{1,0:T(8,128)} %get-tuple-element.23), channel_id=1, source_target_pairs={{0,8},{4,12},{8,0},{12,4},{1,9},{5,13},{9,1},{13,5},{2,10},{6,14},... | collective-permute-start | bytes 233480 | tf_op jit(solution)/shard_map/ppermute | solution.py:42
  13.4 0.9 %copy-start.3 = (f32[8,2432]{1,0:T(8,128)S(1)}, f32[8,2432]{1,0:T(8,128)}, u32[]{:S(2)}) copy-start(f32[8,2432]{1,0:T(8,128)} %get-tuple-element.20._.refs_0_) | copy-start | bytes 233476
  14.2 4.7 %copy-start.7 = (f32[2048]{0:T(1024)S(1)}, f32[2048]{0:T(1024)}, u32[]{:S(2)}) copy-start(f32[2048]{0:T(1024)} %param.20) | copy-start | bytes 24580
  14.2 4.7 %copy-start.8 = (f32[256]{0:T(256)S(1)}, f32[256]{0:T(256)}, u32[]{:S(2)}) copy-start(f32[256]{0:T(256)} %param.22) | copy-start | bytes 3076
  14.2 13.1 %copy-start = (bf16[8,4,128,128]{3,2,1,0:T(8,128)(2,1)S(1)}, bf16[8,4,128,128]{3,2,1,0:T(8,128)(2,1)}, u32[]{:S(2)}) copy-start(bf16[8,4,128,128]{3,2,1,0:T(8,128)(2,1)} %refs_4_.1) | copy-start | bytes 3145732
  14.3 13.1 %copy-start.1 = (bf16[8,4,128,128]{3,2,1,0:T(8,128)(2,1)S(1)}, bf16[8,4,128,128]{3,2,1,0:T(8,128)(2,1)}, u32[]{:S(2)}) copy-start(bf16[8,4,128,128]{3,2,1,0:T(8,128)(2,1)} %refs_5_.1) | copy-start | bytes 3145732
  14.3 13.1 %copy-start.4 = (f32[8,4,128]{2,1,0:T(4,128)S(1)}, f32[8,4,128]{2,1,0:T(4,128)}, u32[]{:S(2)}) copy-start(f32[8,4,128]{2,1,0:T(4,128)} %param.25) | copy-start | bytes 49156
  14.3 13.1 %copy-start.5 = (f32[8,4,128]{2,1,0:T(4,128)S(1)}, f32[8,4,128]{2,1,0:T(4,128)}, u32[]{:S(2)}) copy-start(f32[8,4,128]{2,1,0:T(4,128)} %param.26) | copy-start | bytes 49156
  14.3 13.1 %copy-start.9 = (s32[8]{0:T(128)S(1)}, s32[8]{0:T(128)}, u32[]{:S(2)}) copy-start(s32[8]{0:T(128)} %refs_3_.1) | copy-start | bytes 100
  19.0 1.2 %collective-permute-start.3 = (bf16[8,2304]{1,0:T(8,128)(2,1)S(1)}, bf16[8,2304]{1,0:T(8,128)(2,1)S(1)}, u32[]{:S(2)}, u32[]{:S(2)}) collective-permute-start(bf16[8,2304]{1,0:T(8,128)(2,1)S(1)} %norm.1.mine), channel_id=1, source_target_pairs={{0,1},{1,0},{2,3},{3,2},{4,5},{5,4},{6,7},{7,6},{8,9},{9,8},{10,11... | collective-permute-start | bytes 110600 | tf_op jit(solution)/shard_map/ppermute | solution.py:80
  20.3 3.8 %collective-permute-start.4 = (bf16[2,8,2304]{2,1,0:T(8,128)(2,1)S(1)}, bf16[2,8,2304]{2,1,0:T(8,128)(2,1)S(1)}, u32[]{:S(2)}, u32[]{:S(2)}) collective-permute-start(bf16[2,8,2304]{2,1,0:T(8,128)(2,1)S(1)} %pair.2.refs_2_), channel_id=1, source_target_pairs={{1,8},{2,4},{3,12},{4,1},{5,9},{6,5},{7,13},{8,2},{9,10},{10,6},{1... | collective-permute-start | bytes 221192 | tf_op jit(solution)/shard_map/ppermute | solution.py:75
  21.0 6.4 %collective-permute-start.5 = (bf16[2,8,2304]{2,1,0:T(8,128)(2,1)S(1)}, bf16[2,8,2304]{2,1,0:T(8,128)(2,1)S(1)}, u32[]{:S(2)}, u32[]{:S(2)}) collective-permute-start(bf16[2,8,2304]{2,1,0:T(8,128)(2,1)S(1)} %pair.2.refs_2_), channel_id=1, source_target_pairs={{0,4},{1,12},{2,0},{3,8},{4,5},{5,13},{6,1},{7,9},{8,6},{9,14},{10... | collective-permute-start | bytes 221192 | tf_op jit(solution)/shard_map/ppermute | solution.py:75
  29.4 20.1 %copy-start.2 = (f32[1,32,4096]{2,1,0:T(8,128)S(1)}, f32[1,32,4096]{2,1,0:T(8,128)}, u32[]{:S(2)}) copy-start(f32[1,32,4096]{2,1,0:T(8,128)} %param.16) | copy-start | bytes 1572868
  29.4 20.1 %copy-start.6 = (f32[4096]{0:T(1024)S(1)}, f32[4096]{0:T(1024)}, u32[]{:S(2)}) copy-start(f32[4096]{0:T(1024)} %param.29) | copy-start | bytes 49156
  29.5 8.4 %collective-permute-start.6 = (f16[136,128]{1,0:T(8,128)(2,1)S(1)}, f16[136,128]{1,0:T(8,128)(2,1)S(1)}, u32[]{:S(2)}, u32[]{:S(2)}) collective-permute-start(f16[136,128]{1,0:T(8,128)(2,1)S(1)} %convert_element_type.31), channel_id=1, source_target_pairs={{0,12},{4,8},{8,4},{12,0},{1,13},{5,9},{9,5},{13,1},{2,14},{6,10},... | collective-permute-start | bytes 104456 | tf_op jit(solution)/shard_map/ppermute | solution.py:42
  34.6 4.4 %collective-permute-start.7 = (f16[136,128]{1,0:T(8,128)(2,1)S(1)}, f16[136,128]{1,0:T(8,128)(2,1)S(1)}, u32[]{:S(2)}, u32[]{:S(2)}) collective-permute-start(f16[136,128]{1,0:T(8,128)(2,1)S(1)} %convert_element_type.33), channel_id=1, source_target_pairs={{0,4},{4,0},{8,12},{12,8},{1,5},{5,1},{9,13},{13,9},{2,6},{6,2},{1... | collective-permute-start | bytes 104456 | tf_op jit(solution)/shard_map/ppermute | solution.py:42
  35.0 4.9 %collective-permute-start.8 = (f16[136,128]{1,0:T(8,128)(2,1)S(1)}, f16[136,128]{1,0:T(8,128)(2,1)S(1)}, u32[]{:S(2)}, u32[]{:S(2)}) collective-permute-start(f16[136,128]{1,0:T(8,128)(2,1)S(1)} %convert_element_type.35), channel_id=1, source_target_pairs={{0,8},{4,12},{8,0},{12,4},{1,9},{5,13},{9,1},{13,5},{2,10},{6,14},... | collective-permute-start | bytes 104456 | tf_op jit(solution)/shard_map/ppermute | solution.py:42
  37.9 22.9 %copy-start.10 = (bf16[32,4096]{1,0:T(8,128)(2,1)S(1)}, bf16[32,4096]{1,0:T(8,128)(2,1)}, u32[]{:S(2)}) copy-start(bf16[32,4096]{1,0:T(8,128)(2,1)} %residual.1) | copy-start | bytes 786436
  40.2 1.3 %collective-permute-start.9 = (bf16[8,2048]{1,0:T(8,128)(2,1)S(1)}, bf16[8,2048]{1,0:T(8,128)(2,1)S(1)}, u32[]{:S(2)}, u32[]{:S(2)}) collective-permute-start(bf16[8,2048]{1,0:T(8,128)(2,1)S(1)} %merge.1.mine), channel_id=1, source_target_pairs={{0,1},{1,0},{2,3},{3,2},{4,5},{5,4},{6,7},{7,6},{8,9},{9,8},{10,11... | collective-permute-start | bytes 98312 | tf_op jit(solution)/shard_map/ppermute | solution.py:80
  41.4 3.8 %collective-permute-start.10 = (bf16[2,8,2048]{2,1,0:T(8,128)(2,1)S(1)}, bf16[2,8,2048]{2,1,0:T(8,128)(2,1)S(1)}, u32[]{:S(2)}, u32[]{:S(2)}) collective-permute-start(bf16[2,8,2048]{2,1,0:T(8,128)(2,1)S(1)} %pair.3.refs_2_), channel_id=1, source_target_pairs={{1,8},{2,4},{3,12},{4,1},{5,9},{6,5},{7,13},{8,2},{9,10},{10,6},{1... | collective-permute-start | bytes 196616 | tf_op jit(solution)/shard_map/ppermute | solution.py:75
  42.1 7.4 %collective-permute-start.11 = (bf16[2,8,2048]{2,1,0:T(8,128)(2,1)S(1)}, bf16[2,8,2048]{2,1,0:T(8,128)(2,1)S(1)}, u32[]{:S(2)}, u32[]{:S(2)}) collective-permute-start(bf16[2,8,2048]{2,1,0:T(8,128)(2,1)S(1)} %pair.3.refs_2_), channel_id=1, source_target_pairs={{0,4},{1,12},{2,0},{3,8},{4,5},{5,13},{6,1},{7,9},{8,6},{9,14},{10... | collective-permute-start | bytes 196616 | tf_op jit(solution)/shard_map/ppermute | solution.py:75
  52.6 1.6 %collective-permute-start.12 = (f32[16,4096]{1,0:T(8,128)S(1)}, f32[16,4096]{1,0:T(8,128)S(1)}, u32[]{:S(2)}, u32[]{:S(2)}) collective-permute-start(f32[16,4096]{1,0:T(8,128)S(1)} %get-tuple-element.32), channel_id=1, source_target_pairs={{0,1},{1,0},{2,3},{3,2},{4,5},{5,4},{6,7},{7,6},{8,9},{9,8},{10,11... | collective-permute-start | bytes 786440 | tf_op jit(solution)/shard_map/ppermute | solution.py:80
  54.2 6.6 %collective-permute-start.13 = (f16[16,4096]{1,0:T(8,128)(2,1)S(1)}, f16[16,4096]{1,0:T(8,128)(2,1)S(1)}, u32[]{:S(2)}, u32[]{:S(2)}) collective-permute-start(f16[16,4096]{1,0:T(8,128)(2,1)S(1)} %get-tuple-element.33), channel_id=1, source_target_pairs={{0,2},{1,3},{2,0},{3,1},{4,6},{5,7},{6,4},{7,5},{8,10},{9,11},{10,... | collective-permute-start | bytes 393224 | tf_op jit(solution)/shard_map/ppermute | solution.py:80
  60.8 1.4 %collective-permute-start.14 = (bf16[16,4096]{1,0:T(8,128)(2,1)S(1)}, bf16[16,4096]{1,0:T(8,128)(2,1)S(1)}, u32[]{:S(2)}, u32[]{:S(2)}) collective-permute-start(bf16[16,4096]{1,0:T(8,128)(2,1)S(1)} %add_convert_fusion), channel_id=1, source_target_pairs={{0,1},{1,0},{2,3},{3,2},{4,5},{5,4},{6,7},{7,6},{8,9},{9,8},{10,11... | collective-permute-start | bytes 393224 | tf_op jit(solution)/shard_map/ppermute | solution.py:80
